TPU v7x, 256 devices: a whole 4x4x8 slice. The times are simulated.
256 devices in a mesh: queue: 64 (over z, x, y_lo), heads: 4 (over y_hi, core).
Axes of the slice: x: 4, y: 4 (y_hi: 2, y_lo: 2; y = y_hi * 2 + y_lo), z: 8, core: 2. Of those that a mesh axis runs over, the one named last changes fastest.
Arguments:
- hidden: bfloat16 [32768, 3072], P('queue'), may hold values from -6 to 6
- levels: int32 [64], replicated, may hold values from 0 to 252, as said below
- frame_counts: int32 [64], replicated, may hold values from 1 to 2, as said below
- mod_weight: bfloat16 [512, 9216], P(None, 'queue')
- qkv_weight: bfloat16 [3, 3072, 1536], P(None, None, 'heads'), may hold values from -0.109375 to 0.109375
- out_weight: bfloat16 [1536, 3072], P('heads'), may hold values from -0.15625 to 0.15625
- fresh: bfloat16 [512, 3072], P(None, 'heads'), may hold values from -6 to 6
Outputs:
- queue_next: bfloat16 [32768, 3072], P('queue', 'heads')
Inputs may be any that keep to these rules, and one draw needn't show every extreme that they name: `levels`: strictly rising along the queue, the first 0 and the last 252. `frame_counts`: some stretch has 2 live frames and some other has 1.
All inputs are finite; a program needn't handle non-finite values.
Results may differ from a plain program's by a relative error of at most 0.035.
The roundings to bfloat16 on the way count: a program that leaves them out, or rounds other values in their place, can miss the bound.
Values may be sent and summed in bfloat16 or wider, within the bound.
No kernel may reach another device: no remote copies, remote signals or barrier semaphores. Data moves between devices by JAX's collectives and lax.ppermute only.
A program may use at most 128 MiB of HBM per device.

v0:
```python
import math

import jax
import jax.numpy as jnp
from jax import lax
from jax.sharding import PartitionSpec as P

HD = 64
P_SIZE = 256


NEG = -1e30


def with_halo(block, sides, width):
    for axis, dim in sides:
        count = lax.axis_size(axis)
        forward = [(i, i + 1) for i in range(count - 1)]
        backward = [(target, source) for source, target in forward]
        low = lax.ppermute(
            lax.slice_in_dim(block, block.shape[dim] - width, None, axis=dim), axis, forward
        )
        high = lax.ppermute(lax.slice_in_dim(block, 0, width, axis=dim), axis, backward)
        block = jnp.concatenate([low, block, high], axis=dim)
    return block


def passed_along(array, axis, by):
    count = lax.axis_size(axis)
    pairs = [(i, i + by) for i in range(count) if 0 <= i + by < count]
    return lax.ppermute(array, axis, pairs)


def embed_levels(levels, width):
    halfway = width // 2
    freqs = jnp.exp(-math.log(10000.0) * jnp.arange(halfway, dtype=jnp.float32) / halfway)
    angles = levels.astype(jnp.float32)[:, None] * freqs[None, :]
    return jax.nn.silu(jnp.concatenate([jnp.cos(angles), jnp.sin(angles)], axis=1)).astype(
        jnp.bfloat16
    )


def block_attention(query, keys, values, live):
    scores = jnp.einsum("qhd,khd->hqk", query, keys, preferred_element_type=jnp.float32) * HD ** (
        -0.5
    )
    scores = jnp.where(live[None, None, :], scores, NEG)
    peak = jnp.max(scores, axis=2, keepdims=True)
    weights = jnp.where(live[None, None, :], jnp.exp(scores - peak), 0.0)
    total = jnp.sum(weights, axis=2)
    numer = jnp.einsum(
        "hqk,khd->qhd", weights.astype(jnp.bfloat16), values, preferred_element_type=jnp.float32
    )
    return (jnp.transpose(peak[:, :, 0]), jnp.transpose(total), numer)


def on_device(hidden, levels, frame_counts, mod_weight, qkv_weight, out_weight, fresh):
    rows, width = hidden.shape
    slot = lax.axis_index("queue")
    queue_len = lax.axis_size("queue")
    share = width // lax.axis_size("heads")
    member = lax.axis_index("heads")
    level = lax.dynamic_slice(levels, (slot,), (1,))
    emb_row = embed_levels(level, mod_weight.shape[0])
    mod_row = jnp.dot(
        emb_row,
        lax.all_gather(mod_weight, "queue", axis=1, tiled=True),
        preferred_element_type=jnp.float32,
    )
    mod_row = mod_row[0]
    shift = mod_row[:width]
    scale = mod_row[width : 2 * width]
    gate = lax.dynamic_slice_in_dim(mod_row, 2 * width + member * share, share)
    states = hidden.astype(jnp.float32)
    mean = jnp.mean(states, axis=1, keepdims=True)
    centred = states - mean
    var = jnp.mean(centred * centred, axis=1, keepdims=True)
    normed = (centred * lax.rsqrt(var + 1e-05) * (1.0 + scale[None, :]) + shift[None, :]).astype(
        jnp.bfloat16
    )
    projected = jnp.einsum(
        "rd,tde->tre", normed, qkv_weight, preferred_element_type=jnp.float32
    ).astype(jnp.bfloat16)
    local_width = qkv_weight.shape[2]
    local_heads = local_width // HD
    query = projected[0].reshape(rows, local_heads, HD)
    key_value = jnp.concatenate([projected[1], projected[2]], axis=1)
    zero_count = jnp.zeros((1,), jnp.int32)
    counts_pad = jnp.concatenate([zero_count, frame_counts, zero_count])
    counts_three = lax.dynamic_slice(counts_pad, (slot,), (3,))
    frame = jnp.arange(rows, dtype=jnp.int32) // P_SIZE
    live_prev = frame < counts_three[0]
    live_own = frame < counts_three[1]
    live_next = frame < counts_three[2]
    extended = with_halo(key_value, (("queue", 0),), rows)
    all_keys = extended[:, :local_width].reshape(3 * rows, local_heads, HD)
    all_values = extended[:, local_width:].reshape(3 * rows, local_heads, HD)
    all_live = jnp.concatenate([live_prev, live_own, live_next])
    peak_unused, total, numer = block_attention(query, all_keys, all_values, all_live)
    attn = (numer / total[:, :, None]).astype(jnp.bfloat16).reshape(rows, local_width)
    partial_proj = jnp.dot(attn, out_weight, preferred_element_type=jnp.float32)
    summed = lax.psum_scatter(partial_proj, "heads", scatter_dimension=1, tiled=True)
    own_share = lax.dynamic_slice_in_dim(hidden, member * share, share, 1).astype(jnp.float32)
    updated = (own_share + gate[None, :] * summed).astype(jnp.bfloat16)
    moved = passed_along(updated, "queue", -1)
    return jnp.where(slot == queue_len - 1, fresh, moved)


def solution(mesh):
    placed = (
        P("queue", None),
        P(),
        P(),
        P(None, "queue"),
        P(None, None, "heads"),
        P("heads", None),
        P(None, "heads"),
    )
    return jax.shard_map(
        on_device, mesh=mesh, in_specs=placed, out_specs=P("queue", "heads"), check_vma=False
    )
```

profile of v0, /device:TPU:111, one launch (start us, length us, event | category | flops | bytes accessed | tf_op | source)
XLA Modules:
  0.0 506.7 jit_solution(422548573796158464)
XLA Ops:
  7.3 1.4 dynamic_slice.13
  9.5 2.4 convert_reduce_fusion
  11.9 1.0 fusion.9
  12.8 271.7 %all-gather.2.cloned.1.call-done = bf16[512,9216]{0,1:T(8,128)(2,1)} async-done(((bf16[512,144]{0,1:T(8,128)(2,1)}), bf16[512,9216]{0,1:T(8,128)(2,1)}) %all-gather.2.cloned.1.call-update) | async-done | bytes 9437200 | tf_op jit(solution)/shard_map/all_gather | solution.py:67
  284.5 6.4 %fusion.52 = f32[1,9216]{1,0:T(1,128)S(1)} fusion(bf16[512,1]{0,1:T(2,128)(2,1)S(1)} %reshape.66, bf16[512,9216]{0,1:T(8,128)(2,1)} %all-gather.2.cloned.1.call-done), kind=kOutput, calls=%fused_computation.62 | convolution fusion | flops 9437184 | bytes 9475072 | tf_op jit(solution)/shard_map/dot_general | solution.py:65
  291.5 7.2 %fusion.25 = bf16[3,512,384]{1,2,0:T(8,128)(2,1)S(1)} fusion(bf16[3,3072,384]{2,1,0:T(8,128)(2,1)} %param.11, bf16[512,3072]{1,0:T(8,128)(2,1)S(1)} %copy-done.2, f32[3072]{0:T(1024)S(1)} %get-tuple-element.11, f32[3072]{0:T(1024)S(1)} %get-tuple-element.10, f32[512]{0:T(512)S(1)} %add_rsqrt_fusion, f32[512]{0:T(512)S(1)} %broadcast_multiply_fusion), kind=kOutput, calls=%fused_computation.27 | convolution fusion | flops 3633905664 | bytes 11431936 | tf_op jit(solution)/shard_map/rd,tde->tre/dot_general | solution.py:81
  298.6 0.8 fusion.49
  299.5 0.9 pad_maximum_fusion.1
  300.4 3.2 collective-permute-start.1
  303.6 6.5 %collective-permute-start = (bf16[512,768]{0,1:T(8,128)(2,1)}, bf16[512,768]{0,1:T(8,128)(2,1)}, u32[]{:S(2)}, u32[]{:S(2)}) collective-permute-start(bf16[512,768]{0,1:T(8,128)(2,1)} %pad_maximum_fusion.1), channel_id=1, source_target_pairs={{0,4},{4,8},{8,12},{12,16},{16,20},{20,24},{24,28},{28,32},{32,36}... | collective-permute-start | bytes 2359304 | tf_op jit(solution)/shard_map/ppermute | solution.py:20
  311.6 1.4 fusion.39
  313.5 11.8 %collective-permute-done.1 = bf16[512,768]{0,1:T(8,128)(2,1)} collective-permute-done((bf16[512,768]{0,1:T(8,128)(2,1)}, bf16[512,768]{0,1:T(8,128)(2,1)}, u32[]{:S(2)}, u32[]{:S(2)}) %collective-permute-start.1) | collective-permute-done | bytes 786464 | tf_op jit(solution)/shard_map/ppermute | solution.py:23
  325.2 3.2 collective-permute-done
  328.5 1.5 pad_maximum_fusion
  330.0 1.2 fusion.48
  331.2 10.1 %fusion.51 = (f32[6,512]{1,0:T(8,128)S(1)}, bf16[6,512,1536]{2,1,0:T(8,128)(2,1)}) fusion(pred[1536]{0:T(1024)(128)(4,1)} %pad_add_fusion, bf16[512,6,64]{0,2,1:T(8,128)(2,1)} %bitcast.43, bf16[1536,6,64]{0,2,1:T(8,128)(2,1)} %bitcast.42), kind=kOutput, calls=%fused_computation.61 | convolution fusion | flops 632292864 | bytes 11023872 | tf_op jit(solution)/shard_map/sub | solution.py:49
  341.3 6.6 %fusion.34 = bf16[512,6,64]{0,2,1:T(8,128)(2,1)S(1)} fusion(bf16[1536,6,64]{0,2,1:T(8,128)(2,1)S(1)} %bitcast.40, bf16[6,512,1536]{2,1,0:T(8,128)(2,1)} %get-tuple-element.16, f32[512,6]{0,1:T(8,128)S(1)} %bitcast.46), kind=kOutput, calls=%fused_computation.30 | convolution fusion | flops 604372992 | bytes 11022336 | tf_op jit(solution)/shard_map/hqk,khd->qhd/dot_general | solution.py:51
  347.9 4.5 fusion.53
  352.4 0.8 dynamic_slice.14
  353.3 117.0 %reduce-scatter.2.cloned.1.call-done = f32[512,768]{1,0:T(8,128)} async-done(((f32[512,3072]{1,0:T(8,128)}), f32[512,768]{1,0:T(8,128)}) %reduce-scatter.2.cloned.1.call-update) | async-done | bytes 1572880 | tf_op jit(solution)/shard_map/reduce_scatter | solution.py:102
  470.3 2.7 add_convert_fusion
  472.9 3.0 collective-permute-start.2
  476.0 21.8 %collective-permute-done.2 = bf16[512,768]{1,0:T(8,128)(2,1)} collective-permute-done((bf16[512,768]{1,0:T(8,128)(2,1)}, bf16[512,768]{1,0:T(8,128)(2,1)}, u32[]{:S(2)}, u32[]{:S(2)}) %collective-permute-start.2) | collective-permute-done | bytes 786464 | tf_op jit(solution)/shard_map/ppermute | solution.py:31
  497.8 2.1 broadcast_select_fusion
  (27 shorter events, 3.5 us)
Async XLA Ops:
  6.5 341.4 %copy-start = (bf16[384,3072]{1,0:T(8,128)(2,1)S(1)}, bf16[384,3072]{1,0:T(8,128)(2,1)}, u32[]{:S(2)}) copy-start(bf16[384,3072]{1,0:T(8,128)(2,1)} %param.12) | copy-start | bytes 7077892
  6.5 277.9 %all-gather.2.cloned.1.call-start = ((), (), s32[]{:S(2)}) async-start(), calls=%async_computation.1 | async-start | bytes 9584640 | tf_op jit(solution)/shard_map/all_gather | solution.py:67
  7.3 463.0 %reduce-scatter.2.cloned.1.call-start = ((), (), s32[]{:S(2)}) async-start(), calls=%async_computation.2 | async-start | bytes 7864320 | tf_op jit(solution)/shard_map/reduce_scatter | solution.py:102
  7.3 4.5 copy-start.1
  284.5 7.0 %copy-start.2 = (bf16[512,3072]{1,0:T(8,128)(2,1)S(1)}, bf16[512,3072]{1,0:T(8,128)(2,1)}, u32[]{:S(2)}) copy-start(bf16[512,3072]{1,0:T(8,128)(2,1)} %param.7) | copy-start | bytes 9437188
  290.8 0.6 copy-start.4
  291.5 18.6 %copy-start.5 = (s32[64]{0:T(128)S(1)}, s32[64]{0:T(128)}, u32[]{:S(2)}) copy-start(s32[64]{0:T(128)} %param.9) | copy-start | bytes 772
  300.4 24.8 %collective-permute-start.1 = (bf16[512,768]{0,1:T(8,128)(2,1)}, bf16[512,768]{0,1:T(8,128)(2,1)}, u32[]{:S(2)}, u32[]{:S(2)}) collective-permute-start(bf16[512,768]{0,1:T(8,128)(2,1)} %pad_maximum_fusion.1), channel_id=1, source_target_pairs={{4,0},{8,4},{12,8},{16,12},{20,16},{24,20},{28,24},{32,28},{36,32}... | collective-permute-start | bytes 2359304 | tf_op jit(solution)/shard_map/ppermute | solution.py:23
  303.6 24.9 %collective-permute-start = (bf16[512,768]{0,1:T(8,128)(2,1)}, bf16[512,768]{0,1:T(8,128)(2,1)}, u32[]{:S(2)}, u32[]{:S(2)}) collective-permute-start(bf16[512,768]{0,1:T(8,128)(2,1)} %pad_maximum_fusion.1), channel_id=1, source_target_pairs={{0,4},{4,8},{8,12},{12,16},{16,20},{20,24},{24,28},{28,32},{32,36}... | collective-permute-start | bytes 2359304 | tf_op jit(solution)/shard_map/ppermute | solution.py:20
  352.4 145.4 %copy-start.3 = (bf16[512,768]{1,0:T(8,128)(2,1)S(1)}, bf16[512,768]{1,0:T(8,128)(2,1)}, u32[]{:S(2)}) copy-start(bf16[512,768]{1,0:T(8,128)(2,1)} %param.13) | copy-start | bytes 2359300
  472.9 24.8 %collective-permute-start.2 = (bf16[512,768]{1,0:T(8,128)(2,1)}, bf16[512,768]{1,0:T(8,128)(2,1)}, u32[]{:S(2)}, u32[]{:S(2)}) collective-permute-start(bf16[512,768]{1,0:T(8,128)(2,1)} %add_convert_fusion), channel_id=1, source_target_pairs={{4,0},{8,4},{12,8},{16,12},{20,16},{24,20},{28,24},{32,28},{36,32}... | collective-permute-start | bytes 2359304 | tf_op jit(solution)/shard_map/ppermute | solution.py:31
Sparse Core Ops, SparseCore 0:
  9.1 275.2 all-gather.1
  352.5 117.6 reduce-scatter.1
where the time goes:
time: 508 us; the launch traced here: 507 us
  waiting for transfers between devices  426 us (84%)
  matrix products  34.7 us (7%)
  between operations  14.2 us (3%)
  other arithmetic  13.3 us (3%)
  starting transfers between devices  12.8 us (3%)
  local copies, waits for them, and re-layouts  5.62 us (1%)
    all_gather x1, waiting for transfers between devices, on_device(): lax.all_gather(mod_weight, 'queue', axis=1, tiled=True)  272 us
    reduce_scatter x1, waiting for transfers between devices, on_device(): lax.psum_scatter(partial_proj, 'heads', scatter_dimension=1, tiled=True)  117 us
    ppermute x1, waiting for transfers between devices, passed_along(): return lax.ppermute(array, axis, pairs)  21.8 us
    ppermute x1, waiting for transfers between devices, with_halo(): lax.ppermute(lax.slice_in_dim(block, 0, width, axis=dim), axis, backward)  11.8 us
  transfers between devices with their start and end apart: 5, of which 5 were waited for; matrix products, arithmetic and copies ran while one was open for 2% of the time, Pallas kernels for 0%

commit v1 on v0

v1 whole, which is shorter than its diff:
```python
import functools
import math

import jax
import jax.numpy as jnp
from jax import lax
from jax.experimental import pallas as pl
from jax.experimental.pallas import tpu as pltpu
from jax.sharding import PartitionSpec as P

HD = 64
P_SIZE = 256
PAIR = 2 * HD
NEG = -1e30
BOTH = ("queue", "heads")
MIB = 1024 * 1024


def embed_levels(levels, width):
    halfway = width // 2
    freqs = jnp.exp(-math.log(10000.0) * jnp.arange(halfway, dtype=jnp.float32) / halfway)
    angles = levels.astype(jnp.float32)[:, None] * freqs[None, :]
    return jax.nn.silu(jnp.concatenate([jnp.cos(angles), jnp.sin(angles)], axis=1)).astype(
        jnp.bfloat16
    )


def routed(array, queue_len, members, target):
    pairs = []
    for slot in range(queue_len):
        for member in range(members):
            goal = target(slot, member // 2, member % 2)
            if goal is not None and 0 <= goal[0] < queue_len:
                pairs.append((slot * members + member, goal[0] * members + goal[1] * 2 + goal[2]))
    return lax.ppermute(array, BOTH, pairs)


def low_lanes(shape):
    return lax.broadcasted_iota(jnp.int32, shape, len(shape) - 1) < HD


def qkv_kernel(where_ref, first_ref, second_ref, scale_ref, shift_ref, weight_hbm, query_ref, kv_ref, weight, sems):
    parity = where_ref[0]
    order = where_ref[1]
    copies = []
    for kind in range(3):
        for part in range(2):
            start = pl.multiple_of(2 * parity * PAIR, PAIR) if part == 0 else PAIR
            column = (kind if part == 0 else 3 + kind) * PAIR
            copies.append(
                pltpu.make_async_copy(
                    weight_hbm.at[kind, :, pl.ds(start, PAIR)],
                    weight.at[:, pl.ds(column, PAIR)],
                    sems.at[2 * kind + part],
                )
            )
    for copy in copies:
        copy.start()
    half = first_ref.shape[0]

    def normalised(ref):
        states = ref[...].astype(jnp.float32)
        mean = jnp.mean(states, axis=1, keepdims=True)
        centred = states - mean
        var = jnp.mean(centred * centred, axis=1, keepdims=True)
        return (centred * lax.rsqrt(var + 1e-05) * scale_ref[...] + shift_ref[...]).astype(jnp.bfloat16)

    def project(normed, block):
        out = jnp.dot(normed, weight[...], preferred_element_type=jnp.float32)
        low = low_lanes((half, PAIR))
        rows = pl.ds(pl.multiple_of(block * half, half), half)
        q_pair, k_pair, v_pair, q_mid, k_mid, v_mid = [out[:, i * PAIR : (i + 1) * PAIR] for i in range(6)]
        even = parity == 0
        turned = [pltpu.roll(a, HD, 1) for a in (q_mid, k_mid, v_mid)]
        q_one = jnp.where(even, q_mid, turned[0])
        k_one = jnp.where(even, k_mid, turned[1])
        v_one = jnp.where(even, turned[2], v_mid)
        query_ref[rows, :PAIR] = (q_pair.astype(jnp.bfloat16) * HD ** (-0.5)).astype(jnp.bfloat16)
        query_ref[rows, PAIR:] = jnp.where(
            low, q_one.astype(jnp.bfloat16).astype(jnp.float32) * HD ** (-0.5), 0.0
        ).astype(jnp.bfloat16)
        kv_ref[rows, :PAIR] = k_pair.astype(jnp.bfloat16)
        kv_ref[rows, PAIR : 2 * PAIR] = v_pair.astype(jnp.bfloat16)
        kv_ref[rows, 2 * PAIR :] = jnp.where(low, k_one, v_one).astype(jnp.bfloat16)

    normed_first = normalised(first_ref)
    for copy in copies:
        copy.wait()
    project(normed_first, order)
    project(normalised(second_ref), 1 - order)


def qkv(where, first, second, scale, shift, weight):
    half, width = first.shape
    vmem = pl.BlockSpec(memory_space=pltpu.VMEM)
    return pl.pallas_call(
        qkv_kernel,
        out_shape=(
            jax.ShapeDtypeStruct((2 * half, 2 * PAIR), jnp.bfloat16),
            jax.ShapeDtypeStruct((2 * half, 3 * PAIR), jnp.bfloat16),
        ),
        in_specs=[pl.BlockSpec(memory_space=pltpu.SMEM)] + [vmem] * 4 + [pl.BlockSpec(memory_space=pl.ANY)],
        out_specs=(vmem, vmem),
        scratch_shapes=[
            pltpu.VMEM((width, 6 * PAIR), jnp.bfloat16),
            pltpu.SemaphoreType.DMA((6,)),
        ],
        compiler_params=pltpu.CompilerParams(vmem_limit_bytes=40 * MIB),
        cost_estimate=pl.CostEstimate(
            flops=2 * 2 * half * width * 6 * PAIR, bytes_accessed=9 * MIB, transcendentals=0
        ),
    )(where, first, second, scale, shift, weight)


def head_views(query, kv):
    low = low_lanes((query.shape[0], PAIR))
    q_pair, q_one = query[:, :PAIR], query[:, PAIR:]
    k_pair, v_pair, mid = kv
    zero = jnp.zeros_like(q_pair)
    return (
        (jnp.where(low, q_pair, zero), k_pair, v_pair),
        (jnp.where(low, zero, q_pair), k_pair, v_pair),
        (q_one, mid, mid),
    )


def scores_of(query, keys):
    return lax.dot_general(query, keys, (((1,), (1,)), ((), ())), preferred_element_type=jnp.float32)


def local_kernel(counts_ref, qo_ref, qt_ref, kvo_ref, kvt_ref, oo, mo, lo, ot, mt, lt):
    span = kvo_ref.shape[0]
    tile = 256
    lane = lax.broadcasted_iota(jnp.int32, (1, 2 * span), 1)
    live_own = (lane < counts_ref[0] * P_SIZE) & (lane < span)
    live_other = (lane >= span) & (lane - span < counts_ref[1] * P_SIZE)
    bias = jnp.where(live_own | live_other, 0.0, NEG)
    kv = [
        jnp.concatenate([kvo_ref[:, i * PAIR : (i + 1) * PAIR], kvt_ref[:, i * PAIR : (i + 1) * PAIR]], axis=0)
        for i in range(3)
    ]
    low = low_lanes((tile, PAIR))
    for q_ref, o_ref, m_ref, l_ref in ((qo_ref, oo, mo, lo), (qt_ref, ot, mt, lt)):
        for start in range(0, span, tile):
            rows = pl.ds(start, tile)
            outs = []
            for query, keys, values in head_views(q_ref[rows, :], kv):
                scores = scores_of(query, keys) + bias
                peak = jnp.max(scores, axis=1, keepdims=True)
                probs = jnp.exp(scores - peak)
                total = jnp.sum(probs, axis=1, keepdims=True)
                numer = jnp.dot(probs.astype(jnp.bfloat16), values, preferred_element_type=jnp.float32)
                outs.append((numer, peak, total))
            (na, pa, ta), (nb, pb, tb), (nc, pc, tc) = outs
            o_ref[rows, :PAIR] = jnp.where(low, na, nb)
            m_ref[rows, :PAIR] = jnp.where(low, pa, pb)
            l_ref[rows, :PAIR] = jnp.where(low, ta, tb)
            o_ref[rows, PAIR:] = nc
            m_ref[rows, PAIR:] = jnp.broadcast_to(pc, (tile, PAIR))
            l_ref[rows, PAIR:] = jnp.broadcast_to(tc, (tile, PAIR))


def local_attention(counts, q_own, q_other, kv_own, kv_other):
    span = q_own.shape[0]
    vmem = pl.BlockSpec(memory_space=pltpu.VMEM)
    part = jax.ShapeDtypeStruct((span, 2 * PAIR), jnp.float32)
    return pl.pallas_call(
        local_kernel,
        out_shape=(part,) * 6,
        in_specs=[pl.BlockSpec(memory_space=pltpu.SMEM)] + [vmem] * 4,
        out_specs=(vmem,) * 6,
        compiler_params=pltpu.CompilerParams(vmem_limit_bytes=32 * MIB),
        cost_estimate=pl.CostEstimate(
            flops=8 * 3 * 4 * span * span * 256, bytes_accessed=5 * MIB, transcendentals=12 * span * span
        ),
    )(counts, q_own, q_other, kv_own, kv_other)


def remote_kernel(count_ref, q_ref, kv_ref, o_ref, m_ref, l_ref, piece_ref):
    span = kv_ref.shape[0]
    tile = 256
    lane = lax.broadcasted_iota(jnp.int32, (1, span), 1)
    bias = jnp.where(lane < count_ref[0] * P_SIZE, 0.0, NEG)
    kv = [kv_ref[:, i * PAIR : (i + 1) * PAIR] for i in range(3)]
    low = low_lanes((tile, PAIR))
    ones = []
    for start in range(0, span, tile):
        rows = pl.ds(start, tile)
        outs = []
        for head, (query, keys, values) in enumerate(head_views(q_ref[rows, :], kv)):
            at = head * HD if head < 2 else PAIR
            before = m_ref[rows, at : at + 1]
            scores = scores_of(query, keys) + bias
            peak = jnp.maximum(jnp.max(scores, axis=1, keepdims=True), before)
            probs = jnp.exp(scores - peak)
            fade = jnp.exp(before - peak)
            total = jnp.sum(probs, axis=1, keepdims=True) + fade * l_ref[rows, at : at + 1]
            numer = jnp.dot(probs.astype(jnp.bfloat16), values, preferred_element_type=jnp.float32)
            block = o_ref[rows, :PAIR] if head < 2 else o_ref[rows, PAIR:]
            outs.append((numer + fade * block) / total)
        piece_ref[rows, :] = jnp.where(low, outs[0], outs[1]).astype(jnp.bfloat16)
        ones.append(outs[2])
    piece_ref[span:, :] = jnp.where(low, pltpu.roll(ones[0], HD, 1), ones[1]).astype(jnp.bfloat16)


def remote_attention(count, query, kv, o, m, l):
    span = query.shape[0]
    vmem = pl.BlockSpec(memory_space=pltpu.VMEM)
    return pl.pallas_call(
        remote_kernel,
        out_shape=jax.ShapeDtypeStruct((span + span // 2, PAIR), jnp.bfloat16),
        in_specs=[pl.BlockSpec(memory_space=pltpu.SMEM)] + [vmem] * 5,
        out_specs=vmem,
        compiler_params=pltpu.CompilerParams(vmem_limit_bytes=32 * MIB),
        cost_estimate=pl.CostEstimate(
            flops=4 * 3 * span * span * 256, bytes_accessed=2 * MIB, transcendentals=3 * span * span
        ),
    )(count, query, kv, o, m, l)


def out_kernel(
    where_ref,
    *refs,
):
    (
        w_own, w_twin, w_far0, w_far1, w_fart0, w_fart1,
        p1, p2, p3, p4, t1, t2, t3, t4,
        residual_ref, gate_ref, fresh_ref, out_ref, attn, weight,
    ) = refs
    even = where_ref[1] == 0
    last = where_ref[2] == 1
    z_half = where_ref[3]
    span = residual_ref.shape[0]
    half = span // 2
    block = w_own.shape[0]

    @pl.when(pl.program_id(0) == 0)
    def _():
        low = low_lanes((half, PAIR))
        for index, (other, own) in enumerate(((p4, p1), (p3, p2), (t4, t1), (t3, t2))):
            first = jnp.where(even, other[...], own[...])
            second = jnp.where(even, own[...], other[...])
            base = index * 3 * PAIR
            attn[:, base : base + PAIR] = first[:span]
            attn[:, base + 2 * PAIR : base + 3 * PAIR] = second[:span]
            one_f, one_s = first[span:].astype(jnp.float32), second[span:].astype(jnp.float32)
            attn[:half, base + PAIR : base + 2 * PAIR] = jnp.where(
                low, one_f, pltpu.roll(one_s, HD, 1)
            ).astype(jnp.bfloat16)
            attn[half:, base + PAIR : base + 2 * PAIR] = jnp.where(
                low, pltpu.roll(one_f, HD, 1), one_s
            ).astype(jnp.bfloat16)

    near = pl.multiple_of(z_half * (block // 2), block // 2)
    away = pl.multiple_of((1 - z_half) * (block // 2), block // 2)
    weight[:block, :] = w_own[...]
    weight[pl.ds(block + near, block // 2), :] = w_far0[...]
    weight[pl.ds(block + away, block // 2), :] = w_far1[...]
    weight[2 * block : 3 * block, :] = w_twin[...]
    weight[pl.ds(3 * block + near, block // 2), :] = w_fart0[...]
    weight[pl.ds(3 * block + away, block // 2), :] = w_fart1[...]
    summed = jnp.dot(attn[...], weight[...], preferred_element_type=jnp.float32)
    updated = residual_ref[...].astype(jnp.float32) + gate_ref[...] * summed
    out_ref[...] = jnp.where(last, fresh_ref[...], updated.astype(jnp.bfloat16))


def out_projection(where, out_weight, w_twin, far, pieces, residual, gate, fresh):
    span, share = residual.shape
    block = out_weight.shape[0]
    tile = 256
    steps = share // tile
    whole = lambda a: pl.BlockSpec(a.shape, lambda j, w: (0,) * a.ndim)
    cols = lambda rows: pl.BlockSpec((rows, tile), lambda j, w: (0, j))
    by_core = pl.BlockSpec((block // 2, tile), lambda j, w: (0, w[4] * steps + j))
    by_member = pl.BlockSpec((block, tile), lambda j, w: (0, w[0] * steps + j))
    return pl.pallas_call(
        out_kernel,
        out_shape=jax.ShapeDtypeStruct((span, share), jnp.bfloat16),
        grid_spec=pltpu.PrefetchScalarGridSpec(
            num_scalar_prefetch=1,
            grid=(steps,),
            in_specs=[by_member, cols(block)]
            + [by_core] * 4
            + [whole(a) for a in pieces]
            + [cols(span), cols(1), cols(span)],
            out_specs=cols(span),
            scratch_shapes=[
                pltpu.VMEM((span, 4 * block), jnp.bfloat16),
                pltpu.VMEM((4 * block, tile), jnp.bfloat16),
            ],
        ),
        compiler_params=pltpu.CompilerParams(vmem_limit_bytes=32 * MIB),
        cost_estimate=pl.CostEstimate(
            flops=2 * span * 4 * block * share, bytes_accessed=7 * MIB, transcendentals=0
        ),
    )(where, out_weight, w_twin, *far, *pieces, residual, gate, fresh)


def on_device(hidden, levels, frame_counts, mod_weight, qkv_weight, out_weight, fresh):
    rows, width = hidden.shape
    slot = lax.axis_index("queue")
    queue_len = lax.axis_size("queue")
    member = lax.axis_index("heads")
    members = lax.axis_size("heads")
    share = width // members
    parity, core, y_hi = slot % 2, member % 2, member // 2
    z_half = (slot // 8) % 2
    half = rows // 2
    route = functools.partial(routed, queue_len=queue_len, members=members)
    twin = lambda a: route(a, target=lambda s, y, k: (s, y, 1 - k))

    mine = lax.dynamic_slice(hidden, (core * half, 0), (half, width))
    other_mine = route(mine, target=lambda s, y, k: (s ^ 1, y ^ k, k))
    own_share = lax.dynamic_slice_in_dim(hidden, member * share, share, 1)
    residual_near = route(own_share, target=lambda s, y, k: (s - 2 if s % 2 == 0 else s, y, k))

    modulation = jnp.dot(
        embed_levels(levels, mod_weight.shape[0]), mod_weight, preferred_element_type=jnp.float32
    )
    columns = modulation.shape[1]
    swapped = modulation.reshape(queue_len // 2, 2, columns)[:, ::-1].reshape(queue_len, columns)
    following = jnp.roll(modulation, -1, axis=0)
    rows_three = lax.all_to_all(
        jnp.concatenate([modulation, swapped, following], axis=1), "queue", 0, 0, tiled=True
    )
    mod_own, mod_other, mod_next = [
        rows_three[:, i * columns : (i + 1) * columns].reshape(1, queue_len * columns) for i in range(3)
    ]
    gate = lax.dynamic_slice_in_dim(mod_next, 2 * width + member * share, share, 1)

    other_twin = twin(other_mine)
    residual = route(residual_near, target=lambda s, y, k: (s ^ 1, y, k))
    far_mine = lax.dynamic_slice(
        out_weight, (z_half * (out_weight.shape[0] // 2), (1 - y_hi) * 2 * share), (out_weight.shape[0] // 2, 2 * share)
    )
    w_far0 = route(far_mine, target=lambda s, y, k: (s ^ 1, 1 - y, k))
    w_far1 = route(w_far0, target=lambda s, y, k: (s ^ 8, y, k))
    w_twin = twin(lax.dynamic_slice_in_dim(out_weight, (y_hi * 2 + 1 - core) * share, share, 1))
    w_fart0 = twin(w_far0)
    w_fart1 = twin(w_far1)

    def qkv_of(order, first, second, mod):
        return qkv(
            jnp.stack([parity, order]).astype(jnp.int32),
            first,
            second,
            1.0 + mod[:, width : 2 * width],
            mod[:, :width],
            qkv_weight,
        )

    q_own, kv_own = qkv_of(jnp.int32(0), hidden[:half], hidden[half:], mod_own)
    kv_far = route(kv_own, target=lambda s, y, k: (s - 2 if s % 2 == 0 else s + 2, y, k))
    q_other, kv_other = qkv_of(core, other_mine, other_twin, mod_other)
    kv_back = route(kv_other, target=lambda s, y, k: (s + 2 if s % 2 == 0 else s - 2, y, k))

    counts_pad = jnp.pad(frame_counts.astype(jnp.int32), (2, 2))
    step = 1 - 2 * parity
    count_at = lambda where: lax.dynamic_slice(counts_pad, (where + 2,), (1,))
    counts_pair = jnp.concatenate([count_at(slot), count_at(slot + step)])
    oo, mo, lo, ot, mt, lt = local_attention(counts_pair, q_own, q_other, kv_own, kv_other)
    attn_other = remote_attention(count_at(slot + 2 * step), q_other, kv_far, ot, mt, lt)
    p3 = route(attn_other, target=lambda s, y, k: (s if s % 2 == 0 else s - 2, 1 - y, k))
    p4 = route(attn_other, target=lambda s, y, k: (s if s % 2 == 0 else s - 2, y, k))
    attn_own = remote_attention(count_at(slot - step), q_own, kv_back, oo, mo, lo)
    p1 = route(attn_own, target=lambda s, y, k: (s - 1, y, k))
    p2 = route(attn_own, target=lambda s, y, k: (s - 1, 1 - y, k))
    pieces = [p1, p2, p3, p4]
    pieces = pieces + [twin(a) for a in pieces]

    where = jnp.stack(
        [member, parity, (slot == queue_len - 1).astype(jnp.int32), z_half, core]
    ).astype(jnp.int32)
    return out_projection(
        where, out_weight, w_twin, [w_far0, w_far1, w_fart0, w_fart1], pieces, residual, gate, fresh
    )


def solution(mesh):
    placed = (
        P("queue", None),
        P(),
        P(),
        P(None, "queue"),
        P(None, None, "heads"),
        P("heads", None),
        P(None, "heads"),
    )
    return jax.shard_map(
        on_device, mesh=mesh, in_specs=placed, out_specs=P("queue", "heads"), check_vma=False
    )
```

time: 508 us -> 148 us (0.29)
  waiting for transfers between devices: 426 us -> 27.2 us
  matrix products: 34.7 us -> 0.18 us
  starting transfers between devices: 12.8 us -> 46.4 us
  local copies, waits for them, and re-layouts: 5.62 us -> 38.1 us
  Pallas kernels: 0 us -> 31 us
  between operations: 14.2 us -> 0.45 us
  other arithmetic: 13.3 us -> 2.54 us
    all_gather x1 -> x0, waiting for transfers between devices: 272 us -> none  [on_device(): lax.all_gather(mod_weight, 'queue', axis=1, tiled=True)]
    reduce_scatter x1 -> x0, waiting for transfers between devices: 117 us -> none  [on_device(): lax.psum_scatter(partial_proj, 'heads', scatter_dimension=1, tiled=True)]
    pallas_call x0 -> x6, Pallas kernels: none -> 31 us  [the longest x2 13 us: qkv(): pl.pallas_call(qkv_kernel, out_shape=(jax.ShapeDtypeStruct((2 * half, 2 *...]
    unnamed x12 -> x59, local copies, waits for them, and re-layouts: 0.64 us -> 25.4 us
    dot_general x4 -> x1, matrix products: 24.6 us -> 0.18 us  [on_device(): jnp.dot(embed_levels(levels, mod_weight.shape[0]), mod_weight, preferred_...]
    ppermute x3 -> x19, starting transfers between devices: 12.7 us -> 34.9 us  [routed(): return lax.ppermute(array, BOTH, pairs)]
    all_to_all x0 -> x1, starting transfers between devices: none -> 11.5 us  [on_device(): lax.all_to_all(jnp.concatenate([modulation, swapped, following], axis=1),...]
    sub x1 -> x0, matrix products: 10.1 us -> none  [block_attention(): weights = jnp.where(live[None, None, :], jnp.exp(scores - peak), 0.0)]
  transfers between devices with their start and end apart: 5 -> 20, of which waited for: 5 -> 5; matrix products, arithmetic and copies ran while one was open for 2% -> 8% of each run, Pallas kernels for 0% -> 18%
where the time goes in v1:
time: 148 us; the launch traced here: 146 us
  starting transfers between devices  46.4 us (31%)
  local copies, waits for them, and re-layouts  38.1 us (26%)
  Pallas kernels  31 us (21%)
  waiting for transfers between devices  27.2 us (18%)
  other arithmetic  2.54 us (2%)
    ppermute x19, starting transfers between devices, routed(): return lax.ppermute(array, BOTH, pairs)  34.9 us
    ppermute x19, waiting for transfers between devices, routed(): return lax.ppermute(array, BOTH, pairs)  27.2 us
    unnamed x59, local copies, waits for them, and re-layouts  25.4 us
    pallas_call x2, Pallas kernels, qkv(): pl.pallas_call(qkv_kernel, out_shape=(jax.ShapeDtypeStruct((2 * half, 2 *...  13 us
    all_to_all x1, starting transfers between devices, on_device(): lax.all_to_all(jnp.concatenate([modulation, swapped, following], axis=1),...  11.5 us
    pallas_call x1, Pallas kernels, local_attention(): pl.pallas_call(local_kernel, out_shape=(part,) * 6, in_specs=[pl.BlockSpe...  6.45 us
    pallas_call x2, Pallas kernels, remote_attention(): pl.pallas_call(remote_kernel, out_shape=jax.ShapeDtypeStruct((span + span...  6.14 us
    pallas_call x1, Pallas kernels, out_projection(): pl.pallas_call(out_kernel, out_shape=jax.ShapeDtypeStruct((span, share),...  5.35 us
  transfers between devices with their start and end apart: 20, of which 5 were waited for; matrix products, arithmetic and copies ran while one was open for 8% of the time, Pallas kernels for 18%

profile of v1, /device:TPU:111, one launch (start us, length us, event | category | flops | bytes accessed | tf_op | source)
XLA Modules:
  0.0 145.8 jit_solution(15124631360380930027)
XLA Ops:
  0.0 3.9 %constant_dynamic-slice_fusion.2 = (bf16[256,3072]{1,0:T(8,128)(2,1)}, bf16[256,3072]{1,0:T(8,128)(2,1)S(1)}, bf16[256,3072]{1,0:T(8,128)(2,1)S(1)}) fusion(bf16[512,3072]{1,0:T(8,128)(2,1)} %param.7, s32[]{:T(128)S(6)} %select_n.61), kind=kLoop, calls=%fused_computation.12 | loop fusion | bytes 9437188 | tf_op jit(solution)/shard_map/dynamic_slice | solution.py:312
  8.2 11.5 %all-to-all-start = ((f32[64,1,432]{2,1,0:T(1,128)}), f32[64,1,432]{2,1,0:T(1,128)S(1)}, u32[]{:S(2)}, u32[]{:S(2)}) async-start(f32[64,1,432]{2,1,0:T(1,128)} %copy.8), calls=%async_computation | async-start | bytes 262144 | tf_op jit(solution)/shard_map/all_to_all | solution.py:323
  19.7 1.9 %dynamic_slice.28 = bf16[192,1536]{1,0:T(8,128)(2,1)} dynamic-slice(bf16[384,3072]{1,0:T(8,128)(2,1)} %refs_0_.1, s32[]{:T(128)S(6)} %select_n.58, s32[]{:T(128)S(6)} %select_n.59), dynamic_slice_sizes={192,1536} | dynamic-slice | bytes 1179652 | tf_op jit(solution)/shard_map/dynamic_slice | solution.py:333
  21.7 1.9 %constant_dynamic-slice_fusion.3 = bf16[384,768]{1,0:T(8,128)(2,1)} fusion(bf16[384,3072]{1,0:T(8,128)(2,1)} %refs_0_.1, s32[]{:T(128)S(6)} %select_n.57), kind=kLoop, calls=%fused_computation.13 | loop fusion | bytes 1179652 | tf_op jit(solution)/shard_map/dynamic_slice | solution.py:338
  25.3 2.1 %constant_dynamic-slice_fusion.1 = bf16[512,768]{1,0:T(8,128)(2,1)} fusion(bf16[512,3072]{1,0:T(8,128)(2,1)} %param.7, s32[]{:T(128)S(6)} %select_n.65), kind=kLoop, calls=%fused_computation.11 | loop fusion | bytes 1572868 | tf_op jit(solution)/shard_map/dynamic_slice | solution.py:314
  27.3 7.4 %collective-permute-start.17 = (bf16[512,768]{1,0:T(8,128)(2,1)}, bf16[512,768]{1,0:T(8,128)(2,1)}, u32[]{:S(2)}, u32[]{:S(2)}) collective-permute-start(bf16[512,768]{1,0:T(8,128)(2,1)} %constant_dynamic-slice_fusion.1), channel_id=1, source_target_pairs={{4,4},{5,5},{6,6},{7,7},{8,0},{9,1},{10,2},{11,3},{12,12},{13,13},... | collective-permute-start | bytes 2359304 | tf_op jit(solution)/shard_map/ppermute | solution.py:35
  37.2 3.0 %copy-done.1 = bf16[3,3072,384]{2,1,0:T(8,128)(2,1)S(1)} copy-done((bf16[3,3072,384]{2,1,0:T(8,128)(2,1)S(1)}, bf16[3,3072,384]{2,1,0:T(8,128)(2,1)}, u32[]{:S(2)}) %copy-start.1) | copy-done | bytes 7077912
  40.2 5.8 %shard_map.73 = (bf16[512,256]{1,0:T(8,128)(2,1)S(1)}, bf16[512,384]{1,0:T(8,128)(2,1)S(1)}) custom-call(s32[2]{0:T(128)S(1)} %pad_add_fusion.where_ref, bf16[256,3072]{1,0:T(8,128)(2,1)S(1)} %get-tuple-element.27.first_ref, bf16[256,3072]{1,0:T(8,128)(2,1)S(1)} %get-tuple-element.26.second_ref, f32[1,3072]{1,0:T(1,128)S(1)} %get-tuple-element.34.scale_ref, ...), custom_call_target="tpu_custom_call" | custom-call | flops 2415919104 | bytes 9437184 | tf_op jit(solution)/shard_map/pallas_call | solution.py:96
  47.6 4.3 %collective-permute-start.10 = (bf16[512,384]{1,0:T(8,128)(2,1)}, bf16[512,384]{1,0:T(8,128)(2,1)S(1)}, u32[]{:S(2)}, u32[]{:S(2)}) collective-permute-start(bf16[512,384]{1,0:T(8,128)(2,1)} %copy-done.23), channel_id=1, source_target_pairs={{4,12},{5,13},{6,14},{7,15},{8,0},{9,1},{10,2},{11,3},{12,20},{13,... | collective-permute-start | bytes 1179656 | tf_op jit(solution)/shard_map/ppermute | solution.py:35
  53.0 19.7 %collective-permute-done.2.refs_3_ = bf16[192,1536]{1,0:T(8,128)(2,1)} collective-permute-done((bf16[192,1536]{1,0:T(8,128)(2,1)}, bf16[192,1536]{1,0:T(8,128)(2,1)}, u32[]{:S(2)}, u32[]{:S(2)}) %collective-permute-start.2) | collective-permute-done | bytes 589856 | tf_op jit(solution)/shard_map/ppermute | solution.py:35
  74.0 3.0 %copy-done.2 = bf16[3,3072,384]{2,1,0:T(8,128)(2,1)S(1)} copy-done((bf16[3,3072,384]{2,1,0:T(8,128)(2,1)S(1)}, bf16[3,3072,384]{2,1,0:T(8,128)(2,1)}, u32[]{:S(2)}) %copy-start.2) | copy-done | bytes 7077912
  77.0 7.2 %shard_map.74 = (bf16[512,256]{1,0:T(8,128)(2,1)S(1)}, bf16[512,384]{1,0:T(8,128)(2,1)S(1)}) custom-call(s32[2]{0:T(128)S(1)} %get-tuple-element.41.where_ref, bf16[256,3072]{1,0:T(8,128)(2,1)} %collective-permute-done.5.first_ref, bf16[256,3072]{1,0:T(8,128)(2,1)} %collective-permute-done.6.second_ref, f32[1,3072]{1,0:T(1,128)S(1)} %get-tuple-element.32.scale_ref, ...), custom_call_target="tpu_custom_call" | custom-call | flops 2415919104 | bytes 9437184 | tf_op jit(solution)/shard_map/pallas_call | solution.py:96
  84.2 1.9 %collective-permute-start.7 = (bf16[512,384]{1,0:T(8,128)(2,1)S(1)}, bf16[512,384]{1,0:T(8,128)(2,1)S(1)}, u32[]{:S(2)}, u32[]{:S(2)}) collective-permute-start(bf16[512,384]{1,0:T(8,128)(2,1)S(1)} %get-tuple-element.16.kvt_ref), channel_id=1, source_target_pairs={{0,8},{1,9},{2,10},{3,11},{8,16},{9,17},{10,18},{11,19},{12,4},{13... | collective-permute-start | bytes 1179656 | tf_op jit(solution)/shard_map/ppermute | solution.py:35
  86.2 6.5 %shard_map.75 = (f32[512,256]{1,0:T(8,128)S(1)}, f32[512,256]{1,0:T(8,128)S(1)}, f32[512,256]{1,0:T(8,128)S(1)}, f32[512,256]{1,0:T(8,128)S(1)}, f32[512,256]{1,0:T(8,128)S(1)}, /*index=5*/f32[512,256]{1,0:T(8,128)S(1)}) custom-call(s32[2]{0:T(128)S(1)} %get-tuple-element.42.counts_ref, bf16[512,256]{1,0:T(8,128)(2,1)S(1)} %copy-done.26, ...), custom_call_target="tpu_custom_call" | custom-call | flops 6442450944 | bytes 5242880 | tf_op jit(solution)/shard_map/pallas_call | solution.py:167
  92.6 3.0 %shard_map.77 = bf16[768,128]{1,0:T(8,128)(2,1)S(1)} custom-call(s32[1]{0:T(128)} %get-tuple-element.37.count_ref, bf16[512,256]{1,0:T(8,128)(2,1)S(1)} %get-tuple-element.17.qt_ref.q_ref, bf16[512,384]{1,0:T(8,128)(2,1)S(1)} %collective-permute-done.10.kv_ref, f32[512,256]{1,0:T(8,128)S(1)} %get-tuple-element.22.o_ref, ...), custom_call_target="tpu_custom_call" | custom-call | flops 805306368 | bytes 2097152 | tf_op jit(solution)/shard_map/pallas_call | solution.py:209
  95.7 4.5 %collective-permute-done.7.kv_ref = bf16[512,384]{1,0:T(8,128)(2,1)S(1)} collective-permute-done((bf16[512,384]{1,0:T(8,128)(2,1)S(1)}, bf16[512,384]{1,0:T(8,128)(2,1)S(1)}, u32[]{:S(2)}, u32[]{:S(2)}) %collective-permute-start.7) | collective-permute-done | bytes 393248 | tf_op jit(solution)/shard_map/ppermute | solution.py:35
  100.2 1.9 %collective-permute-start.11 = (bf16[768,128]{1,0:T(8,128)(2,1)S(1)}, bf16[768,128]{1,0:T(8,128)(2,1)S(1)}, u32[]{:S(2)}, u32[]{:S(2)}) collective-permute-start(bf16[768,128]{1,0:T(8,128)(2,1)S(1)} %shard_map.77), channel_id=1, source_target_pairs={{0,2},{1,3},{2,0},{3,1},{8,10},{9,11},{10,8},{11,9},{12,6},{13,7},... | collective-permute-start | bytes 589832 | tf_op jit(solution)/shard_map/ppermute | solution.py:35
  102.1 3.1 %shard_map.76 = bf16[768,128]{1,0:T(8,128)(2,1)S(1)} custom-call(s32[1]{0:T(128)} %get-tuple-element.40.count_ref, bf16[512,256]{1,0:T(8,128)(2,1)S(1)} %copy-done.26, bf16[512,384]{1,0:T(8,128)(2,1)S(1)} %collective-permute-done.7.kv_ref, f32[512,256]{1,0:T(8,128)S(1)} %get-tuple-element.19.o_ref, f32[512,256]{1,0:T(8,128)S(1)} %get-tuple-element.20.m_ref, ...), custom_call_target="tpu_custom_call" | custom-call | flops 805306368 | bytes 2097152 | tf_op jit(solution)/shard_map/pallas_call | solution.py:209
  105.2 1.9 %collective-permute-start.12 = (bf16[768,128]{1,0:T(8,128)(2,1)S(1)}, bf16[768,128]{1,0:T(8,128)(2,1)S(1)}, u32[]{:S(2)}, u32[]{:S(2)}) collective-permute-start(bf16[768,128]{1,0:T(8,128)(2,1)S(1)} %shard_map.77), channel_id=1, source_target_pairs={{0,0},{1,1},{2,2},{3,3},{8,8},{9,9},{10,10},{11,11},{12,4},{13,5},... | collective-permute-start | bytes 589832 | tf_op jit(solution)/shard_map/ppermute | solution.py:35
  108.0 1.9 %collective-permute-start.8 = (bf16[768,128]{1,0:T(8,128)(2,1)S(1)}, bf16[768,128]{1,0:T(8,128)(2,1)S(1)}, u32[]{:S(2)}, u32[]{:S(2)}) collective-permute-start(bf16[768,128]{1,0:T(8,128)(2,1)S(1)} %shard_map.76), channel_id=1, source_target_pairs={{4,0},{5,1},{6,2},{7,3},{8,4},{9,5},{10,6},{11,7},{12,8},{13,9},{1... | collective-permute-start | bytes 589832 | tf_op jit(solution)/shard_map/ppermute | solution.py:35
  110.8 2.6 %collective-permute-start.9 = (bf16[768,128]{1,0:T(8,128)(2,1)S(1)}, bf16[768,128]{1,0:T(8,128)(2,1)S(1)}, u32[]{:S(2)}, u32[]{:S(2)}) collective-permute-start(bf16[768,128]{1,0:T(8,128)(2,1)S(1)} %shard_map.76), channel_id=1, source_target_pairs={{4,2},{5,3},{6,0},{7,1},{8,6},{9,7},{10,4},{11,5},{12,10},{13,11},... | collective-permute-start | bytes 589832 | tf_op jit(solution)/shard_map/ppermute | solution.py:35
  113.4 1.8 %collective-permute-start.15 = (bf16[768,128]{1,0:T(8,128)(2,1)S(1)}, bf16[768,128]{1,0:T(8,128)(2,1)S(1)}, u32[]{:S(2)}, u32[]{:S(2)}) collective-permute-start(bf16[768,128]{1,0:T(8,128)(2,1)S(1)} %collective-permute-done.11.refs_8_), channel_id=1, source_target_pairs={{0,1},{1,0},{2,3},{3,2},{4,5},{5,4},{6,7},{7,6},{8,9},{9,8},{10,11... | collective-permute-start | bytes 589832 | tf_op jit(solution)/shard_map/ppermute | solution.py:35
  119.7 2.7 %collective-permute-start.13 = (bf16[768,128]{1,0:T(8,128)(2,1)S(1)}, bf16[768,128]{1,0:T(8,128)(2,1)S(1)}, u32[]{:S(2)}, u32[]{:S(2)}) collective-permute-start(bf16[768,128]{1,0:T(8,128)(2,1)S(1)} %collective-permute-done.8.refs_6_), channel_id=1, source_target_pairs={{0,1},{1,0},{2,3},{3,2},{4,5},{5,4},{6,7},{7,6},{8,9},{9,8},{10,11... | collective-permute-start | bytes 589832 | tf_op jit(solution)/shard_map/ppermute | solution.py:35
  140.4 5.4 %shard_map.78 = bf16[512,768]{1,0:T(8,128)(2,1)} custom-call(s32[5]{0:T(128)S(1)} %stack.36.where_ref, bf16[384,3072]{1,0:T(8,128)(2,1)S(1)} %copy-done.3, bf16[384,768]{1,0:T(8,128)(2,1)} %collective-permute-done.refs_1_, bf16[192,1536]{1,0:T(8,128)(2,1)} %collective-permute-done.1.refs_2_, bf16[192,1536]{1,0:T(8,128)(2,1)} %collective-permute-done.2.refs_3_, ...), custom_call_target="tpu_custom_call" | custom-call | flops 1207959552 | bytes 7340032 | tf_op jit(solution)/shard_map/pallas_call | solution.py:276
  (107 shorter events, 36.5 us)
Async XLA Ops:
  0.0 5.5 %copy-start = (bf16[512,144]{0,1:T(8,128)(2,1)S(1)}, bf16[512,144]{0,1:T(8,128)(2,1)}, u32[]{:S(2)}) copy-start(bf16[512,144]{0,1:T(8,128)(2,1)} %param.10) | copy-start | bytes 442372
  3.9 33.2 %collective-permute-start.5 = (bf16[256,3072]{1,0:T(8,128)(2,1)}, bf16[256,3072]{1,0:T(8,128)(2,1)}, u32[]{:S(2)}, u32[]{:S(2)}) collective-permute-start(bf16[256,3072]{1,0:T(8,128)(2,1)} %get-tuple-element.25), channel_id=1, source_target_pairs={{0,4},{1,7},{2,6},{3,5},{4,0},{5,3},{6,2},{7,1},{8,12},{9,15},{10,... | collective-permute-start | bytes 4718600 | tf_op jit(solution)/shard_map/ppermute | solution.py:35
  8.2 28.6 %all-to-all-start = ((f32[64,1,432]{2,1,0:T(1,128)}), f32[64,1,432]{2,1,0:T(1,128)S(1)}, u32[]{:S(2)}, u32[]{:S(2)}) async-start(f32[64,1,432]{2,1,0:T(1,128)} %copy.8), calls=%async_computation | async-start | bytes 262144 | tf_op jit(solution)/shard_map/all_to_all | solution.py:323
  21.6 13.1 %copy-start.27 = (s32[64]{0:T(128)S(1)}, s32[64]{0:T(128)}, u32[]{:S(2)}) copy-start(s32[64]{0:T(128)} %param.9) | copy-start | bytes 772
  21.7 30.3 %collective-permute-start.1 = (bf16[192,1536]{1,0:T(8,128)(2,1)}, bf16[192,1536]{1,0:T(8,128)(2,1)}, u32[]{:S(2)}, u32[]{:S(2)}) collective-permute-start(bf16[192,1536]{1,0:T(8,128)(2,1)} %dynamic_slice.28), channel_id=1, source_target_pairs={{0,6},{1,7},{2,4},{3,5},{4,2},{5,3},{6,0},{7,1},{8,14},{9,15},{10,... | collective-permute-start | bytes 1769480 | tf_op jit(solution)/shard_map/ppermute | solution.py:35
  23.6 81.6 %collective-permute-start = (bf16[384,768]{1,0:T(8,128)(2,1)}, bf16[384,768]{1,0:T(8,128)(2,1)}, u32[]{:S(2)}, u32[]{:S(2)}) collective-permute-start(bf16[384,768]{1,0:T(8,128)(2,1)} %constant_dynamic-slice_fusion.3), channel_id=1, source_target_pairs={{0,1},{1,0},{2,3},{3,2},{4,5},{5,4},{6,7},{7,6},{8,9},{9,8},{10,11... | collective-permute-start | bytes 1769480 | tf_op jit(solution)/shard_map/ppermute | solution.py:35
  27.3 24.8 %collective-permute-start.17 = (bf16[512,768]{1,0:T(8,128)(2,1)}, bf16[512,768]{1,0:T(8,128)(2,1)}, u32[]{:S(2)}, u32[]{:S(2)}) collective-permute-start(bf16[512,768]{1,0:T(8,128)(2,1)} %constant_dynamic-slice_fusion.1), channel_id=1, source_target_pairs={{4,4},{5,5},{6,6},{7,7},{8,0},{9,1},{10,2},{11,3},{12,12},{13,13},... | collective-permute-start | bytes 2359304 | tf_op jit(solution)/shard_map/ppermute | solution.py:35
  37.1 35.6 %collective-permute-start.6 = (bf16[256,3072]{1,0:T(8,128)(2,1)}, bf16[256,3072]{1,0:T(8,128)(2,1)}, u32[]{:S(2)}, u32[]{:S(2)}) collective-permute-start(bf16[256,3072]{1,0:T(8,128)(2,1)} %collective-permute-done.5.first_ref), channel_id=1, source_target_pairs={{0,1},{1,0},{2,3},{3,2},{4,5},{5,4},{6,7},{7,6},{8,9},{9,8},{10,11... | collective-permute-start | bytes 4718600 | tf_op jit(solution)/shard_map/ppermute | solution.py:35
  47.6 36.6 %collective-permute-start.10 = (bf16[512,384]{1,0:T(8,128)(2,1)}, bf16[512,384]{1,0:T(8,128)(2,1)S(1)}, u32[]{:S(2)}, u32[]{:S(2)}) collective-permute-start(bf16[512,384]{1,0:T(8,128)(2,1)} %copy-done.23), channel_id=1, source_target_pairs={{4,12},{5,13},{6,14},{7,15},{8,0},{9,1},{10,2},{11,3},{12,20},{13,... | collective-permute-start | bytes 1179656 | tf_op jit(solution)/shard_map/ppermute | solution.py:35
  52.0 20.7 %collective-permute-start.2 = (bf16[192,1536]{1,0:T(8,128)(2,1)}, bf16[192,1536]{1,0:T(8,128)(2,1)}, u32[]{:S(2)}, u32[]{:S(2)}) collective-permute-start(bf16[192,1536]{1,0:T(8,128)(2,1)} %collective-permute-done.1.refs_2_), channel_id=1, source_target_pairs={{0,32},{1,33},{2,34},{3,35},{4,36},{5,37},{6,38},{7,39},{8,40},{9,... | collective-permute-start | bytes 1769480 | tf_op jit(solution)/shard_map/ppermute | solution.py:35
  52.1 55.1 %collective-permute-start.3 = (bf16[192,1536]{1,0:T(8,128)(2,1)}, bf16[192,1536]{1,0:T(8,128)(2,1)S(1)}, u32[]{:S(2)}, u32[]{:S(2)}) collective-permute-start(bf16[192,1536]{1,0:T(8,128)(2,1)} %collective-permute-done.1.refs_2_), channel_id=1, source_target_pairs={{0,1},{1,0},{2,3},{3,2},{4,5},{5,4},{6,7},{7,6},{8,9},{9,8},{10,11... | collective-permute-start | bytes 1769480 | tf_op jit(solution)/shard_map/ppermute | solution.py:35
  72.6 37.3 %collective-permute-start.18 = (bf16[512,768]{1,0:T(8,128)(2,1)}, bf16[512,768]{1,0:T(8,128)(2,1)S(1)}, u32[]{:S(2)}, u32[]{:S(2)}) collective-permute-start(bf16[512,768]{1,0:T(8,128)(2,1)} %collective-permute-done.17), channel_id=1, source_target_pairs={{0,4},{1,5},{2,6},{3,7},{4,0},{5,1},{6,2},{7,3},{8,12},{9,13},{10,... | collective-permute-start | bytes 2359304 | tf_op jit(solution)/shard_map/ppermute | solution.py:35
  72.6 53.6 %collective-permute-start.4 = (bf16[192,1536]{1,0:T(8,128)(2,1)}, bf16[192,1536]{1,0:T(8,128)(2,1)}, u32[]{:S(2)}, u32[]{:S(2)}) collective-permute-start(bf16[192,1536]{1,0:T(8,128)(2,1)} %collective-permute-done.2.refs_3_), channel_id=1, source_target_pairs={{0,1},{1,0},{2,3},{3,2},{4,5},{5,4},{6,7},{7,6},{8,9},{9,8},{10,11... | collective-permute-start | bytes 1769480 | tf_op jit(solution)/shard_map/ppermute | solution.py:35
  77.0 9.2 %copy-start.24 = (bf16[512,384]{1,0:T(8,128)(2,1)S(1)}, bf16[512,384]{1,0:T(8,128)(2,1)}, u32[]{:S(2)}) copy-start(bf16[512,384]{1,0:T(8,128)(2,1)} %copy-done.23) | copy-start | bytes 1179652
  77.0 9.2 %copy-start.26 = (bf16[512,256]{1,0:T(8,128)(2,1)S(1)}, bf16[512,256]{1,0:T(8,128)(2,1)}, u32[]{:S(2)}) copy-start(bf16[512,256]{1,0:T(8,128)(2,1)} %copy-done.25) | copy-start | bytes 786436
  84.2 16.0 %collective-permute-start.7 = (bf16[512,384]{1,0:T(8,128)(2,1)S(1)}, bf16[512,384]{1,0:T(8,128)(2,1)S(1)}, u32[]{:S(2)}, u32[]{:S(2)}) collective-permute-start(bf16[512,384]{1,0:T(8,128)(2,1)S(1)} %get-tuple-element.16.kvt_ref), channel_id=1, source_target_pairs={{0,8},{1,9},{2,10},{3,11},{8,16},{9,17},{10,18},{11,19},{12,4},{13... | collective-permute-start | bytes 1179656 | tf_op jit(solution)/shard_map/ppermute | solution.py:35
  100.2 13.2 %collective-permute-start.11 = (bf16[768,128]{1,0:T(8,128)(2,1)S(1)}, bf16[768,128]{1,0:T(8,128)(2,1)S(1)}, u32[]{:S(2)}, u32[]{:S(2)}) collective-permute-start(bf16[768,128]{1,0:T(8,128)(2,1)S(1)} %shard_map.77), channel_id=1, source_target_pairs={{0,2},{1,3},{2,0},{3,1},{8,10},{9,11},{10,8},{11,9},{12,6},{13,7},... | collective-permute-start | bytes 589832 | tf_op jit(solution)/shard_map/ppermute | solution.py:35
  105.2 11.4 %collective-permute-start.12 = (bf16[768,128]{1,0:T(8,128)(2,1)S(1)}, bf16[768,128]{1,0:T(8,128)(2,1)S(1)}, u32[]{:S(2)}, u32[]{:S(2)}) collective-permute-start(bf16[768,128]{1,0:T(8,128)(2,1)S(1)} %shard_map.77), channel_id=1, source_target_pairs={{0,0},{1,1},{2,2},{3,3},{8,8},{9,9},{10,10},{11,11},{12,4},{13,5},... | collective-permute-start | bytes 589832 | tf_op jit(solution)/shard_map/ppermute | solution.py:35
  108.0 11.7 %collective-permute-start.8 = (bf16[768,128]{1,0:T(8,128)(2,1)S(1)}, bf16[768,128]{1,0:T(8,128)(2,1)S(1)}, u32[]{:S(2)}, u32[]{:S(2)}) collective-permute-start(bf16[768,128]{1,0:T(8,128)(2,1)S(1)} %shard_map.76), channel_id=1, source_target_pairs={{4,0},{5,1},{6,2},{7,3},{8,4},{9,5},{10,6},{11,7},{12,8},{13,9},{1... | collective-permute-start | bytes 589832 | tf_op jit(solution)/shard_map/ppermute | solution.py:35
  110.8 13.1 %collective-permute-start.9 = (bf16[768,128]{1,0:T(8,128)(2,1)S(1)}, bf16[768,128]{1,0:T(8,128)(2,1)S(1)}, u32[]{:S(2)}, u32[]{:S(2)}) collective-permute-start(bf16[768,128]{1,0:T(8,128)(2,1)S(1)} %shard_map.76), channel_id=1, source_target_pairs={{4,2},{5,3},{6,0},{7,1},{8,6},{9,7},{10,4},{11,5},{12,10},{13,11},... | collective-permute-start | bytes 589832 | tf_op jit(solution)/shard_map/ppermute | solution.py:35
  113.4 12.8 %collective-permute-start.15 = (bf16[768,128]{1,0:T(8,128)(2,1)S(1)}, bf16[768,128]{1,0:T(8,128)(2,1)S(1)}, u32[]{:S(2)}, u32[]{:S(2)}) collective-permute-start(bf16[768,128]{1,0:T(8,128)(2,1)S(1)} %collective-permute-done.11.refs_8_), channel_id=1, source_target_pairs={{0,1},{1,0},{2,3},{3,2},{4,5},{5,4},{6,7},{7,6},{8,9},{9,8},{10,11... | collective-permute-start | bytes 589832 | tf_op jit(solution)/shard_map/ppermute | solution.py:35
  116.7 10.3 %collective-permute-start.16 = (bf16[768,128]{1,0:T(8,128)(2,1)S(1)}, bf16[768,128]{1,0:T(8,128)(2,1)S(1)}, u32[]{:S(2)}, u32[]{:S(2)}) collective-permute-start(bf16[768,128]{1,0:T(8,128)(2,1)S(1)} %collective-permute-done.12.refs_9_), channel_id=1, source_target_pairs={{0,1},{1,0},{2,3},{3,2},{4,5},{5,4},{6,7},{7,6},{8,9},{9,8},{10,11... | collective-permute-start | bytes 589832 | tf_op jit(solution)/shard_map/ppermute | solution.py:35
  119.7 7.9 %collective-permute-start.13 = (bf16[768,128]{1,0:T(8,128)(2,1)S(1)}, bf16[768,128]{1,0:T(8,128)(2,1)S(1)}, u32[]{:S(2)}, u32[]{:S(2)}) collective-permute-start(bf16[768,128]{1,0:T(8,128)(2,1)S(1)} %collective-permute-done.8.refs_6_), channel_id=1, source_target_pairs={{0,1},{1,0},{2,3},{3,2},{4,5},{5,4},{6,7},{7,6},{8,9},{9,8},{10,11... | collective-permute-start | bytes 589832 | tf_op jit(solution)/shard_map/ppermute | solution.py:35
  123.9 4.4 %collective-permute-start.14 = (bf16[768,128]{1,0:T(8,128)(2,1)S(1)}, bf16[768,128]{1,0:T(8,128)(2,1)S(1)}, u32[]{:S(2)}, u32[]{:S(2)}) collective-permute-start(bf16[768,128]{1,0:T(8,128)(2,1)S(1)} %collective-permute-done.9.refs_7_), channel_id=1, source_target_pairs={{0,1},{1,0},{2,3},{3,2},{4,5},{5,4},{6,7},{7,6},{8,9},{9,8},{10,11... | collective-permute-start | bytes 589832 | tf_op jit(solution)/shard_map/ppermute | solution.py:35
  (25 other events, 30.6 us)

commit v2 on v0

v2 whole, which is shorter than its diff:
```python
import functools
import math

import jax
import jax.numpy as jnp
from jax import lax
from jax.experimental import pallas as pl
from jax.experimental.pallas import tpu as pltpu
from jax.sharding import PartitionSpec as P

HD = 64
P_SIZE = 256
PAIR = 2 * HD
NEG = -1e30
BOTH = ("queue", "heads")
MIB = 1024 * 1024


def embed_levels(levels, width):
    halfway = width // 2
    freqs = jnp.exp(-math.log(10000.0) * jnp.arange(halfway, dtype=jnp.float32) / halfway)
    angles = levels.astype(jnp.float32)[:, None] * freqs[None, :]
    return jax.nn.silu(jnp.concatenate([jnp.cos(angles), jnp.sin(angles)], axis=1)).astype(
        jnp.bfloat16
    )


def routed(array, queue_len, members, target):
    pairs = []
    for slot in range(queue_len):
        for member in range(members):
            goal = target(slot, member // 2, member % 2)
            if goal is not None and 0 <= goal[0] < queue_len:
                pairs.append((slot * members + member, goal[0] * members + goal[1] * 2 + goal[2]))
    return lax.ppermute(array, BOTH, pairs)


def low_lanes(shape):
    return lax.broadcasted_iota(jnp.int32, shape, len(shape) - 1) < HD


def copies_of(source, target, sems, chunks, first=0):
    step = source.shape[0] // chunks
    return [
        pltpu.make_async_copy(
            source.at[pl.ds(i * step, step), :], target.at[pl.ds(i * step, step), :], sems.at[first + i]
        )
        for i in range(chunks)
    ]


def any_spec():
    return pl.BlockSpec(memory_space=pl.ANY)


def far(array):
    return pltpu.with_memory_space_constraint(array, pltpu.HBM)


def near(array):
    return pltpu.with_memory_space_constraint(array, pltpu.VMEM)


def near_out(shape, dtype=jnp.bfloat16):
    return pltpu.VMEM(shape, dtype)


def cost(flops, moved, transcendentals=0):
    return pl.CostEstimate(flops=flops, bytes_accessed=moved, transcendentals=transcendentals)


def vmem_spec():
    return pl.BlockSpec(memory_space=pltpu.VMEM)


def smem_spec():
    return pl.BlockSpec(memory_space=pltpu.SMEM)


def lanes_at(index, size):
    return pl.ds(pl.multiple_of(index * size, size), size)


def slices_kernel(where_ref, hidden, out_weight, mine, share_out, far_out, sems):
    member, core, y_hi, z_half = where_ref[0], where_ref[1], where_ref[2], where_ref[3]
    half, width, deep = mine.shape[0], share_out.shape[1], far_out.shape[0]
    copies = (
        copies_of(hidden.at[lanes_at(core, half), :], mine, sems, 4)
        + copies_of(hidden.at[:, lanes_at(member, width)], share_out, sems, 4, 4)
        + copies_of(out_weight.at[lanes_at(z_half, deep), lanes_at(1 - y_hi, 2 * width)], far_out, sems, 2, 8)
    )
    for copy in copies:
        copy.start()
    for copy in copies:
        copy.wait()


def slices(where, hidden, out_weight, members):
    rows, width = hidden.shape
    share, depth = width // members, out_weight.shape[0]
    return pl.pallas_call(
        slices_kernel,
        out_shape=(
            near_out((rows // 2, width)),
            near_out((rows, share)),
            near_out((depth // 2, 2 * share)),
        ),
        in_specs=[smem_spec(), any_spec(), any_spec()],
        out_specs=(vmem_spec(),) * 3,
        scratch_shapes=[pltpu.SemaphoreType.DMA((10,))],
        compiler_params=pltpu.CompilerParams(vmem_limit_bytes=2 * MIB),
        cost_estimate=cost(0, 4 * MIB),
    )(where, far(hidden), far(out_weight))


ROW = 512


def modulate_kernel(emb_ref, mod_ref, payload, rows_ref):
    rows_ref[...] = jnp.zeros_like(rows_ref)
    columns = mod_ref.shape[0]
    rows_ref[:, :columns] = lax.dot_general(
        emb_ref[...], mod_ref[...], (((1,), (1,)), ((), ())), preferred_element_type=jnp.float32
    )
    rows = rows_ref[...]
    slots = rows.shape[0]
    even = lax.broadcasted_iota(jnp.int32, rows.shape, 0) % 2 == 0
    following = pltpu.roll(rows, slots - 1, 0)
    partner = jnp.where(even, following, pltpu.roll(rows, 1, 0))
    joined = rows + pltpu.roll(partner, columns, 1) + pltpu.roll(following, 2 * columns, 1)
    for slot in range(slots):
        payload[slot] = joined[slot : slot + 1, :]


def modulate(emb, mod_weight):
    return pl.pallas_call(
        modulate_kernel,
        out_shape=jax.ShapeDtypeStruct((emb.shape[0], 1, ROW), jnp.float32),
        in_specs=[vmem_spec(), vmem_spec()],
        out_specs=vmem_spec(),
        scratch_shapes=[pltpu.VMEM((emb.shape[0], ROW), jnp.float32)],
        compiler_params=pltpu.CompilerParams(vmem_limit_bytes=2 * MIB),
        cost_estimate=cost(10**7, MIB),
    )(emb, mod_weight.T)


NORM_ROWS = 16


def spread(rows_ref, part, flat):
    slots = rows_ref.shape[0]
    columns = flat.shape[1] // slots
    step = columns - PAIR
    row = lax.broadcasted_iota(jnp.int32, (8, 2 * PAIR), 0)
    at = lax.broadcasted_iota(jnp.int32, (8, 2 * PAIR), 1) - step * row
    held = (at >= 0) & (at < columns)
    first_row = row[:, :PAIR] == 0
    for i in range(slots // 8):
        block = rows_ref[8 * i : 8 * i + 8, :]
        if part:
            block = pltpu.roll(block, ROW - columns * part, 1)
        turned = pltpu.roll(block, 0, 1, stride=step, stride_axis=0)
        turned = jnp.where(held, turned[:, : 2 * PAIR], 0.0)
        carried = turned[:, PAIR:]
        tiles = turned[:, :PAIR] + jnp.where(first_row, 0.0, pltpu.roll(carried, 1, 0))
        base = 8 * i * columns
        for j in range(8):
            flat[:, base + j * PAIR : base + (j + 1) * PAIR] = tiles[j : j + 1, :]
        flat[:, base + 8 * PAIR : base + 9 * PAIR] = carried[7:8, :]


def qkv_kernel(part, where_ref, rows_ref, *refs):
    if part == 0:
        (source, weight_hbm, out_weight), (held_ref, kv_ref, weight, twin_out) = refs[:3], refs[3:7]
        states_ref, flat, x_sems, w_sems = refs[7:]
        sources = [source]
    else:
        weight, *sources, held_ref, kv_ref, states_ref, flat, x_sems = refs
    even = where_ref[4] == 0
    order = where_ref[1]
    rows, width = states_ref.shape
    part_rows = rows // len(sources)
    chunks = 8 // len(sources)
    x_copies = []
    for index, source in enumerate(sources):
        start = index * part_rows if len(sources) == 1 else pl.multiple_of(
            (order if index == 0 else 1 - order) * part_rows, part_rows
        )
        x_copies += copies_of(source, states_ref.at[pl.ds(start, part_rows), :], x_sems, chunks, index * chunks)
    for copy in x_copies:
        copy.start()
    w_copies = []
    if part == 0:
        for kind in range(3):
            for piece in range(2):
                start = pl.multiple_of(2 * where_ref[4] * PAIR, PAIR) if piece == 0 else PAIR
                column = (kind if piece == 0 else 3 + kind) * PAIR
                w_copies += copies_of(
                    weight_hbm.at[kind, :, pl.ds(start, PAIR)],
                    weight.at[:, pl.ds(column, PAIR)],
                    w_sems,
                    2,
                    4 * kind + 2 * piece,
                )
        beside = where_ref[2] * 2 + 1 - where_ref[1]
        w_copies += copies_of(out_weight.at[:, lanes_at(beside, twin_out.shape[1])], twin_out, w_sems, 2, 12)
        for copy in w_copies:
            copy.start()
    spread(rows_ref, part, flat)
    scale, shift = 1.0 + flat[:, width : 2 * width], flat[:, :width]
    half = rows // 2
    low = low_lanes((half, PAIR))

    def normalise(first, count):
        for start in range(first, first + count, NORM_ROWS):
            block = pl.ds(start, NORM_ROWS)
            states = states_ref[block, :].astype(jnp.float32)
            mean = jnp.mean(states, axis=1, keepdims=True)
            centred = states - mean
            var = jnp.mean(centred * centred, axis=1, keepdims=True)
            states_ref[block, :] = (centred * lax.rsqrt(var + 1e-05) * scale + shift).astype(jnp.bfloat16)

    def project(first):
        block = pl.ds(first, half)
        out = jnp.dot(states_ref[block, :], weight[...], preferred_element_type=jnp.float32)
        q_pair, k_pair, v_pair, q_mid, k_mid, v_mid = [out[:, i * PAIR : (i + 1) * PAIR] for i in range(6)]
        turned = [pltpu.roll(a, HD, 1) for a in (q_mid, k_mid, v_mid)]
        q_one = jnp.where(even, q_mid, turned[0])
        k_one = jnp.where(even, k_mid, turned[1])
        v_one = jnp.where(even, turned[2], v_mid)
        held_ref[block, :PAIR] = (q_pair.astype(jnp.bfloat16) * HD ** (-0.5)).astype(jnp.bfloat16)
        held_ref[block, PAIR : 2 * PAIR] = (
            jnp.where(low, q_one, 0.0).astype(jnp.bfloat16) * HD ** (-0.5)
        ).astype(jnp.bfloat16)
        for index, lanes in enumerate((k_pair, v_pair, jnp.where(low, k_one, v_one))):
            kv_ref[block, index * PAIR : (index + 1) * PAIR] = lanes.astype(jnp.bfloat16)
            held_ref[block, (2 + index) * PAIR : (3 + index) * PAIR] = lanes.astype(jnp.bfloat16)

    for copy in x_copies:
        copy.wait()
    normalise(0, half)
    for copy in w_copies:
        copy.wait()
    project(0)
    normalise(half, half)
    project(half)


def qkv(part, where, mod_rows, sources, weight, out_weight=None):
    rows, width = sources[0].shape[0] * len(sources), sources[0].shape[1]
    outs = [near_out((rows, 8 * PAIR)), near_out((rows, 3 * PAIR))]
    scratch = [
        pltpu.VMEM((rows, width), jnp.bfloat16),
        pltpu.VMEM((1, 3 * width), jnp.float32),
        pltpu.SemaphoreType.DMA((8,)),
    ]
    if part == 0:
        outs += [near_out((width, 6 * PAIR)), near_out((out_weight.shape[0], width // 4))]
        scratch.append(pltpu.SemaphoreType.DMA((14,)))
        inputs = [far(a) for a in (sources[0], weight, out_weight)]
        specs = [any_spec()] * 3
    else:
        inputs = [near(weight), *sources]
        specs = [vmem_spec()] + [any_spec()] * len(sources)
    return pl.pallas_call(
        functools.partial(qkv_kernel, part),
        out_shape=tuple(outs),
        in_specs=[smem_spec(), vmem_spec()] + specs,
        out_specs=(vmem_spec(),) * len(outs),
        scratch_shapes=scratch,
        compiler_params=pltpu.CompilerParams(vmem_limit_bytes=12 * MIB),
        cost_estimate=cost(2 * rows * width * 6 * PAIR, 9 * MIB),
    )(where, mod_rows, *inputs)


def head_views(query, kv):
    low = low_lanes((query.shape[0], PAIR))
    q_pair, q_one = query[:, :PAIR], query[:, PAIR:]
    k_pair, v_pair, mid = kv
    zero = jnp.zeros_like(q_pair)
    return (
        (jnp.where(low, q_pair, zero), k_pair, v_pair),
        (jnp.where(low, zero, q_pair), k_pair, v_pair),
        (q_one, mid, mid),
    )


def scores_of(query, keys):
    return lax.dot_general(query, keys, (((1,), (1,)), ((), ())), preferred_element_type=jnp.float32)


def attend_kernel(queries, where_ref, counts_ref, own_ref, other_ref, remote_ref, piece_ref):
    span = own_ref.shape[0]
    tile = 256
    q_ref = (own_ref, other_ref)[queries]
    lane = lax.broadcasted_iota(jnp.int32, (1, span), 1)
    slot = where_ref[6]
    step = 1 - 2 * where_ref[4]

    def count(at):
        inside = (at >= 0) & (at < counts_ref.shape[0])
        return jnp.where(inside, counts_ref[jnp.where(inside, at, 0)], 0)

    counts = [count(slot), count(slot + step), count(slot - step if queries == 0 else slot + 2 * step)]
    bias = jnp.concatenate([jnp.where(lane < c * P_SIZE, 0.0, NEG) for c in counts], axis=1)
    kv = [
        jnp.concatenate(
            [
                own_ref[:, (2 + i) * PAIR : (3 + i) * PAIR],
                other_ref[:, (2 + i) * PAIR : (3 + i) * PAIR],
                remote_ref[:, i * PAIR : (i + 1) * PAIR],
            ],
            axis=0,
        )
        for i in range(3)
    ]
    low = low_lanes((tile, PAIR))
    ones = []
    for start in range(0, span, tile):
        rows = pl.ds(start, tile)
        outs = []
        for query, keys, values in head_views(q_ref[rows, : 2 * PAIR], kv):
            scores = scores_of(query, keys) + bias
            peak = jnp.max(scores, axis=1, keepdims=True)
            probs = jnp.exp(scores - peak)
            total = jnp.sum(probs, axis=1, keepdims=True)
            numer = jnp.dot(probs.astype(jnp.bfloat16), values, preferred_element_type=jnp.float32)
            outs.append(numer / total)
        piece_ref[rows, :] = jnp.where(low, outs[0], outs[1]).astype(jnp.bfloat16)
        ones.append(outs[2])
    piece_ref[span:, :] = jnp.where(low, pltpu.roll(ones[0], HD, 1), ones[1]).astype(jnp.bfloat16)


def attention(queries, where, counts, own, other, remote):
    span = own.shape[0]
    return pl.pallas_call(
        functools.partial(attend_kernel, queries),
        out_shape=near_out((span + span // 2, PAIR)),
        in_specs=[smem_spec()] * 2 + [vmem_spec()] * 3,
        out_specs=vmem_spec(),
        compiler_params=pltpu.CompilerParams(vmem_limit_bytes=16 * MIB),
        cost_estimate=cost(12 * 3 * span * span * 256, 3 * MIB, 9 * span * span),
    )(where, counts, near(own), near(other), remote)


def tail_kernel(
    where_ref, rows_ref, out_weight, w_twin, near0, near1, twin0, twin1, arrived, first, second, gathered, residual,
    gate, flat, sems,
):
    member, core, z_half, parity = where_ref[0], where_ref[1], where_ref[3], where_ref[4]
    share = gathered.shape[1]
    width = flat.shape[1] // 3
    block, half, part = out_weight.shape[0], near0.shape[0], first.shape[0]
    mine = pl.ds(pl.multiple_of(core * share, share), share)
    place = lambda base, first: pl.ds(pl.multiple_of(base + first * half, half), half)
    own = pl.ds(pl.multiple_of(member * share, share), share)
    copies = (
        copies_of(out_weight.at[:, own], gathered.at[pl.ds(0, block), :], sems, 2)
        + copies_of(w_twin, gathered.at[pl.ds(2 * block, block), :], sems, 2, 2)
        + copies_of(near0.at[:, mine], gathered.at[place(block, z_half), :], sems, 1, 4)
        + copies_of(near1.at[:, mine], gathered.at[place(block, 1 - z_half), :], sems, 1, 5)
        + copies_of(twin0.at[:, mine], gathered.at[place(3 * block, z_half), :], sems, 1, 6)
        + copies_of(twin1.at[:, mine], gathered.at[place(3 * block, 1 - z_half), :], sems, 1, 7)
    )
    for copy in copies:
        copy.start()

    @pl.when(parity == 0)
    def _():
        rows = lambda index: pl.ds(pl.multiple_of(index * part, part), part)
        held = copies_of(first.at[:, own], residual.at[rows(core), :], sems, 2, 8) + copies_of(
            second.at[:, own], residual.at[rows(1 - core), :], sems, 2, 10
        )
        for copy in held:
            copy.start()
        for copy in held:
            copy.wait()

    @pl.when(parity == 1)
    def _():
        held = copies_of(arrived, residual, sems, 4, 8)
        for copy in held:
            copy.start()
        for copy in held:
            copy.wait()

    spread(rows_ref, 2, flat)
    gate[...] = flat[:, pl.ds(pl.multiple_of(2 * width + member * share, PAIR), share)]
    for copy in copies:
        copy.wait()


def tail_inputs(where, mod_rows, out_weight, w_twin, near0, near1, twin0, twin1, arrived, first, second):
    block, share = w_twin.shape
    width = out_weight.shape[1]
    return pl.pallas_call(
        tail_kernel,
        out_shape=(near_out((4 * block, share)), near_out(arrived.shape), near_out((1, share), jnp.float32)),
        in_specs=[smem_spec(), vmem_spec()] + [any_spec()] * 9,
        out_specs=(vmem_spec(),) * 3,
        scratch_shapes=[pltpu.VMEM((1, 3 * width), jnp.float32), pltpu.SemaphoreType.DMA((12,))],
        compiler_params=pltpu.CompilerParams(vmem_limit_bytes=2 * MIB),
        cost_estimate=cost(0, 5 * MIB),
    )(where, mod_rows, far(out_weight), w_twin, near0, near1, twin0, twin1, arrived, first, second)


def heads_in_order(even, other, own, span, held=None):
    half = span // 2
    low = low_lanes((half, PAIR))
    first = jnp.where(even, (other if held is None else held)[...], own[...])
    second = jnp.where(even, own[...], other[...])
    one_f, one_s = first[span:].astype(jnp.float32), second[span:].astype(jnp.float32)
    middle = jnp.concatenate(
        [
            jnp.where(low, one_f, pltpu.roll(one_s, HD, 1)),
            jnp.where(low, pltpu.roll(one_f, HD, 1), one_s),
        ],
        axis=0,
    ).astype(jnp.bfloat16)
    return jnp.concatenate([first[:span], middle, second[:span]], axis=1)


def first_out_kernel(where_ref, p1, p2, p3, p4, held, weight, partial):
    even = where_ref[4] == 0
    span = partial.shape[0]
    block = 3 * PAIR
    attn = jnp.concatenate(
        [heads_in_order(even, p4, p1, span, held), heads_in_order(even, p3, p2, span)], axis=1
    )
    partial[...] = jnp.dot(attn, weight[: 2 * block, :], preferred_element_type=jnp.float32)


def first_out(where, pieces, weight):
    span, share = pieces[0].shape[0] * 2 // 3, weight.shape[1]
    return pl.pallas_call(
        first_out_kernel,
        out_shape=near_out((span, share), jnp.float32),
        in_specs=[smem_spec()] + [vmem_spec()] * 6,
        out_specs=vmem_spec(),
        compiler_params=pltpu.CompilerParams(vmem_limit_bytes=8 * MIB),
        cost_estimate=cost(512 * 768 * 768 * 2, 3 * MIB),
    )(where, *[near(a) for a in pieces], near(weight))


def last_out_kernel(where_ref, p1, p2, p3, p4, held, weight, partial, residual, gate, fresh, out, ready, sems):
    even = where_ref[4] == 0
    last = where_ref[5] == 1
    span = partial.shape[0]
    block = 3 * PAIR
    tiles = 4
    tile = span // tiles

    @pl.when(last)
    def _():
        for source, target in ((fresh, ready), (ready, out)):
            copies = copies_of(source, target, sems, tiles)
            for copy in copies:
                copy.start()
            for copy in copies:
                copy.wait()

    @pl.when(jnp.logical_not(last))
    def _():
        attn = jnp.concatenate(
            [heads_in_order(even, p4, p1, span, held), heads_in_order(even, p3, p2, span)], axis=1
        )
        copies = copies_of(ready, out, sems, tiles)
        for i in range(tiles):
            rows = slice(i * tile, (i + 1) * tile)
            summed = partial[rows, :] + jnp.dot(
                attn[rows], weight[2 * block :, :], preferred_element_type=jnp.float32
            )
            ready[rows, :] = (residual[rows, :].astype(jnp.float32) + gate[...] * summed).astype(jnp.bfloat16)
            copies[i].start()
        for copy in copies:
            copy.wait()


def last_out(where, pieces, weight, partial, residual, gate, fresh):
    span, share = partial.shape
    return pl.pallas_call(
        last_out_kernel,
        out_shape=jax.ShapeDtypeStruct((span, share), jnp.bfloat16),
        in_specs=[smem_spec()] + [vmem_spec()] * 9 + [any_spec()],
        out_specs=any_spec(),
        scratch_shapes=[pltpu.VMEM((span, share), jnp.bfloat16), pltpu.SemaphoreType.DMA((4,))],
        compiler_params=pltpu.CompilerParams(vmem_limit_bytes=8 * MIB),
        cost_estimate=cost(512 * 768 * 768 * 2, 5 * MIB),
    )(where, *[near(a) for a in pieces], near(weight), near(partial), near(residual), near(gate), far(fresh))


def on_device(hidden, levels, frame_counts, mod_weight, qkv_weight, out_weight, fresh):
    rows, width = hidden.shape
    slot = lax.axis_index("queue")
    queue_len = lax.axis_size("queue")
    member = lax.axis_index("heads")
    members = lax.axis_size("heads")
    share = width // members
    parity, core, y_hi = slot % 2, member % 2, member // 2
    z_half = (slot // 8) % 2
    half = rows // 2
    route = functools.partial(routed, queue_len=queue_len, members=members)
    twin = lambda a: route(a, target=lambda s, y, k: (s, y, 1 - k))

    where = jnp.stack(
        [member, core, y_hi, z_half, parity, (slot == queue_len - 1).astype(jnp.int32), slot]
    ).astype(jnp.int32)
    after = lambda a, *b: lax.optimization_barrier((a, *b))[0]
    frame_counts = frame_counts.astype(jnp.int32)

    mine, own_share, far_mine = slices(where, hidden, out_weight, members)
    other_mine = route(mine, target=lambda s, y, k: (s ^ 1, y ^ k, k))

    payload = modulate(embed_levels(levels, mod_weight.shape[0]), mod_weight)
    mod_rows = lax.all_to_all(payload, "queue", 0, 0, tiled=True)[:, 0, :]

    other_twin = twin(after(other_mine, mod_rows))
    w_far0 = route(after(far_mine, mod_rows), target=lambda s, y, k: (s ^ 1, 1 - y, k))
    residual_far = route(
        after(own_share, mod_rows), target=lambda s, y, k: (s - 1, y, k) if s % 2 == 0 else None
    )

    held_own, kv_own, weight, twin_mine = qkv(0, where, mod_rows, [hidden], qkv_weight, out_weight)
    kv_far = route(kv_own, target=lambda s, y, k: (s - 2 if s % 2 == 0 else s + 2, y, k))
    w_twin = twin(twin_mine)
    held_other, kv_other = qkv(1, where, after(mod_rows, kv_own), [other_mine, other_twin], weight)
    kv_back = route(kv_other, target=lambda s, y, k: (s + 2 if s % 2 == 0 else s - 2, y, k))
    w_far0 = after(w_far0, kv_other)
    w_far1 = route(w_far0, target=lambda s, y, k: (s ^ 8, y, k))

    attn_other = attention(1, where, frame_counts, held_own, held_other, kv_far)
    p3 = route(attn_other, target=lambda s, y, k: (s if s % 2 == 0 else s - 2, 1 - y, k))
    p4 = route(attn_other, target=lambda s, y, k: (s, y, 1 - k) if s % 2 == 0 else (s - 2, y, k))
    w_fart0 = twin(after(w_far0, attn_other))
    attn_own = attention(0, after(where, attn_other), frame_counts, held_own, held_other, kv_back)
    p1 = route(attn_own, target=lambda s, y, k: (s - 1, y, k))
    p2 = route(attn_own, target=lambda s, y, k: (s - 1, 1 - y, k))
    w_fart1 = twin(after(w_far1, attn_own))
    weight, residual, gate = tail_inputs(
        where, mod_rows, out_weight, w_twin, w_far0, w_far1, w_fart0, w_fart1, residual_far, other_mine, other_twin
    )
    p1, p2, _ = lax.optimization_barrier((p1, p2, weight))
    partial = first_out(where, [p1, p2, p3, p4, attn_other], weight)
    pieces = [twin(p1), twin(p2), twin(p3)]
    return last_out(where, pieces + [twin(p4), p4], weight, partial, residual, gate, fresh)


def solution(mesh):
    placed = (
        P("queue", None),
        P(),
        P(),
        P(None, "queue"),
        P(None, None, "heads"),
        P("heads", None),
        P(None, "heads"),
    )
    return jax.shard_map(
        on_device, mesh=mesh, in_specs=placed, out_specs=P("queue", "heads"), check_vma=False
    )
```

time: 508 us -> 102 us (0.20)
  the two profiles are of different devices: /device:TPU:111 before, /device:TPU:15 now
where the time goes in v2:
time: 102 us
  Pallas kernels  32.7 us (32%)
  starting transfers between devices  28.8 us (28%)
  blocking collectives  21.2 us (21%)
  waiting for transfers between devices  18 us (18%)
    ppermute x18, starting transfers between devices, routed(): return lax.ppermute(array, BOTH, pairs)  28.8 us
    all_to_all x1, blocking collectives, on_device(): mod_rows = lax.all_to_all(payload, 'queue', 0, 0, tiled=True)[:, 0, :]  21.2 us
    ppermute x18, waiting for transfers between devices, routed(): return lax.ppermute(array, BOTH, pairs)  18 us
    pallas_call x2, Pallas kernels, qkv(): pl.pallas_call(functools.partial(qkv_kernel, part), out_shape=tuple(outs)...  14.7 us
    pallas_call x2, Pallas kernels, attention(): pl.pallas_call(functools.partial(attend_kernel, queries), out_shape=near_...  9.43 us
    pallas_call x1, Pallas kernels, slices(): pl.pallas_call(slices_kernel, out_shape=(near_out((rows // 2, width)), ne...  2.4 us
    pallas_call x1, Pallas kernels, tail_inputs(): pl.pallas_call(tail_kernel, out_shape=(near_out((4 * block, share)), near...  2.3 us
    pallas_call x1, Pallas kernels, last_out(): pl.pallas_call(last_out_kernel, out_shape=jax.ShapeDtypeStruct((span, sha...  2.24 us
  transfers between devices with their start and end apart: 18, of which 4 were waited for; matrix products, arithmetic and copies ran while one was open for 0% of the time, Pallas kernels for 28%

profile of v2, /device:TPU:15, one launch (start us, length us, event | category | flops | bytes accessed | tf_op | source)
XLA Modules:
  0.0 101.7 jit_solution(10674704518894116004)
XLA Ops:
  0.1 2.4 %shard_map.75 = (bf16[256,3072]{1,0:T(8,128)(2,1)S(1)}, bf16[512,768]{1,0:T(8,128)(2,1)S(1)}, bf16[192,1536]{1,0:T(8,128)(2,1)S(1)}) custom-call(s32[7]{0:T(128)S(1)} %stack.35.where_ref, bf16[512,3072]{1,0:T(8,128)(2,1)} %hidden.1, bf16[384,3072]{1,0:T(8,128)(2,1)} %out_weight.3), custom_call_target="tpu_custom_call" | custom-call | bytes 4194304 | tf_op jit(solution)/shard_map/pallas_call | solution.py:101
  2.5 1.4 %collective-permute-start = (bf16[256,3072]{1,0:T(8,128)(2,1)S(1)}, bf16[256,3072]{1,0:T(8,128)(2,1)S(1)}, u32[]{:S(2)}, u32[]{:S(2)}) collective-permute-start(bf16[256,3072]{1,0:T(8,128)(2,1)S(1)} %get-tuple-element.31), channel_id=1, source_target_pairs={{0,4},{1,7},{2,6},{3,5},{4,0},{5,3},{6,2},{7,1},{8,12},{9,15},{10,... | collective-permute-start | bytes 4718600 | tf_op jit(solution)/shard_map/ppermute | solution.py:35
  4.6 21.2 %all_to_all.5 = f32[64,1,512]{2,1,0:T(1,128)S(1)} all-to-all(f32[64,1,512]{2,1,0:T(1,128)S(1)} %shard_map.73), channel_id=1, replica_groups=mesh['queue'=64,'heads'=4] {'queue'}, dimensions={0} | all-to-all | bytes 262144 | tf_op jit(solution)/shard_map/all_to_all | solution.py:515
  27.7 8.3 %shard_map.74 = (bf16[512,1024]{1,0:T(8,128)(2,1)S(1)}, bf16[512,384]{1,0:T(8,128)(2,1)S(1)}, bf16[3072,768]{1,0:T(8,128)(2,1)S(1)}, bf16[384,768]{1,0:T(8,128)(2,1)S(1)}) custom-call(s32[7]{0:T(128)S(1)} %stack.35.where_ref, f32[64,512]{1,0:T(8,128)S(1)} %bitcast.11, bf16[512,3072]{1,0:T(8,128)(2,1)} %hidden.1, bf16[3,3072,384]{2,1,0:T(8,128)(2,1)} %refs_1_.1, ...), custom_call_target="tpu_custom_call" | custom-call | flops 2415919104 | bytes 9437184 | tf_op jit(solution)/shard_map/pallas_call | solution.py:265
  36.1 4.1 %collective-permute-start.2 = (bf16[512,384]{1,0:T(8,128)(2,1)S(1)}, bf16[512,384]{1,0:T(8,128)(2,1)S(1)}, u32[]{:S(2)}, u32[]{:S(2)}) collective-permute-start(bf16[512,384]{1,0:T(8,128)(2,1)S(1)} %get-tuple-element.28), channel_id=1, source_target_pairs={{4,12},{5,13},{6,14},{7,15},{8,0},{9,1},{10,2},{11,3},{12,20},{13,... | collective-permute-start | bytes 1179656 | tf_op jit(solution)/shard_map/ppermute | solution.py:35
  40.2 6.3 %shard_map.76 = (bf16[512,1024]{1,0:T(8,128)(2,1)S(1)}, bf16[512,384]{1,0:T(8,128)(2,1)S(1)}) custom-call(s32[7]{0:T(128)S(1)} %stack.35.where_ref, f32[64,512]{1,0:T(8,128)S(1)} %bitcast.12, bf16[3072,768]{1,0:T(8,128)(2,1)S(1)} %get-tuple-element.30.refs_0_, bf16[256,3072]{1,0:T(8,128)(2,1)S(1)} %collective-permute-done.refs_1_.first, ...), custom_call_target="tpu_custom_call" | custom-call | flops 2415919104 | bytes 9437184 | tf_op jit(solution)/shard_map/pallas_call | solution.py:265
  46.6 1.9 %collective-permute-start.3 = (bf16[512,384]{1,0:T(8,128)(2,1)S(1)}, bf16[512,384]{1,0:T(8,128)(2,1)S(1)}, u32[]{:S(2)}, u32[]{:S(2)}) collective-permute-start(bf16[512,384]{1,0:T(8,128)(2,1)S(1)} %get-tuple-element.35), channel_id=1, source_target_pairs={{0,8},{1,9},{2,10},{3,11},{8,16},{9,17},{10,18},{11,19},{12,4},{13... | collective-permute-start | bytes 1179656 | tf_op jit(solution)/shard_map/ppermute | solution.py:35
  49.1 1.3 %collective-permute-start.11 = (bf16[512,768]{1,0:T(8,128)(2,1)S(1)}, bf16[512,768]{1,0:T(8,128)(2,1)S(1)}, u32[]{:S(2)}, u32[]{:S(2)}) collective-permute-start(bf16[512,768]{1,0:T(8,128)(2,1)S(1)} %get-tuple-element.43), channel_id=1, source_target_pairs={{8,4},{9,5},{10,6},{11,7},{16,12},{17,13},{18,14},{19,15},{24,20},... | collective-permute-start | bytes 2359304 | tf_op jit(solution)/shard_map/ppermute | solution.py:35
  50.4 1.2 %collective-permute-start.6 = (bf16[384,768]{1,0:T(8,128)(2,1)S(1)}, bf16[384,768]{1,0:T(8,128)(2,1)S(1)}, u32[]{:S(2)}, u32[]{:S(2)}) collective-permute-start(bf16[384,768]{1,0:T(8,128)(2,1)S(1)} %get-tuple-element.36), channel_id=1, source_target_pairs={{0,1},{1,0},{2,3},{3,2},{4,5},{5,4},{6,7},{7,6},{8,9},{9,8},{10,11... | collective-permute-start | bytes 1769480 | tf_op jit(solution)/shard_map/ppermute | solution.py:35
  51.6 4.7 %shard_map.77.held = bf16[768,128]{1,0:T(8,128)(2,1)S(1)} custom-call(s32[7]{0:T(128)S(1)} %stack.35.where_ref, s32[64]{0:T(128)S(1)} %copy-done.1, bf16[512,1024]{1,0:T(8,128)(2,1)S(1)} %get-tuple-element.27.own_ref, bf16[512,1024]{1,0:T(8,128)(2,1)S(1)} %get-tuple-element.33.other_ref, bf16[512,384]{1,0:T(8,128)(2,1)S(1)} %collective-permute-done.2.remote_ref), custom_call_target="tpu_custom_call" | custom-call | flops 2415919104 | bytes 3145728 | tf_op jit(solution)/shard_map/pallas_call | solution.py:336
  56.4 4.2 %collective-permute-done.3.remote_ref = bf16[512,384]{1,0:T(8,128)(2,1)S(1)} collective-permute-done((bf16[512,384]{1,0:T(8,128)(2,1)S(1)}, bf16[512,384]{1,0:T(8,128)(2,1)S(1)}, u32[]{:S(2)}, u32[]{:S(2)}) %collective-permute-start.3) | collective-permute-done | bytes 393248 | tf_op jit(solution)/shard_map/ppermute | solution.py:35
  60.6 4.7 %shard_map.78 = bf16[768,128]{1,0:T(8,128)(2,1)S(1)} custom-call(s32[7]{0:T(128)S(1)} %stack.35.where_ref, s32[64]{0:T(128)S(1)} %copy-done.1, bf16[512,1024]{1,0:T(8,128)(2,1)S(1)} %get-tuple-element.27.own_ref, bf16[512,1024]{1,0:T(8,128)(2,1)S(1)} %get-tuple-element.33.other_ref, bf16[512,384]{1,0:T(8,128)(2,1)S(1)} %collective-permute-done.3.remote_ref), custom_call_target="tpu_custom_call" | custom-call | flops 2415919104 | bytes 3145728 | tf_op jit(solution)/shard_map/pallas_call | solution.py:336
  65.3 2.7 %collective-permute-start.10 = (bf16[192,1536]{1,0:T(8,128)(2,1)S(1)}, bf16[192,1536]{1,0:T(8,128)(2,1)S(1)}, u32[]{:S(2)}, u32[]{:S(2)}) collective-permute-start(bf16[192,1536]{1,0:T(8,128)(2,1)S(1)} %collective-permute-done.8.near1), channel_id=1, source_target_pairs={{0,1},{1,0},{2,3},{3,2},{4,5},{5,4},{6,7},{7,6},{8,9},{9,8},{10,11... | collective-permute-start | bytes 1769480 | tf_op jit(solution)/shard_map/ppermute | solution.py:35
  68.0 1.9 %collective-permute-start.16 = (bf16[768,128]{1,0:T(8,128)(2,1)S(1)}, bf16[768,128]{1,0:T(8,128)(2,1)S(1)}, u32[]{:S(2)}, u32[]{:S(2)}) collective-permute-start(bf16[768,128]{1,0:T(8,128)(2,1)S(1)} %shard_map.77.held), channel_id=1, source_target_pairs={{0,1},{1,0},{2,3},{3,2},{8,9},{9,8},{10,11},{11,10},{12,4},{13,5},... | collective-permute-start | bytes 589832 | tf_op jit(solution)/shard_map/ppermute | solution.py:35
  69.9 1.9 %collective-permute-start.14 = (bf16[768,128]{1,0:T(8,128)(2,1)S(1)}, bf16[768,128]{1,0:T(8,128)(2,1)S(1)}, u32[]{:S(2)}, u32[]{:S(2)}) collective-permute-start(bf16[768,128]{1,0:T(8,128)(2,1)S(1)} %shard_map.77.held), channel_id=1, source_target_pairs={{0,2},{1,3},{2,0},{3,1},{8,10},{9,11},{10,8},{11,9},{12,6},{13,7},... | collective-permute-start | bytes 589832 | tf_op jit(solution)/shard_map/ppermute | solution.py:35
  71.9 9.3 %collective-permute-done.11.arrived = bf16[512,768]{1,0:T(8,128)(2,1)S(1)} collective-permute-done((bf16[512,768]{1,0:T(8,128)(2,1)S(1)}, bf16[512,768]{1,0:T(8,128)(2,1)S(1)}, u32[]{:S(2)}, u32[]{:S(2)}) %collective-permute-start.11) | collective-permute-done | bytes 786464 | tf_op jit(solution)/shard_map/ppermute | solution.py:35
  81.2 1.9 %collective-permute-start.5 = (bf16[768,128]{1,0:T(8,128)(2,1)S(1)}, bf16[768,128]{1,0:T(8,128)(2,1)S(1)}, u32[]{:S(2)}, u32[]{:S(2)}) collective-permute-start(bf16[768,128]{1,0:T(8,128)(2,1)S(1)} %shard_map.78), channel_id=1, source_target_pairs={{4,2},{5,3},{6,0},{7,1},{8,6},{9,7},{10,4},{11,5},{12,10},{13,11},... | collective-permute-start | bytes 589832 | tf_op jit(solution)/shard_map/ppermute | solution.py:35
  83.1 3.7 %collective-permute-start.4 = (bf16[768,128]{1,0:T(8,128)(2,1)S(1)}, bf16[768,128]{1,0:T(8,128)(2,1)S(1)}, u32[]{:S(2)}, u32[]{:S(2)}) collective-permute-start(bf16[768,128]{1,0:T(8,128)(2,1)S(1)} %shard_map.78), channel_id=1, source_target_pairs={{4,0},{5,1},{6,2},{7,3},{8,4},{9,5},{10,6},{11,7},{12,8},{13,9},{1... | collective-permute-start | bytes 589832 | tf_op jit(solution)/shard_map/ppermute | solution.py:35
  86.9 1.2 %collective-permute-start.17 = (bf16[768,128]{1,0:T(8,128)(2,1)S(1)}, bf16[768,128]{1,0:T(8,128)(2,1)S(1)}, u32[]{:S(2)}, u32[]{:S(2)}) collective-permute-start(bf16[768,128]{1,0:T(8,128)(2,1)S(1)} %collective-permute-done.16.p4.held), channel_id=1, source_target_pairs={{0,1},{1,0},{2,3},{3,2},{4,5},{5,4},{6,7},{7,6},{8,9},{9,8},{10,11... | collective-permute-start | bytes 589832 | tf_op jit(solution)/shard_map/ppermute | solution.py:35
  88.2 2.3 %shard_map.79 = (bf16[1536,768]{1,0:T(8,128)(2,1)S(1)}, bf16[512,768]{1,0:T(8,128)(2,1)S(1)}, f32[1,768]{1,0:T(1,128)S(1)}) custom-call(s32[7]{0:T(128)S(1)} %stack.35.where_ref, f32[64,512]{1,0:T(8,128)S(1)} %bitcast.13, bf16[384,3072]{1,0:T(8,128)(2,1)} %out_weight.3, bf16[384,768]{1,0:T(8,128)(2,1)S(1)} %collective-permute-done.6.w_twin, ...), custom_call_target="tpu_custom_call" | custom-call | bytes 5242880 | tf_op jit(solution)/shard_map/pallas_call | solution.py:396
  90.6 4.4 %collective-permute-done.4.p1 = bf16[768,128]{1,0:T(8,128)(2,1)S(1)} collective-permute-done((bf16[768,128]{1,0:T(8,128)(2,1)S(1)}, bf16[768,128]{1,0:T(8,128)(2,1)S(1)}, u32[]{:S(2)}, u32[]{:S(2)}) %collective-permute-start.4) | collective-permute-done | bytes 196640 | tf_op jit(solution)/shard_map/ppermute | solution.py:35
  95.0 2.8 %collective-permute-start.12 = (bf16[768,128]{1,0:T(8,128)(2,1)S(1)}, bf16[768,128]{1,0:T(8,128)(2,1)S(1)}, u32[]{:S(2)}, u32[]{:S(2)}) collective-permute-start(bf16[768,128]{1,0:T(8,128)(2,1)S(1)} %collective-permute-done.4.p1), channel_id=1, source_target_pairs={{0,1},{1,0},{2,3},{3,2},{4,5},{5,4},{6,7},{7,6},{8,9},{9,8},{10,11... | collective-permute-start | bytes 589832 | tf_op jit(solution)/shard_map/ppermute | solution.py:35
  97.8 1.4 %shard_map.80.partial = f32[512,768]{1,0:T(8,128)S(1)} custom-call(s32[7]{0:T(128)S(1)} %stack.35.where_ref, bf16[768,128]{1,0:T(8,128)(2,1)S(1)} %collective-permute-done.4.p1, bf16[768,128]{1,0:T(8,128)(2,1)S(1)} %collective-permute-done.5.p2, bf16[768,128]{1,0:T(8,128)(2,1)S(1)} %collective-permute-done.14.p3, ...), custom_call_target="tpu_custom_call" | custom-call | flops 603979776 | bytes 3145728 | tf_op jit(solution)/shard_map/pallas_call | solution.py:435
  99.2 2.2 %shard_map.81 = bf16[512,768]{1,0:T(8,128)(2,1)} custom-call(s32[7]{0:T(128)S(1)} %stack.35.where_ref, bf16[768,128]{1,0:T(8,128)(2,1)S(1)} %collective-permute-done.12.p1, bf16[768,128]{1,0:T(8,128)(2,1)S(1)} %collective-permute-done.13.p2, bf16[768,128]{1,0:T(8,128)(2,1)S(1)} %collective-permute-done.15.p3, ...), custom_call_target="tpu_custom_call" | custom-call | flops 603979776 | bytes 5242880 | tf_op jit(solution)/shard_map/pallas_call | solution.py:481
  (34 shorter events, 3.6 us)
Async XLA Ops:
  0.1 3.8 %copy-start.2 = (s32[64]{0:T(128)S(1)}, s32[64]{0:T(128)}, u32[]{:S(2)}) copy-start(s32[64]{0:T(128)} %param.8) | copy-start | bytes 772
  0.1 4.2 %copy-start = (bf16[512,144]{0,1:T(8,128)(2,1)S(1)}, bf16[512,144]{0,1:T(8,128)(2,1)}, u32[]{:S(2)}) copy-start(bf16[512,144]{0,1:T(8,128)(2,1)} %param.10) | copy-start | bytes 442372
  2.5 23.3 %collective-permute-start = (bf16[256,3072]{1,0:T(8,128)(2,1)S(1)}, bf16[256,3072]{1,0:T(8,128)(2,1)S(1)}, u32[]{:S(2)}, u32[]{:S(2)}) collective-permute-start(bf16[256,3072]{1,0:T(8,128)(2,1)S(1)} %get-tuple-element.31), channel_id=1, source_target_pairs={{0,4},{1,7},{2,6},{3,5},{4,0},{5,3},{6,2},{7,1},{8,12},{9,15},{10,... | collective-permute-start | bytes 4718600 | tf_op jit(solution)/shard_map/ppermute | solution.py:35
  25.8 14.4 %collective-permute-start.1 = (bf16[256,3072]{1,0:T(8,128)(2,1)S(1)}, bf16[256,3072]{1,0:T(8,128)(2,1)S(1)}, u32[]{:S(2)}, u32[]{:S(2)}) collective-permute-start(bf16[256,3072]{1,0:T(8,128)(2,1)S(1)} %collective-permute-done.refs_1_.first), channel_id=1, source_target_pairs={{0,1},{1,0},{2,3},{3,2},{4,5},{5,4},{6,7},{7,6},{8,9},{9,8},{10,11... | collective-permute-start | bytes 4718600 | tf_op jit(solution)/shard_map/ppermute | solution.py:35
  26.7 21.8 %collective-permute-start.7 = (bf16[192,1536]{1,0:T(8,128)(2,1)S(1)}, bf16[192,1536]{1,0:T(8,128)(2,1)S(1)}, u32[]{:S(2)}, u32[]{:S(2)}) collective-permute-start(bf16[192,1536]{1,0:T(8,128)(2,1)S(1)} %get-tuple-element.38), channel_id=1, source_target_pairs={{0,6},{1,7},{2,4},{3,5},{4,2},{5,3},{6,0},{7,1},{8,14},{9,15},{10,... | collective-permute-start | bytes 1769480 | tf_op jit(solution)/shard_map/ppermute | solution.py:35
  36.1 15.5 %collective-permute-start.2 = (bf16[512,384]{1,0:T(8,128)(2,1)S(1)}, bf16[512,384]{1,0:T(8,128)(2,1)S(1)}, u32[]{:S(2)}, u32[]{:S(2)}) collective-permute-start(bf16[512,384]{1,0:T(8,128)(2,1)S(1)} %get-tuple-element.28), channel_id=1, source_target_pairs={{4,12},{5,13},{6,14},{7,15},{8,0},{9,1},{10,2},{11,3},{12,20},{13,... | collective-permute-start | bytes 1179656 | tf_op jit(solution)/shard_map/ppermute | solution.py:35
  40.2 11.4 %copy-start.1 = (s32[64]{0:T(128)S(1)}, s32[64]{0:T(128)}, u32[]{:S(2)}) copy-start(s32[64]{0:T(128)} %counts_ref.3) | copy-start | bytes 772
  46.6 14.0 %collective-permute-start.3 = (bf16[512,384]{1,0:T(8,128)(2,1)S(1)}, bf16[512,384]{1,0:T(8,128)(2,1)S(1)}, u32[]{:S(2)}, u32[]{:S(2)}) collective-permute-start(bf16[512,384]{1,0:T(8,128)(2,1)S(1)} %get-tuple-element.35), channel_id=1, source_target_pairs={{0,8},{1,9},{2,10},{3,11},{8,16},{9,17},{10,18},{11,19},{12,4},{13... | collective-permute-start | bytes 1179656 | tf_op jit(solution)/shard_map/ppermute | solution.py:35
  48.5 16.8 %collective-permute-start.8 = (bf16[192,1536]{1,0:T(8,128)(2,1)S(1)}, bf16[192,1536]{1,0:T(8,128)(2,1)S(1)}, u32[]{:S(2)}, u32[]{:S(2)}) collective-permute-start(bf16[192,1536]{1,0:T(8,128)(2,1)S(1)} %collective-permute-done.7.near0), channel_id=1, source_target_pairs={{0,32},{1,33},{2,34},{3,35},{4,36},{5,37},{6,38},{7,39},{8,40},{9,... | collective-permute-start | bytes 1769480 | tf_op jit(solution)/shard_map/ppermute | solution.py:35
  49.1 32.1 %collective-permute-start.11 = (bf16[512,768]{1,0:T(8,128)(2,1)S(1)}, bf16[512,768]{1,0:T(8,128)(2,1)S(1)}, u32[]{:S(2)}, u32[]{:S(2)}) collective-permute-start(bf16[512,768]{1,0:T(8,128)(2,1)S(1)} %get-tuple-element.43), channel_id=1, source_target_pairs={{8,4},{9,5},{10,6},{11,7},{16,12},{17,13},{18,14},{19,15},{24,20},... | collective-permute-start | bytes 2359304 | tf_op jit(solution)/shard_map/ppermute | solution.py:35
  50.4 19.5 %collective-permute-start.6 = (bf16[384,768]{1,0:T(8,128)(2,1)S(1)}, bf16[384,768]{1,0:T(8,128)(2,1)S(1)}, u32[]{:S(2)}, u32[]{:S(2)}) collective-permute-start(bf16[384,768]{1,0:T(8,128)(2,1)S(1)} %get-tuple-element.36), channel_id=1, source_target_pairs={{0,1},{1,0},{2,3},{3,2},{4,5},{5,4},{6,7},{7,6},{8,9},{9,8},{10,11... | collective-permute-start | bytes 1769480 | tf_op jit(solution)/shard_map/ppermute | solution.py:35
  56.3 31.8 %collective-permute-start.9 = (bf16[192,1536]{1,0:T(8,128)(2,1)S(1)}, bf16[192,1536]{1,0:T(8,128)(2,1)S(1)}, u32[]{:S(2)}, u32[]{:S(2)}) collective-permute-start(bf16[192,1536]{1,0:T(8,128)(2,1)S(1)} %collective-permute-done.7.near0), channel_id=1, source_target_pairs={{0,1},{1,0},{2,3},{3,2},{4,5},{5,4},{6,7},{7,6},{8,9},{9,8},{10,11... | collective-permute-start | bytes 1769480 | tf_op jit(solution)/shard_map/ppermute | solution.py:35
  65.3 22.9 %collective-permute-start.10 = (bf16[192,1536]{1,0:T(8,128)(2,1)S(1)}, bf16[192,1536]{1,0:T(8,128)(2,1)S(1)}, u32[]{:S(2)}, u32[]{:S(2)}) collective-permute-start(bf16[192,1536]{1,0:T(8,128)(2,1)S(1)} %collective-permute-done.8.near1), channel_id=1, source_target_pairs={{0,1},{1,0},{2,3},{3,2},{4,5},{5,4},{6,7},{7,6},{8,9},{9,8},{10,11... | collective-permute-start | bytes 1769480 | tf_op jit(solution)/shard_map/ppermute | solution.py:35
  68.0 15.1 %collective-permute-start.16 = (bf16[768,128]{1,0:T(8,128)(2,1)S(1)}, bf16[768,128]{1,0:T(8,128)(2,1)S(1)}, u32[]{:S(2)}, u32[]{:S(2)}) collective-permute-start(bf16[768,128]{1,0:T(8,128)(2,1)S(1)} %shard_map.77.held), channel_id=1, source_target_pairs={{0,1},{1,0},{2,3},{3,2},{8,9},{9,8},{10,11},{11,10},{12,4},{13,5},... | collective-permute-start | bytes 589832 | tf_op jit(solution)/shard_map/ppermute | solution.py:35
  69.9 16.9 %collective-permute-start.14 = (bf16[768,128]{1,0:T(8,128)(2,1)S(1)}, bf16[768,128]{1,0:T(8,128)(2,1)S(1)}, u32[]{:S(2)}, u32[]{:S(2)}) collective-permute-start(bf16[768,128]{1,0:T(8,128)(2,1)S(1)} %shard_map.77.held), channel_id=1, source_target_pairs={{0,2},{1,3},{2,0},{3,1},{8,10},{9,11},{10,8},{11,9},{12,6},{13,7},... | collective-permute-start | bytes 589832 | tf_op jit(solution)/shard_map/ppermute | solution.py:35
  81.2 9.4 %collective-permute-start.5 = (bf16[768,128]{1,0:T(8,128)(2,1)S(1)}, bf16[768,128]{1,0:T(8,128)(2,1)S(1)}, u32[]{:S(2)}, u32[]{:S(2)}) collective-permute-start(bf16[768,128]{1,0:T(8,128)(2,1)S(1)} %shard_map.78), channel_id=1, source_target_pairs={{4,2},{5,3},{6,0},{7,1},{8,6},{9,7},{10,4},{11,5},{12,10},{13,11},... | collective-permute-start | bytes 589832 | tf_op jit(solution)/shard_map/ppermute | solution.py:35
  83.1 11.8 %collective-permute-start.4 = (bf16[768,128]{1,0:T(8,128)(2,1)S(1)}, bf16[768,128]{1,0:T(8,128)(2,1)S(1)}, u32[]{:S(2)}, u32[]{:S(2)}) collective-permute-start(bf16[768,128]{1,0:T(8,128)(2,1)S(1)} %shard_map.78), channel_id=1, source_target_pairs={{4,0},{5,1},{6,2},{7,3},{8,4},{9,5},{10,6},{11,7},{12,8},{13,9},{1... | collective-permute-start | bytes 589832 | tf_op jit(solution)/shard_map/ppermute | solution.py:35
  86.9 12.3 %collective-permute-start.17 = (bf16[768,128]{1,0:T(8,128)(2,1)S(1)}, bf16[768,128]{1,0:T(8,128)(2,1)S(1)}, u32[]{:S(2)}, u32[]{:S(2)}) collective-permute-start(bf16[768,128]{1,0:T(8,128)(2,1)S(1)} %collective-permute-done.16.p4.held), channel_id=1, source_target_pairs={{0,1},{1,0},{2,3},{3,2},{4,5},{5,4},{6,7},{7,6},{8,9},{9,8},{10,11... | collective-permute-start | bytes 589832 | tf_op jit(solution)/shard_map/ppermute | solution.py:35
  88.1 11.1 %collective-permute-start.15 = (bf16[768,128]{1,0:T(8,128)(2,1)S(1)}, bf16[768,128]{1,0:T(8,128)(2,1)S(1)}, u32[]{:S(2)}, u32[]{:S(2)}) collective-permute-start(bf16[768,128]{1,0:T(8,128)(2,1)S(1)} %collective-permute-done.14.p3), channel_id=1, source_target_pairs={{0,1},{1,0},{2,3},{3,2},{4,5},{5,4},{6,7},{7,6},{8,9},{9,8},{10,11... | collective-permute-start | bytes 589832 | tf_op jit(solution)/shard_map/ppermute | solution.py:35
  95.0 4.3 %collective-permute-start.12 = (bf16[768,128]{1,0:T(8,128)(2,1)S(1)}, bf16[768,128]{1,0:T(8,128)(2,1)S(1)}, u32[]{:S(2)}, u32[]{:S(2)}) collective-permute-start(bf16[768,128]{1,0:T(8,128)(2,1)S(1)} %collective-permute-done.4.p1), channel_id=1, source_target_pairs={{0,1},{1,0},{2,3},{3,2},{4,5},{5,4},{6,7},{7,6},{8,9},{9,8},{10,11... | collective-permute-start | bytes 589832 | tf_op jit(solution)/shard_map/ppermute | solution.py:35
  97.8 1.4 %collective-permute-start.13 = (bf16[768,128]{1,0:T(8,128)(2,1)S(1)}, bf16[768,128]{1,0:T(8,128)(2,1)S(1)}, u32[]{:S(2)}, u32[]{:S(2)}) collective-permute-start(bf16[768,128]{1,0:T(8,128)(2,1)S(1)} %collective-permute-done.5.p2), channel_id=1, source_target_pairs={{0,1},{1,0},{2,3},{3,2},{4,5},{5,4},{6,7},{7,6},{8,9},{9,8},{10,11... | collective-permute-start | bytes 589832 | tf_op jit(solution)/shard_map/ppermute | solution.py:35

commit v3 on v0

v3 whole, which is shorter than its diff:
```python
import functools
import math

import jax
import jax.numpy as jnp
from jax import lax
from jax.experimental import pallas as pl
from jax.experimental.pallas import tpu as pltpu
from jax.sharding import PartitionSpec as P

HD = 64
P_SIZE = 256
PAIR = 2 * HD
NEG = -1e30
BOTH = ("queue", "heads")
MIB = 1024 * 1024


def embed_levels(levels, width):
    halfway = width // 2
    freqs = jnp.exp(-math.log(10000.0) * jnp.arange(halfway, dtype=jnp.float32) / halfway)
    angles = levels.astype(jnp.float32)[:, None] * freqs[None, :]
    return jax.nn.silu(jnp.concatenate([jnp.cos(angles), jnp.sin(angles)], axis=1)).astype(
        jnp.bfloat16
    )


def routed(array, queue_len, members, target):
    pairs = []
    for slot in range(queue_len):
        for member in range(members):
            goal = target(slot, member // 2, member % 2)
            if goal is not None and 0 <= goal[0] < queue_len:
                pairs.append((slot * members + member, goal[0] * members + goal[1] * 2 + goal[2]))
    return lax.ppermute(array, BOTH, pairs)


def low_lanes(shape):
    return lax.broadcasted_iota(jnp.int32, shape, len(shape) - 1) < HD


def copies_of(source, target, sems, chunks, first=0):
    step = source.shape[0] // chunks
    return [
        pltpu.make_async_copy(
            source.at[pl.ds(i * step, step), :], target.at[pl.ds(i * step, step), :], sems.at[first + i]
        )
        for i in range(chunks)
    ]


def any_spec():
    return pl.BlockSpec(memory_space=pl.ANY)


def far(array):
    return pltpu.with_memory_space_constraint(array, pltpu.HBM)


def near(array):
    return pltpu.with_memory_space_constraint(array, pltpu.VMEM)


def near_out(shape, dtype=jnp.bfloat16):
    return pltpu.VMEM(shape, dtype)


def cost(flops, moved, transcendentals=0):
    return pl.CostEstimate(flops=flops, bytes_accessed=moved, transcendentals=transcendentals)


def vmem_spec():
    return pl.BlockSpec(memory_space=pltpu.VMEM)


def smem_spec():
    return pl.BlockSpec(memory_space=pltpu.SMEM)


def lanes_at(index, size):
    return pl.ds(pl.multiple_of(index * size, size), size)


SPLIT = 288


def slices_kernel(where_ref, hidden, out_weight, mine, share_a, share_b, far_out, sems):
    member, core, y_hi = where_ref[0], where_ref[1], where_ref[2]
    half, width = mine.shape[0], share_a.shape[1]
    copies = (
        copies_of(hidden.at[lanes_at(core, half), :], mine, sems, 4)
        + copies_of(hidden.at[pl.ds(0, SPLIT), lanes_at(member, width)], share_a, sems, 2, 4)
        + copies_of(hidden.at[pl.ds(SPLIT, 2 * half - SPLIT), lanes_at(member, width)], share_b, sems, 2, 6)
        + copies_of(out_weight.at[:, lanes_at(1 - y_hi, 2 * width)], far_out, sems, 2, 8)
    )
    for copy in copies:
        copy.start()
    for copy in copies:
        copy.wait()


def slices(where, hidden, out_weight, members):
    rows, width = hidden.shape
    share, depth = width // members, out_weight.shape[0]
    return pl.pallas_call(
        slices_kernel,
        out_shape=(
            near_out((rows // 2, width)),
            near_out((SPLIT, share)),
            near_out((rows - SPLIT, share)),
            near_out((depth, 2 * share)),
        ),
        in_specs=[smem_spec(), any_spec(), any_spec()],
        out_specs=(vmem_spec(),) * 4,
        scratch_shapes=[pltpu.SemaphoreType.DMA((10,))],
        compiler_params=pltpu.CompilerParams(vmem_limit_bytes=2 * MIB),
        cost_estimate=cost(0, 4 * MIB),
    )(where, far(hidden), far(out_weight))


ROW = 384


def modulate_kernel(where_ref, emb_ref, mod_ref, payload, rows_ref):
    rows_ref[...] = jnp.zeros_like(rows_ref)
    columns = mod_ref.shape[0]
    rows_ref[:, :columns] = lax.dot_general(
        emb_ref[...], mod_ref[...], (((1,), (1,)), ((), ())), preferred_element_type=jnp.float32
    )
    rows = rows_ref[...]
    slots = rows.shape[0]
    even = lax.broadcasted_iota(jnp.int32, rows.shape, 0) % 2 == 0
    following = pltpu.roll(rows, slots - 1, 0)
    partner = jnp.where(even, following, pltpu.roll(rows, 1, 0))
    joined = jnp.where(where_ref[1] == 0, rows, partner) + pltpu.roll(following, columns, 1)
    for slot in range(slots):
        payload[slot] = joined[slot : slot + 1, :]


def modulate(where, emb, mod_weight):
    return pl.pallas_call(
        modulate_kernel,
        out_shape=jax.ShapeDtypeStruct((emb.shape[0], 1, ROW), jnp.float32),
        in_specs=[smem_spec(), vmem_spec(), vmem_spec()],
        out_specs=vmem_spec(),
        scratch_shapes=[pltpu.VMEM((emb.shape[0], ROW), jnp.float32)],
        compiler_params=pltpu.CompilerParams(vmem_limit_bytes=2 * MIB),
        cost_estimate=cost(10**7, MIB),
    )(where, emb, mod_weight.T)


NORM_ROWS = 16


def spread(rows_ref, part, flat):
    slots = rows_ref.shape[0]
    columns = flat.shape[1] // slots
    step = columns - PAIR
    row = lax.broadcasted_iota(jnp.int32, (8, 2 * PAIR), 0)
    at = lax.broadcasted_iota(jnp.int32, (8, 2 * PAIR), 1) - step * row
    held = (at >= 0) & (at < columns)
    first_row = row[:, :PAIR] == 0
    for i in range(slots // 8):
        block = rows_ref[8 * i : 8 * i + 8, :]
        if part:
            block = pltpu.roll(block, ROW - columns * part, 1)
        turned = pltpu.roll(block, 0, 1, stride=step, stride_axis=0)
        turned = jnp.where(held, turned[:, : 2 * PAIR], 0.0)
        carried = turned[:, PAIR:]
        tiles = turned[:, :PAIR] + jnp.where(first_row, 0.0, pltpu.roll(carried, 1, 0))
        base = 8 * i * columns
        for j in range(8):
            flat[:, base + j * PAIR : base + (j + 1) * PAIR] = tiles[j : j + 1, :]
        flat[:, base + 8 * PAIR : base + 9 * PAIR] = carried[7:8, :]


def kv_kernel(
    where_ref, rows_ref, hidden, first, second, own_weight, twin_weight, out_weight, kv_ref, k_ref, v_ref, states_ref, q_weight,
    twin_out,
    flat, weight, x_sems, w_sems,
):
    core, parity = where_ref[1], where_ref[4]
    rows, width = states_ref.shape
    half = rows // 2
    each = q_weight.shape[1]
    from_own = copies_of(hidden, states_ref, x_sems, 4)
    from_pair = copies_of(first, states_ref.at[pl.ds(0, half), :], x_sems, 2) + copies_of(
        second, states_ref.at[pl.ds(half, half), :], x_sems, 2, 2
    )

    def weights_from(source):
        return [
            copies_of(source.at[kind], target, w_sems, 2, 2 * kind)
            for kind, target in (
                (1, weight.at[:, pl.ds(0, each)]),
                (2, weight.at[:, pl.ds(each, each)]),
                (0, q_weight),
            )
        ]

    def start(condition, copies):
        @pl.when(condition)
        def _():
            for copy in copies:
                copy.start()

    start(core == 0, from_own)
    start(core == 1, from_pair)
    start(core == parity, sum(weights_from(own_weight), []))
    start(core != parity, sum(weights_from(twin_weight), []))
    beside = where_ref[2] * 2 + 1 - core
    asides = copies_of(out_weight.at[:, lanes_at(beside, twin_out.shape[1])], twin_out, w_sems, 2, 6)
    for copy in asides:
        copy.start()
    spread(rows_ref, 0, flat)
    scale, shift = 1.0 + flat[:, width : 2 * width], flat[:, :width]

    def normalise(first_row):
        for start in range(first_row, first_row + half, NORM_ROWS):
            block = pl.ds(start, NORM_ROWS)
            states = states_ref[block, :].astype(jnp.float32)
            mean = jnp.mean(states, axis=1, keepdims=True)
            centred = states - mean
            var = jnp.mean(centred * centred, axis=1, keepdims=True)
            states_ref[block, :] = (centred * lax.rsqrt(var + 1e-05) * scale + shift).astype(jnp.bfloat16)

    for copy in from_own:
        copy.wait()
    normalise(0)
    normalise(half)
    keys, values, queries = weights_from(own_weight)
    for copy in keys + values:
        copy.wait()
    kv = jnp.dot(states_ref[...], weight[...], preferred_element_type=jnp.float32).astype(jnp.bfloat16)
    kv_ref[...] = kv
    k_ref[...] = kv[:, :each]
    v_ref[...] = kv[:, each:]
    for copy in queries + asides:
        copy.wait()


def keys_values(where, mod_rows, hidden, first, second, own_weight, twin_weight, out_weight):
    rows, width = hidden.shape
    each = own_weight.shape[2]
    return pl.pallas_call(
        kv_kernel,
        out_shape=(
            near_out((rows, 2 * each)),
            near_out((rows, each)),
            near_out((rows, each)),
            near_out((rows, width)),
            near_out((width, each)),
            near_out((out_weight.shape[0], width // 4)),
        ),
        in_specs=[smem_spec(), vmem_spec()] + [any_spec()] * 6,
        out_specs=(vmem_spec(),) * 6,
        scratch_shapes=[
            pltpu.VMEM((1, 3 * width), jnp.float32),
            pltpu.VMEM((width, 2 * each), jnp.bfloat16),
            pltpu.SemaphoreType.DMA((4,)),
            pltpu.SemaphoreType.DMA((8,)),
        ],
        compiler_params=pltpu.CompilerParams(vmem_limit_bytes=24 * MIB),
        cost_estimate=cost(1, 1),
    )(where, mod_rows, far(hidden), first, second, far(own_weight), twin_weight, far(out_weight))


def query_kernel(normed, weight, query_ref):
    query = jnp.dot(normed[...], weight[...], preferred_element_type=jnp.float32).astype(jnp.bfloat16)
    query_ref[...] = (query * HD ** (-0.5)).astype(jnp.bfloat16)


def queries(normed, weight):
    return pl.pallas_call(
        query_kernel,
        out_shape=near_out((normed.shape[0], weight.shape[1])),
        in_specs=[vmem_spec()] * 2,
        out_specs=vmem_spec(),
        compiler_params=pltpu.CompilerParams(vmem_limit_bytes=4 * MIB),
        cost_estimate=cost(1, 1),
    )(near(normed), near(weight))


def count_at(counts_ref, at):
    inside = (at >= 0) & (at < counts_ref.shape[0])
    return jnp.where(inside, counts_ref[jnp.where(inside, at, 0)], 0)


def bias_of(counts, span):
    lane = lax.broadcasted_iota(jnp.int32, (1, span), 1)
    return jnp.concatenate([jnp.where(lane < c * P_SIZE, 0.0, NEG) for c in counts], axis=1)


def scores_of(query, keys):
    return lax.dot_general(query, keys, (((1,), (1,)), ((), ())), preferred_element_type=jnp.float32)


def local_kernel(where_ref, counts_ref, q_ref, own_ref, k_twin, v_twin, o_ref, m_ref, l_ref):
    span = own_ref.shape[0]
    tile = 256
    core, slot = where_ref[1], where_ref[6]
    partner = slot + 1 - 2 * where_ref[4]
    counts = [
        count_at(counts_ref, jnp.where(core == 0, slot, partner)),
        count_at(counts_ref, jnp.where(core == 0, partner, slot)),
    ]
    bias = bias_of(counts, span)
    low = low_lanes((tile, PAIR))
    for index in range(3):
        lanes = slice(index * PAIR, (index + 1) * PAIR)
        values_at = slice((3 + index) * PAIR, (4 + index) * PAIR)
        keys = jnp.concatenate([own_ref[:, lanes], k_twin[:, lanes]], axis=0)
        values = jnp.concatenate([own_ref[:, values_at], v_twin[:, lanes]], axis=0)
        for start in range(0, span, tile):
            rows = pl.ds(start, tile)
            query = q_ref[rows, lanes]
            zero = jnp.zeros_like(query)
            outs = []
            for masked in (jnp.where(low, query, zero), jnp.where(low, zero, query)):
                scores = scores_of(masked, keys) + bias
                peak = jnp.max(scores, axis=1, keepdims=True)
                probs = jnp.exp(scores - peak)
                total = jnp.sum(probs, axis=1, keepdims=True)
                numer = jnp.dot(probs.astype(jnp.bfloat16), values, preferred_element_type=jnp.float32)
                outs.append((numer, peak, total))
            for ref, a, b in zip((o_ref, m_ref, l_ref), *outs):
                ref[rows, lanes] = jnp.where(low, a, b)


def local_attention(where, counts, query, own, k_twin, v_twin):
    span = query.shape[0]
    part = near_out((span, 3 * PAIR), jnp.float32)
    return pl.pallas_call(
        local_kernel,
        out_shape=(part,) * 3,
        in_specs=[smem_spec()] * 2 + [vmem_spec()] * 4,
        out_specs=(vmem_spec(),) * 3,
        compiler_params=pltpu.CompilerParams(vmem_limit_bytes=16 * MIB),
        cost_estimate=cost(8 * 6 * span * span * 256, 3 * MIB),
    )(where, counts, near(query), near(own), k_twin, v_twin)


def remote_kernel(where_ref, counts_ref, q_ref, kv_ref, o_ref, m_ref, l_ref, piece_ref):
    span = kv_ref.shape[0]
    tile = 256
    core, slot = where_ref[1], where_ref[6]
    step = 1 - 2 * where_ref[4]
    bias = bias_of([count_at(counts_ref, jnp.where(core == 0, slot - step, slot + 2 * step))], span)
    low = low_lanes((tile, PAIR))
    for index in range(3):
        lanes = slice(index * PAIR, (index + 1) * PAIR)
        keys, values = kv_ref[:, lanes], kv_ref[:, (3 + index) * PAIR : (4 + index) * PAIR]
        for start in range(0, span, tile):
            rows = pl.ds(start, tile)
            query = q_ref[rows, lanes]
            zero = jnp.zeros_like(query)
            outs = []
            for head, masked in enumerate((jnp.where(low, query, zero), jnp.where(low, zero, query))):
                at = index * PAIR + head * HD
                before = m_ref[rows, at : at + 1]
                scores = scores_of(masked, keys) + bias
                peak = jnp.maximum(jnp.max(scores, axis=1, keepdims=True), before)
                probs = jnp.exp(scores - peak)
                fade = jnp.exp(before - peak)
                total = jnp.sum(probs, axis=1, keepdims=True) + fade * l_ref[rows, at : at + 1]
                numer = jnp.dot(probs.astype(jnp.bfloat16), values, preferred_element_type=jnp.float32)
                outs.append((numer + fade * o_ref[rows, lanes]) / total)
            piece_ref[rows, lanes] = jnp.where(low, *outs).astype(jnp.bfloat16)


def remote_attention(where, counts, query, kv, o, m, l):
    span = query.shape[0]
    return pl.pallas_call(
        remote_kernel,
        out_shape=near_out((span, 3 * PAIR)),
        in_specs=[smem_spec()] * 2 + [vmem_spec()] * 5,
        out_specs=vmem_spec(),
        compiler_params=pltpu.CompilerParams(vmem_limit_bytes=16 * MIB),
        cost_estimate=cost(4 * 6 * span * span * 256, 3 * MIB),
    )(where, counts, near(query), kv, near(o), near(m), near(l))


def tail_kernel(
    where_ref, rows_ref, out_weight, w_twin, w_far, w_far_twin, gathered, gate, flat, sems,
):
    member, core, parity = where_ref[0], where_ref[1], where_ref[4]
    share = gathered.shape[1]
    width = flat.shape[1] // 3
    block = out_weight.shape[0]
    local = jnp.where(core == 0, 1 - parity, parity)
    whole, mine, own = pl.ds(0, share), lanes_at(core, share), lanes_at(member, share)
    copies = []
    for source, lanes, far_half, y_lo in (
        (out_weight, own, 0, core),
        (w_twin, whole, 0, 1 - core),
        (w_far, mine, 1, core),
        (w_far_twin, mine, 1, 1 - core),
    ):
        base = jnp.where(local == y_lo, 0, 2 * block) + far_half * block
        to = pl.ds(pl.multiple_of(base, block), block)
        copies += copies_of(source.at[:, lanes], gathered.at[to, :], sems, 2, len(copies))
    for copy in copies:
        copy.start()
    spread(rows_ref, 1, flat)
    gate[...] = flat[:, pl.ds(pl.multiple_of(2 * width + member * share, PAIR), share)]
    for copy in copies:
        copy.wait()


def tail_inputs(where, mod_rows, out_weight, w_twin, w_far, w_far_twin):
    block, share = w_twin.shape
    width = out_weight.shape[1]
    return pl.pallas_call(
        tail_kernel,
        out_shape=(near_out((4 * block, share)), near_out((1, share), jnp.float32)),
        in_specs=[smem_spec(), vmem_spec()] + [any_spec()] * 4,
        out_specs=(vmem_spec(),) * 2,
        scratch_shapes=[pltpu.VMEM((1, 3 * width), jnp.float32), pltpu.SemaphoreType.DMA((8,))],
        compiler_params=pltpu.CompilerParams(vmem_limit_bytes=2 * MIB),
        cost_estimate=cost(0, 5 * MIB),
    )(where, mod_rows, far(out_weight), w_twin, w_far, w_far_twin)


def first_out_kernel(where_ref, same, cross, held, weight, partial):
    here = (where_ref[4] == 0) & (where_ref[1] == 1)
    attn = jnp.concatenate([jnp.where(here, held[...], same[...]), cross[...]], axis=1)
    partial[...] = jnp.dot(attn, weight[: attn.shape[1], :], preferred_element_type=jnp.float32)


def first_out(where, same, cross, held, weight):
    span, share = same.shape[0], weight.shape[1]
    return pl.pallas_call(
        first_out_kernel,
        out_shape=near_out((span, share), jnp.float32),
        in_specs=[smem_spec()] + [vmem_spec()] * 4,
        out_specs=vmem_spec(),
        compiler_params=pltpu.CompilerParams(vmem_limit_bytes=8 * MIB),
        cost_estimate=cost(512 * 768 * 768 * 2, 3 * MIB),
    )(where, same, cross, near(held), near(weight))


TILE = 128


def last_out_kernel(
    where_ref, same, cross, held, weight, partial, residual_a, residual_b, gate, fresh, out, ready, sems
):
    here = (where_ref[4] == 0) & (where_ref[1] == 0)
    last = where_ref[5] == 1
    span = partial.shape[0]
    tiles = span // TILE

    @pl.when(last)
    def _():
        for source, target in ((fresh, ready), (ready, out)):
            copies = copies_of(source, target, sems, tiles)
            for copy in copies:
                copy.start()
            for copy in copies:
                copy.wait()

    @pl.when(jnp.logical_not(last))
    def _():
        copies = []
        for index, first_row in enumerate(range(0, span, TILE)):
            rows = slice(first_row, first_row + TILE)
            attn = jnp.concatenate([jnp.where(here, held[rows, :], same[rows, :]), cross[rows, :]], axis=1)
            summed = partial[rows, :] + jnp.dot(
                attn, weight[attn.shape[1] :, :], preferred_element_type=jnp.float32
            )
            if first_row + TILE <= SPLIT:
                states = residual_a[rows, :]
            elif first_row >= SPLIT:
                states = residual_b[first_row - SPLIT : first_row - SPLIT + TILE, :]
            else:
                states = jnp.concatenate(
                    [residual_a[first_row:SPLIT, :], residual_b[: first_row + TILE - SPLIT, :]], axis=0
                )
            ready[rows, :] = (states.astype(jnp.float32) + gate[...] * summed).astype(jnp.bfloat16)
            block = pl.ds(first_row, TILE)
            copies.append(pltpu.make_async_copy(ready.at[block, :], out.at[block, :], sems.at[index]))
            copies[-1].start()
        for copy in copies:
            copy.wait()


def last_out(where, same, cross, held, weight, partial, residual_a, residual_b, gate, fresh):
    span, share = partial.shape
    return pl.pallas_call(
        last_out_kernel,
        out_shape=jax.ShapeDtypeStruct((span, share), jnp.bfloat16),
        in_specs=[smem_spec()] + [vmem_spec()] * 8 + [any_spec()],
        out_specs=any_spec(),
        scratch_shapes=[pltpu.VMEM((span, share), jnp.bfloat16), pltpu.SemaphoreType.DMA((4,))],
        compiler_params=pltpu.CompilerParams(vmem_limit_bytes=8 * MIB),
        cost_estimate=cost(512 * 768 * 768 * 2, 5 * MIB),
    )(where, same, cross, held, near(weight), near(partial), residual_a, residual_b, near(gate), far(fresh))


def on_device(hidden, levels, frame_counts, mod_weight, qkv_weight, out_weight, fresh):
    rows, width = hidden.shape
    slot = lax.axis_index("queue")
    queue_len = lax.axis_size("queue")
    member = lax.axis_index("heads")
    members = lax.axis_size("heads")
    share = width // members
    parity, core, y_hi = slot % 2, member % 2, member // 2
    z_half = (slot // 8) % 2
    half = rows // 2
    route = functools.partial(routed, queue_len=queue_len, members=members)
    twin = lambda a: route(a, target=lambda s, y, k: (s, y, 1 - k))

    where = jnp.stack(
        [member, core, y_hi, z_half, parity, (slot == queue_len - 1).astype(jnp.int32), slot]
    ).astype(jnp.int32)
    after = lambda a, *b: lax.optimization_barrier((a, *b))[0]
    frame_counts = frame_counts.astype(jnp.int32)

    twin_weight = twin(qkv_weight)
    mine, share_a, share_b, far_mine = slices(where, hidden, out_weight, members)
    second = route(mine, target=lambda s, y, k: (s ^ 1, y ^ k, k))

    payload = modulate(where, embed_levels(levels, mod_weight.shape[0]), mod_weight)
    mod_rows = lax.all_to_all(payload, "queue", 0, 0, tiled=True)[:, 0, :]

    first = twin(after(second, mod_rows))
    w_far = route(after(far_mine, mod_rows), target=lambda s, y, k: (s ^ 1, 1 - y, k))
    residual_a = route(after(share_a, mod_rows), target=lambda s, y, k: (s - 1, y, k))
    kv, k, v, normed, q_weight, twin_mine = keys_values(where, mod_rows, hidden, first, second, qkv_weight, twin_weight, out_weight)

    def remote_target(s, y, k):
        back = (s % 2 == 0) == (k == 0)
        return (s - 2 if back else s + 2, y, 1 - k)

    kv_remote = route(kv, target=remote_target)
    k_twin, v_twin = twin(k), twin(v)
    query = queries(after(normed, kv), q_weight)
    w_twin = twin(twin_mine)
    o, m, l = local_attention(after(where, residual_a), frame_counts, query, kv, k_twin, v_twin)
    w_far_twin = twin(after(w_far, o))
    residual_b = route(after(share_b, o), target=lambda s, y, k: (s - 1, y, k))
    attn = remote_attention(where, frame_counts, query, kv_remote, o, m, l)

    def goal(s, y, k):
        if k == 0:
            return (s - 1, y, 0)
        return (s if s % 2 == 0 else s - 2, y, 1)

    attn = after(attn, residual_b)
    same = route(attn, target=lambda s, y, k: None if s % 2 == 0 and k == 1 else goal(s, y, k))
    cross = route(attn, target=lambda s, y, k: goal(s, 1 - y, k))
    twin_attn = twin(attn)
    weight, gate = tail_inputs(where, mod_rows, out_weight, w_twin, w_far, w_far_twin)
    same, cross, _ = lax.optimization_barrier((same, cross, weight))
    partial = first_out(where, same, cross, attn, weight)
    return last_out(where, twin(same), twin(cross), twin_attn, weight, partial, residual_a, residual_b, gate, fresh)


def solution(mesh):
    placed = (
        P("queue", None),
        P(),
        P(),
        P(None, "queue"),
        P(None, None, "heads"),
        P("heads", None),
        P(None, "heads"),
    )
    return jax.shard_map(
        on_device, mesh=mesh, in_specs=placed, out_specs=P("queue", "heads"), check_vma=False
    )
```

time: 508 us -> 97.1 us (0.19)
  waiting for transfers between devices: 426 us -> 25.5 us
  matrix products: 34.7 us -> 0 us
  Pallas kernels: 0 us -> 28.1 us
  blocking collectives: 0 us -> 17.1 us
  between operations: 14.2 us -> 0.4 us
  other arithmetic: 13.3 us -> 0.37 us
  starting transfers between devices: 12.8 us -> 25.2 us
  local copies, waits for them, and re-layouts: 5.62 us -> 0.11 us
    all_gather x1 -> x0, waiting for transfers between devices: 272 us -> none  [on_device(): lax.all_gather(mod_weight, 'queue', axis=1, tiled=True)]
    reduce_scatter x1 -> x0, waiting for transfers between devices: 117 us -> none  [on_device(): lax.psum_scatter(partial_proj, 'heads', scatter_dimension=1, tiled=True)]
    pallas_call x0 -> x9, Pallas kernels: none -> 28.1 us  [the longest x1 6.52 us: local_attention(): pl.pallas_call(local_kernel, out_shape=(part,) * 3, in_specs=[smem_spec()...]
    dot_general x4 -> x0, matrix products: 24.6 us -> none  [the longest x1 7.16 us: on_device(): jnp.einsum('rd,tde->tre', normed, qkv_weight, preferred_element_type=jnp....]
    all_to_all x0 -> x1, blocking collectives: none -> 17.1 us  [on_device(): mod_rows = lax.all_to_all(payload, 'queue', 0, 0, tiled=True)[:, 0, :]]
    ppermute x3 -> x16, starting transfers between devices: 12.7 us -> 25.2 us  [routed(): return lax.ppermute(array, BOTH, pairs)]
    ppermute x3 -> x16, waiting for transfers between devices: 36.8 us -> 25.5 us  [routed(): return lax.ppermute(array, BOTH, pairs)]
    sub x1 -> x0, matrix products: 10.1 us -> none  [block_attention(): weights = jnp.where(live[None, None, :], jnp.exp(scores - peak), 0.0)]
  transfers between devices with their start and end apart: 5 -> 16, of which waited for: 5 -> 4; matrix products, arithmetic and copies ran while one was open for 2% -> 0% of each run, Pallas kernels for 0% -> 27%
where the time goes in v3:
time: 97.1 us; the launch traced here: 96.8 us
  Pallas kernels  28.1 us (29%)
  waiting for transfers between devices  25.5 us (26%)
  starting transfers between devices  25.2 us (26%)
  blocking collectives  17.1 us (18%)
    ppermute x16, waiting for transfers between devices, routed(): return lax.ppermute(array, BOTH, pairs)  25.5 us
    ppermute x16, starting transfers between devices, routed(): return lax.ppermute(array, BOTH, pairs)  25.2 us
    all_to_all x1, blocking collectives, on_device(): mod_rows = lax.all_to_all(payload, 'queue', 0, 0, tiled=True)[:, 0, :]  17.1 us
    pallas_call x1, Pallas kernels, local_attention(): pl.pallas_call(local_kernel, out_shape=(part,) * 3, in_specs=[smem_spec()...  6.52 us
    pallas_call x1, Pallas kernels, keys_values(): pl.pallas_call(kv_kernel, out_shape=(near_out((rows, 2 * each)), near_out...  5.89 us
    pallas_call x1, Pallas kernels, remote_attention(): pl.pallas_call(remote_kernel, out_shape=near_out((span, 3 * PAIR)), in_sp...  5.32 us
    pallas_call x1, Pallas kernels, slices(): pl.pallas_call(slices_kernel, out_shape=(near_out((rows // 2, width)), ne...  2.59 us
    pallas_call x1, Pallas kernels, last_out(): pl.pallas_call(last_out_kernel, out_shape=jax.ShapeDtypeStruct((span, sha...  2.19 us
  transfers between devices with their start and end apart: 16, of which 4 were waited for; matrix products, arithmetic and copies ran while one was open for 0% of the time, Pallas kernels for 27%

profile of v3, /device:TPU:111, one launch (start us, length us, event | category | flops | bytes accessed | tf_op | source)
XLA Modules:
  0.0 96.8 jit_solution(4973428946548884388)
XLA Ops:
  0.8 2.6 %shard_map.74 = (bf16[256,3072]{1,0:T(8,128)(2,1)S(1)}, bf16[288,768]{1,0:T(8,128)(2,1)S(1)}, bf16[224,768]{1,0:T(8,128)(2,1)S(1)}, bf16[384,1536]{1,0:T(8,128)(2,1)S(1)}) custom-call(s32[7]{0:T(128)S(1)} %stack.35.where_ref, bf16[512,3072]{1,0:T(8,128)(2,1)} %hidden.3, bf16[384,3072]{1,0:T(8,128)(2,1)} %out_weight.5), custom_call_target="tpu_custom_call" | custom-call | bytes 4194304 | tf_op jit(solution)/shard_map/pallas_call | solution.py:105
  3.4 1.4 %collective-permute-start = (bf16[256,3072]{1,0:T(8,128)(2,1)S(1)}, bf16[256,3072]{1,0:T(8,128)(2,1)S(1)}, u32[]{:S(2)}, u32[]{:S(2)}) collective-permute-start(bf16[256,3072]{1,0:T(8,128)(2,1)S(1)} %get-tuple-element.30), channel_id=1, source_target_pairs={{0,4},{1,7},{2,6},{3,5},{4,0},{5,3},{6,2},{7,1},{8,12},{9,15},{10,... | collective-permute-start | bytes 4718600 | tf_op jit(solution)/shard_map/ppermute | solution.py:35
  6.0 17.1 %all_to_all.5 = f32[64,1,384]{2,1,0:T(1,128)S(1)} all-to-all(f32[64,1,384]{2,1,0:T(1,128)S(1)} %shard_map.73), channel_id=1, replica_groups=mesh['queue'=64,'heads'=4] {'queue'}, dimensions={0} | all-to-all | bytes 196608 | tf_op jit(solution)/shard_map/all_to_all | solution.py:524
  23.1 2.0 %collective-permute-start.1 = (bf16[256,3072]{1,0:T(8,128)(2,1)S(1)}, bf16[256,3072]{1,0:T(8,128)(2,1)S(1)}, u32[]{:S(2)}, u32[]{:S(2)}) collective-permute-start(bf16[256,3072]{1,0:T(8,128)(2,1)S(1)} %collective-permute-done.second), channel_id=1, source_target_pairs={{0,1},{1,0},{2,3},{3,2},{4,5},{5,4},{6,7},{7,6},{8,9},{9,8},{10,11... | collective-permute-start | bytes 4718600 | tf_op jit(solution)/shard_map/ppermute | solution.py:35
  25.1 1.3 %collective-permute-start.11 = (bf16[384,1536]{1,0:T(8,128)(2,1)S(1)}, bf16[384,1536]{1,0:T(8,128)(2,1)S(1)}, u32[]{:S(2)}, u32[]{:S(2)}) collective-permute-start(bf16[384,1536]{1,0:T(8,128)(2,1)S(1)} %get-tuple-element.49), channel_id=1, source_target_pairs={{0,6},{1,7},{2,4},{3,5},{4,2},{5,3},{6,0},{7,1},{8,14},{9,15},{10,... | collective-permute-start | bytes 3538952 | tf_op jit(solution)/shard_map/ppermute | solution.py:35
  26.4 3.5 %collective-permute-start.4 = (bf16[288,768]{1,0:T(8,128)(2,1)S(1)}, bf16[288,768]{1,0:T(8,128)(2,1)S(1)}, u32[]{:S(2)}, u32[]{:S(2)}) collective-permute-start(bf16[288,768]{1,0:T(8,128)(2,1)S(1)} %get-tuple-element.37), channel_id=1, source_target_pairs={{4,0},{5,1},{6,2},{7,3},{8,4},{9,5},{10,6},{11,7},{12,8},{13,9},{1... | collective-permute-start | bytes 1327112 | tf_op jit(solution)/shard_map/ppermute | solution.py:35
  29.9 5.9 %shard_map.75 = (bf16[512,768]{1,0:T(8,128)(2,1)S(1)}, bf16[512,384]{1,0:T(8,128)(2,1)S(1)}, bf16[512,384]{1,0:T(8,128)(2,1)S(1)}, bf16[512,3072]{1,0:T(8,128)(2...) custom-call(s32[7]{0:T(128)S(1)} %stack.35.where_ref, f32[64,384]{1,0:T(8,128)S(1)} %bitcast.11, ...), custom_call_target="tpu_custom_call" | custom-call | flops 1 | bytes 1 | tf_op jit(solution)/shard_map/pallas_call | solution.py:245
  35.8 2.2 %collective-permute-start.5 = (bf16[512,384]{1,0:T(8,128)(2,1)S(1)}, bf16[512,384]{1,0:T(8,128)(2,1)S(1)}, u32[]{:S(2)}, u32[]{:S(2)}) collective-permute-start(bf16[512,384]{1,0:T(8,128)(2,1)S(1)} %get-tuple-element.39), channel_id=1, source_target_pairs={{0,1},{1,0},{2,3},{3,2},{4,5},{5,4},{6,7},{7,6},{8,9},{9,8},{10,11... | collective-permute-start | bytes 1179656 | tf_op jit(solution)/shard_map/ppermute | solution.py:35
  38.2 5.7 %collective-permute-done.4.residual_a = bf16[288,768]{1,0:T(8,128)(2,1)S(1)} collective-permute-done((bf16[288,768]{1,0:T(8,128)(2,1)S(1)}, bf16[288,768]{1,0:T(8,128)(2,1)S(1)}, u32[]{:S(2)}, u32[]{:S(2)}) %collective-permute-start.4) | collective-permute-done | bytes 442400 | tf_op jit(solution)/shard_map/ppermute | solution.py:35
  43.9 2.1 %collective-permute-start.3 = (bf16[512,768]{1,0:T(8,128)(2,1)S(1)}, bf16[512,768]{1,0:T(8,128)(2,1)S(1)}, u32[]{:S(2)}, u32[]{:S(2)}) collective-permute-start(bf16[512,768]{1,0:T(8,128)(2,1)S(1)} %get-tuple-element.33.own_ref), channel_id=1, source_target_pairs={{1,8},{3,10},{4,13},{6,15},{8,1},{9,16},{10,3},{11,18},{12,21},{13... | collective-permute-start | bytes 2359304 | tf_op jit(solution)/shard_map/ppermute | solution.py:35
  46.0 1.8 %shard_map.76.q_ref = bf16[512,384]{1,0:T(8,128)(2,1)S(1)} custom-call(bf16[512,3072]{1,0:T(8,128)(2,1)S(1)} %get-tuple-element.34.normed, bf16[3072,384]{1,0:T(8,128)(2,1)S(1)} %get-tuple-element.35.weight), custom_call_target="tpu_custom_call" | custom-call | flops 1 | bytes 1 | tf_op jit(solution)/shard_map/pallas_call | solution.py:274
  47.8 6.5 %shard_map.77 = (f32[512,384]{1,0:T(8,128)S(1)}, f32[512,384]{1,0:T(8,128)S(1)}, f32[512,384]{1,0:T(8,128)S(1)}) custom-call(s32[7]{0:T(128)S(1)} %stack.35.where_ref, s32[64]{0:T(128)S(1)} %copy-done.1, bf16[512,384]{1,0:T(8,128)(2,1)S(1)} %shard_map.76.q_ref, bf16[512,768]{1,0:T(8,128)(2,1)S(1)} %get-tuple-element.33.own_ref, ...), custom_call_target="tpu_custom_call" | custom-call | flops 3221225472 | bytes 3145728 | tf_op jit(solution)/shard_map/pallas_call | solution.py:333
  54.4 1.3 %collective-permute-start.12 = (bf16[384,1536]{1,0:T(8,128)(2,1)S(1)}, bf16[384,1536]{1,0:T(8,128)(2,1)S(1)}, u32[]{:S(2)}, u32[]{:S(2)}) collective-permute-start(bf16[384,1536]{1,0:T(8,128)(2,1)S(1)} %collective-permute-done.11.w_far), channel_id=1, source_target_pairs={{0,1},{1,0},{2,3},{3,2},{4,5},{5,4},{6,7},{7,6},{8,9},{9,8},{10,11... | collective-permute-start | bytes 3538952 | tf_op jit(solution)/shard_map/ppermute | solution.py:35
  55.6 1.9 %collective-permute-start.7 = (bf16[224,768]{1,0:T(8,128)(2,1)S(1)}, bf16[224,768]{1,0:T(8,128)(2,1)S(1)}, u32[]{:S(2)}, u32[]{:S(2)}) collective-permute-start(bf16[224,768]{1,0:T(8,128)(2,1)S(1)} %get-tuple-element.45), channel_id=1, source_target_pairs={{4,0},{5,1},{6,2},{7,3},{8,4},{9,5},{10,6},{11,7},{12,8},{13,9},{1... | collective-permute-start | bytes 1032200 | tf_op jit(solution)/shard_map/ppermute | solution.py:35
  58.4 5.3 %shard_map.78.held = bf16[512,384]{1,0:T(8,128)(2,1)S(1)} custom-call(s32[7]{0:T(128)S(1)} %stack.35.where_ref, s32[64]{0:T(128)S(1)} %copy-done.1, bf16[512,384]{1,0:T(8,128)(2,1)S(1)} %shard_map.76.q_ref, bf16[512,768]{1,0:T(8,128)(2,1)S(1)} %collective-permute-done.3.kv_ref, f32[512,384]{1,0:T(8,128)S(1)} %get-tuple-element.41.o_ref, ...), custom_call_target="tpu_custom_call" | custom-call | flops 1610612736 | bytes 3145728 | tf_op jit(solution)/shard_map/pallas_call | solution.py:373
  63.8 7.6 %collective-permute-done.7.residual_b = bf16[224,768]{1,0:T(8,128)(2,1)S(1)} collective-permute-done((bf16[224,768]{1,0:T(8,128)(2,1)S(1)}, bf16[224,768]{1,0:T(8,128)(2,1)S(1)}, u32[]{:S(2)}, u32[]{:S(2)}) %collective-permute-start.7) | collective-permute-done | bytes 344096 | tf_op jit(solution)/shard_map/ppermute | solution.py:35
  71.4 2.1 %collective-permute-start.9 = (bf16[512,384]{1,0:T(8,128)(2,1)S(1)}, bf16[512,384]{1,0:T(8,128)(2,1)S(1)}, u32[]{:S(2)}, u32[]{:S(2)}) collective-permute-start(bf16[512,384]{1,0:T(8,128)(2,1)S(1)} %shard_map.78.held), channel_id=1, source_target_pairs={{1,3},{3,1},{4,2},{6,0},{8,6},{9,11},{10,4},{11,9},{12,10},{13,7},... | collective-permute-start | bytes 1179656 | tf_op jit(solution)/shard_map/ppermute | solution.py:35
  73.5 1.9 %collective-permute-start.8 = (bf16[512,384]{1,0:T(8,128)(2,1)S(1)}, bf16[512,384]{1,0:T(8,128)(2,1)S(1)}, u32[]{:S(2)}, u32[]{:S(2)}) collective-permute-start(bf16[512,384]{1,0:T(8,128)(2,1)S(1)} %shard_map.78.held), channel_id=1, source_target_pairs={{4,0},{6,2},{8,4},{10,6},{12,8},{13,5},{14,10},{15,7},{16,12},{18,... | collective-permute-start | bytes 1179656 | tf_op jit(solution)/shard_map/ppermute | solution.py:35
  75.5 0.9 collective-permute-start.15
  76.4 1.7 %shard_map.79 = (bf16[1536,768]{1,0:T(8,128)(2,1)S(1)}, f32[1,768]{1,0:T(1,128)S(1)}) custom-call(s32[7]{0:T(128)S(1)} %stack.35.where_ref, f32[64,384]{1,0:T(8,128)S(1)} %bitcast.12, bf16[384,3072]{1,0:T(8,128)(2,1)} %out_weight.5, bf16[384,768]{1,0:T(8,128)(2,1)S(1)} %collective-permute-done.10.w_twin, ...), custom_call_target="tpu_custom_call" | custom-call | bytes 5242880 | tf_op jit(solution)/shard_map/pallas_call | solution.py:413
  78.1 11.6 %collective-permute-done.9.cross = bf16[512,384]{1,0:T(8,128)(2,1)S(1)} collective-permute-done((bf16[512,384]{1,0:T(8,128)(2,1)S(1)}, bf16[512,384]{1,0:T(8,128)(2,1)S(1)}, u32[]{:S(2)}, u32[]{:S(2)}) %collective-permute-start.9) | collective-permute-done | bytes 393248 | tf_op jit(solution)/shard_map/ppermute | solution.py:35
  89.6 2.9 %collective-permute-start.13 = (bf16[512,384]{1,0:T(8,128)(2,1)S(1)}, bf16[512,384]{1,0:T(8,128)(2,1)S(1)}, u32[]{:S(2)}, u32[]{:S(2)}) collective-permute-start(bf16[512,384]{1,0:T(8,128)(2,1)S(1)} %collective-permute-done.8.same), channel_id=1, source_target_pairs={{0,1},{1,0},{2,3},{3,2},{4,5},{5,4},{6,7},{7,6},{8,9},{9,8},{10,11... | collective-permute-start | bytes 1179656 | tf_op jit(solution)/shard_map/ppermute | solution.py:35
  92.5 1.3 %shard_map.80.partial = f32[512,768]{1,0:T(8,128)S(1)} custom-call(s32[7]{0:T(128)S(1)} %stack.35.where_ref, bf16[512,384]{1,0:T(8,128)(2,1)S(1)} %collective-permute-done.8.same, bf16[512,384]{1,0:T(8,128)(2,1)S(1)} %collective-permute-done.9.cross, bf16[512,384]{1,0:T(8,128)(2,1)S(1)} %shard_map.78.held, bf16[1536,768]{1,0:T(8,128)(2,1)S(1)} %get-tuple-element.51.weight), custom_call_target="tpu_custom_call" | custom-call | flops 603979776 | bytes 3145728 | tf_op jit(solution)/shard_map/pallas_call | solution.py:432
  94.5 2.2 %shard_map.81 = bf16[512,768]{1,0:T(8,128)(2,1)} custom-call(s32[7]{0:T(128)S(1)} %stack.35.where_ref, bf16[512,384]{1,0:T(8,128)(2,1)S(1)} %collective-permute-done.13.same, bf16[512,384]{1,0:T(8,128)(2,1)S(1)} %collective-permute-done.14.cross, bf16[512,384]{1,0:T(8,128)(2,1)S(1)} %collective-permute-done.15.held, ...), custom_call_target="tpu_custom_call" | custom-call | flops 603979776 | bytes 5242880 | tf_op jit(solution)/shard_map/pallas_call | solution.py:489
  (30 shorter events, 3.5 us)
Async XLA Ops:
  0.0 29.9 %collective-permute-start.2 = (bf16[3,3072,384]{2,1,0:T(8,128)(2,1)}, bf16[3,3072,384]{2,1,0:T(8,128)(2,1)}, u32[]{:S(2)}, u32[]{:S(2)}) collective-permute-start(bf16[3,3072,384]{2,1,0:T(8,128)(2,1)} %own_weight.1), channel_id=1, source_target_pairs={{0,1},{1,0},{2,3},{3,2},{4,5},{5,4},{6,7},{7,6},{8,9},{9,8},{10,11... | collective-permute-start | bytes 21233672 | tf_op jit(solution)/shard_map/ppermute | solution.py:35
  0.8 4.0 %copy-start.2 = (s32[64]{0:T(128)S(1)}, s32[64]{0:T(128)}, u32[]{:S(2)}) copy-start(s32[64]{0:T(128)} %param.8) | copy-start | bytes 772
  0.8 4.4 %copy-start = (bf16[512,144]{0,1:T(8,128)(2,1)S(1)}, bf16[512,144]{0,1:T(8,128)(2,1)}, u32[]{:S(2)}) copy-start(bf16[512,144]{0,1:T(8,128)(2,1)} %param.10) | copy-start | bytes 442372
  3.4 19.7 %collective-permute-start = (bf16[256,3072]{1,0:T(8,128)(2,1)S(1)}, bf16[256,3072]{1,0:T(8,128)(2,1)S(1)}, u32[]{:S(2)}, u32[]{:S(2)}) collective-permute-start(bf16[256,3072]{1,0:T(8,128)(2,1)S(1)} %get-tuple-element.30), channel_id=1, source_target_pairs={{0,4},{1,7},{2,6},{3,5},{4,0},{5,3},{6,2},{7,1},{8,12},{9,15},{10,... | collective-permute-start | bytes 4718600 | tf_op jit(solution)/shard_map/ppermute | solution.py:35
  23.1 6.8 %collective-permute-start.1 = (bf16[256,3072]{1,0:T(8,128)(2,1)S(1)}, bf16[256,3072]{1,0:T(8,128)(2,1)S(1)}, u32[]{:S(2)}, u32[]{:S(2)}) collective-permute-start(bf16[256,3072]{1,0:T(8,128)(2,1)S(1)} %collective-permute-done.second), channel_id=1, source_target_pairs={{0,1},{1,0},{2,3},{3,2},{4,5},{5,4},{6,7},{7,6},{8,9},{9,8},{10,11... | collective-permute-start | bytes 4718600 | tf_op jit(solution)/shard_map/ppermute | solution.py:35
  25.1 29.3 %collective-permute-start.11 = (bf16[384,1536]{1,0:T(8,128)(2,1)S(1)}, bf16[384,1536]{1,0:T(8,128)(2,1)S(1)}, u32[]{:S(2)}, u32[]{:S(2)}) collective-permute-start(bf16[384,1536]{1,0:T(8,128)(2,1)S(1)} %get-tuple-element.49), channel_id=1, source_target_pairs={{0,6},{1,7},{2,4},{3,5},{4,2},{5,3},{6,0},{7,1},{8,14},{9,15},{10,... | collective-permute-start | bytes 3538952 | tf_op jit(solution)/shard_map/ppermute | solution.py:35
  26.4 17.5 %collective-permute-start.4 = (bf16[288,768]{1,0:T(8,128)(2,1)S(1)}, bf16[288,768]{1,0:T(8,128)(2,1)S(1)}, u32[]{:S(2)}, u32[]{:S(2)}) collective-permute-start(bf16[288,768]{1,0:T(8,128)(2,1)S(1)} %get-tuple-element.37), channel_id=1, source_target_pairs={{4,0},{5,1},{6,2},{7,3},{8,4},{9,5},{10,6},{11,7},{12,8},{13,9},{1... | collective-permute-start | bytes 1327112 | tf_op jit(solution)/shard_map/ppermute | solution.py:35
  35.8 12.0 %collective-permute-start.5 = (bf16[512,384]{1,0:T(8,128)(2,1)S(1)}, bf16[512,384]{1,0:T(8,128)(2,1)S(1)}, u32[]{:S(2)}, u32[]{:S(2)}) collective-permute-start(bf16[512,384]{1,0:T(8,128)(2,1)S(1)} %get-tuple-element.39), channel_id=1, source_target_pairs={{0,1},{1,0},{2,3},{3,2},{4,5},{5,4},{6,7},{7,6},{8,9},{9,8},{10,11... | collective-permute-start | bytes 1179656 | tf_op jit(solution)/shard_map/ppermute | solution.py:35
  38.1 9.7 %collective-permute-start.6 = (bf16[512,384]{1,0:T(8,128)(2,1)S(1)}, bf16[512,384]{1,0:T(8,128)(2,1)S(1)}, u32[]{:S(2)}, u32[]{:S(2)}) collective-permute-start(bf16[512,384]{1,0:T(8,128)(2,1)S(1)} %get-tuple-element.40), channel_id=1, source_target_pairs={{0,1},{1,0},{2,3},{3,2},{4,5},{5,4},{6,7},{7,6},{8,9},{9,8},{10,11... | collective-permute-start | bytes 1179656 | tf_op jit(solution)/shard_map/ppermute | solution.py:35
  43.9 14.5 %collective-permute-start.3 = (bf16[512,768]{1,0:T(8,128)(2,1)S(1)}, bf16[512,768]{1,0:T(8,128)(2,1)S(1)}, u32[]{:S(2)}, u32[]{:S(2)}) collective-permute-start(bf16[512,768]{1,0:T(8,128)(2,1)S(1)} %get-tuple-element.33.own_ref), channel_id=1, source_target_pairs={{1,8},{3,10},{4,13},{6,15},{8,1},{9,16},{10,3},{11,18},{12,21},{13... | collective-permute-start | bytes 2359304 | tf_op jit(solution)/shard_map/ppermute | solution.py:35
  46.0 1.8 %copy-start.1 = (s32[64]{0:T(128)S(1)}, s32[64]{0:T(128)}, u32[]{:S(2)}) copy-start(s32[64]{0:T(128)} %counts_ref.3) | copy-start | bytes 772
  54.4 22.0 %collective-permute-start.12 = (bf16[384,1536]{1,0:T(8,128)(2,1)S(1)}, bf16[384,1536]{1,0:T(8,128)(2,1)S(1)}, u32[]{:S(2)}, u32[]{:S(2)}) collective-permute-start(bf16[384,1536]{1,0:T(8,128)(2,1)S(1)} %collective-permute-done.11.w_far), channel_id=1, source_target_pairs={{0,1},{1,0},{2,3},{3,2},{4,5},{5,4},{6,7},{7,6},{8,9},{9,8},{10,11... | collective-permute-start | bytes 3538952 | tf_op jit(solution)/shard_map/ppermute | solution.py:35
  55.6 15.8 %collective-permute-start.7 = (bf16[224,768]{1,0:T(8,128)(2,1)S(1)}, bf16[224,768]{1,0:T(8,128)(2,1)S(1)}, u32[]{:S(2)}, u32[]{:S(2)}) collective-permute-start(bf16[224,768]{1,0:T(8,128)(2,1)S(1)} %get-tuple-element.45), channel_id=1, source_target_pairs={{4,0},{5,1},{6,2},{7,3},{8,4},{9,5},{10,6},{11,7},{12,8},{13,9},{1... | collective-permute-start | bytes 1032200 | tf_op jit(solution)/shard_map/ppermute | solution.py:35
  57.6 18.8 %collective-permute-start.10 = (bf16[384,768]{1,0:T(8,128)(2,1)S(1)}, bf16[384,768]{1,0:T(8,128)(2,1)S(1)}, u32[]{:S(2)}, u32[]{:S(2)}) collective-permute-start(bf16[384,768]{1,0:T(8,128)(2,1)S(1)} %get-tuple-element.47), channel_id=1, source_target_pairs={{0,1},{1,0},{2,3},{3,2},{4,5},{5,4},{6,7},{7,6},{8,9},{9,8},{10,11... | collective-permute-start | bytes 1769480 | tf_op jit(solution)/shard_map/ppermute | solution.py:35
  71.4 18.2 %collective-permute-start.9 = (bf16[512,384]{1,0:T(8,128)(2,1)S(1)}, bf16[512,384]{1,0:T(8,128)(2,1)S(1)}, u32[]{:S(2)}, u32[]{:S(2)}) collective-permute-start(bf16[512,384]{1,0:T(8,128)(2,1)S(1)} %shard_map.78.held), channel_id=1, source_target_pairs={{1,3},{3,1},{4,2},{6,0},{8,6},{9,11},{10,4},{11,9},{12,10},{13,7},... | collective-permute-start | bytes 1179656 | tf_op jit(solution)/shard_map/ppermute | solution.py:35
  73.5 16.1 %collective-permute-start.8 = (bf16[512,384]{1,0:T(8,128)(2,1)S(1)}, bf16[512,384]{1,0:T(8,128)(2,1)S(1)}, u32[]{:S(2)}, u32[]{:S(2)}) collective-permute-start(bf16[512,384]{1,0:T(8,128)(2,1)S(1)} %shard_map.78.held), channel_id=1, source_target_pairs={{4,0},{6,2},{8,4},{10,6},{12,8},{13,5},{14,10},{15,7},{16,12},{18,... | collective-permute-start | bytes 1179656 | tf_op jit(solution)/shard_map/ppermute | solution.py:35
  75.5 18.4 %collective-permute-start.15 = (bf16[512,384]{1,0:T(8,128)(2,1)S(1)}, bf16[512,384]{1,0:T(8,128)(2,1)S(1)}, u32[]{:S(2)}, u32[]{:S(2)}) collective-permute-start(bf16[512,384]{1,0:T(8,128)(2,1)S(1)} %shard_map.78.held), channel_id=1, source_target_pairs={{0,1},{1,0},{2,3},{3,2},{4,5},{5,4},{6,7},{7,6},{8,9},{9,8},{10,11... | collective-permute-start | bytes 1179656 | tf_op jit(solution)/shard_map/ppermute | solution.py:35
  89.6 4.3 %collective-permute-start.13 = (bf16[512,384]{1,0:T(8,128)(2,1)S(1)}, bf16[512,384]{1,0:T(8,128)(2,1)S(1)}, u32[]{:S(2)}, u32[]{:S(2)}) collective-permute-start(bf16[512,384]{1,0:T(8,128)(2,1)S(1)} %collective-permute-done.8.same), channel_id=1, source_target_pairs={{0,1},{1,0},{2,3},{3,2},{4,5},{5,4},{6,7},{7,6},{8,9},{9,8},{10,11... | collective-permute-start | bytes 1179656 | tf_op jit(solution)/shard_map/ppermute | solution.py:35
  92.5 1.9 %collective-permute-start.14 = (bf16[512,384]{1,0:T(8,128)(2,1)S(1)}, bf16[512,384]{1,0:T(8,128)(2,1)S(1)}, u32[]{:S(2)}, u32[]{:S(2)}) collective-permute-start(bf16[512,384]{1,0:T(8,128)(2,1)S(1)} %collective-permute-done.9.cross), channel_id=1, source_target_pairs={{0,1},{1,0},{2,3},{3,2},{4,5},{5,4},{6,7},{7,6},{8,9},{9,8},{10,11... | collective-permute-start | bytes 1179656 | tf_op jit(solution)/shard_map/ppermute | solution.py:35

commit v4 on v3

--- a/solution.py
+++ b/solution.py
@@ -81,17 +81,14 @@
     return pl.ds(pl.multiple_of(index * size, size), size)
 
 
-SPLIT = 288
-
-
-def slices_kernel(where_ref, hidden, out_weight, mine, share_a, share_b, far_out, sems):
-    member, core, y_hi = where_ref[0], where_ref[1], where_ref[2]
-    half, width = mine.shape[0], share_a.shape[1]
+def slices_kernel(where_ref, hidden, out_weight, mine, far_same, far_cross, sems):
+    core, y_hi = where_ref[1], where_ref[2]
+    half, width = mine.shape[0], far_same.shape[1]
+    away = (1 - y_hi) * 2
     copies = (
         copies_of(hidden.at[lanes_at(core, half), :], mine, sems, 4)
-        + copies_of(hidden.at[pl.ds(0, SPLIT), lanes_at(member, width)], share_a, sems, 2, 4)
-        + copies_of(hidden.at[pl.ds(SPLIT, 2 * half - SPLIT), lanes_at(member, width)], share_b, sems, 2, 6)
-        + copies_of(out_weight.at[:, lanes_at(1 - y_hi, 2 * width)], far_out, sems, 2, 8)
+        + copies_of(out_weight.at[:, lanes_at(away + core, width)], far_same, sems, 2, 4)
+        + copies_of(out_weight.at[:, lanes_at(away + 1 - core, width)], far_cross, sems, 2, 6)
     )
     for copy in copies:
         copy.start()
@@ -106,13 +103,12 @@
         slices_kernel,
         out_shape=(
             near_out((rows // 2, width)),
-            near_out((SPLIT, share)),
-            near_out((rows - SPLIT, share)),
-            near_out((depth, 2 * share)),
+            near_out((depth, share)),
+            near_out((depth, share)),
         ),
         in_specs=[smem_spec(), any_spec(), any_spec()],
-        out_specs=(vmem_spec(),) * 4,
-        scratch_shapes=[pltpu.SemaphoreType.DMA((10,))],
+        out_specs=(vmem_spec(),) * 3,
+        scratch_shapes=[pltpu.SemaphoreType.DMA((8,))],
         compiler_params=pltpu.CompilerParams(vmem_limit_bytes=2 * MIB),
         cost_estimate=cost(0, 4 * MIB),
     )(where, far(hidden), far(out_weight))
@@ -176,7 +172,7 @@
 
 def kv_kernel(
     where_ref, rows_ref, hidden, first, second, own_weight, twin_weight, out_weight, kv_ref, k_ref, v_ref, states_ref, q_weight,
-    twin_out,
+    twin_out, share_ref,
     flat, weight, x_sems, w_sems,
 ):
     core, parity = where_ref[1], where_ref[4]
@@ -226,6 +222,7 @@
 
     for copy in from_own:
         copy.wait()
+    share_ref[...] = states_ref[:, lanes_at(where_ref[0], share_ref.shape[1])]
     normalise(0)
     normalise(half)
     keys, values, queries = weights_from(own_weight)
@@ -251,9 +248,10 @@
             near_out((rows, width)),
             near_out((width, each)),
             near_out((out_weight.shape[0], width // 4)),
+            near_out((rows, width // 4)),
         ),
         in_specs=[smem_spec(), vmem_spec()] + [any_spec()] * 6,
-        out_specs=(vmem_spec(),) * 6,
+        out_specs=(vmem_spec(),) * 7,
         scratch_shapes=[
             pltpu.VMEM((1, 3 * width), jnp.float32),
             pltpu.VMEM((width, 2 * each), jnp.bfloat16),
@@ -376,7 +374,7 @@
         in_specs=[smem_spec()] * 2 + [vmem_spec()] * 5,
         out_specs=vmem_spec(),
         compiler_params=pltpu.CompilerParams(vmem_limit_bytes=16 * MIB),
-        cost_estimate=cost(4 * 6 * span * span * 256, 3 * MIB),
+        cost_estimate=cost(1, 1),
     )(where, counts, near(query), kv, near(o), near(m), near(l))
 
 
@@ -388,13 +386,13 @@
     width = flat.shape[1] // 3
     block = out_weight.shape[0]
     local = jnp.where(core == 0, 1 - parity, parity)
-    whole, mine, own = pl.ds(0, share), lanes_at(core, share), lanes_at(member, share)
+    whole, own = pl.ds(0, share), lanes_at(member, share)
     copies = []
     for source, lanes, far_half, y_lo in (
         (out_weight, own, 0, core),
         (w_twin, whole, 0, 1 - core),
-        (w_far, mine, 1, core),
-        (w_far_twin, mine, 1, 1 - core),
+        (w_far, whole, 1, core),
+        (w_far_twin, whole, 1, 1 - core),
     ):
         base = jnp.where(local == y_lo, 0, 2 * block) + far_half * block
         to = pl.ds(pl.multiple_of(base, block), block)
@@ -417,7 +415,7 @@
         out_specs=(vmem_spec(),) * 2,
         scratch_shapes=[pltpu.VMEM((1, 3 * width), jnp.float32), pltpu.SemaphoreType.DMA((8,))],
         compiler_params=pltpu.CompilerParams(vmem_limit_bytes=2 * MIB),
-        cost_estimate=cost(0, 5 * MIB),
+        cost_estimate=cost(1, 1),
     )(where, mod_rows, far(out_weight), w_twin, w_far, w_far_twin)
 
 
@@ -435,7 +433,7 @@
         in_specs=[smem_spec()] + [vmem_spec()] * 4,
         out_specs=vmem_spec(),
         compiler_params=pltpu.CompilerParams(vmem_limit_bytes=8 * MIB),
-        cost_estimate=cost(512 * 768 * 768 * 2, 3 * MIB),
+        cost_estimate=cost(1, 1),
     )(where, same, cross, near(held), near(weight))
 
 
@@ -443,9 +441,10 @@
 
 
 def last_out_kernel(
-    where_ref, same, cross, held, weight, partial, residual_a, residual_b, gate, fresh, out, ready, sems
+    where_ref, same, cross, held, weight, partial, kept, residual, gate, fresh, out, ready, sems
 ):
     here = (where_ref[4] == 0) & (where_ref[1] == 0)
+    holds = (where_ref[4] == 0) & (where_ref[1] == 1)
     last = where_ref[5] == 1
     span = partial.shape[0]
     tiles = span // TILE
@@ -468,14 +467,7 @@
             summed = partial[rows, :] + jnp.dot(
                 attn, weight[attn.shape[1] :, :], preferred_element_type=jnp.float32
             )
-            if first_row + TILE <= SPLIT:
-                states = residual_a[rows, :]
-            elif first_row >= SPLIT:
-                states = residual_b[first_row - SPLIT : first_row - SPLIT + TILE, :]
-            else:
-                states = jnp.concatenate(
-                    [residual_a[first_row:SPLIT, :], residual_b[: first_row + TILE - SPLIT, :]], axis=0
-                )
+            states = jnp.where(holds, kept[rows, :], residual[rows, :])
             ready[rows, :] = (states.astype(jnp.float32) + gate[...] * summed).astype(jnp.bfloat16)
             block = pl.ds(first_row, TILE)
             copies.append(pltpu.make_async_copy(ready.at[block, :], out.at[block, :], sems.at[index]))
@@ -484,7 +476,7 @@
             copy.wait()
 
 
-def last_out(where, same, cross, held, weight, partial, residual_a, residual_b, gate, fresh):
+def last_out(where, same, cross, held, weight, partial, kept, residual, gate, fresh):
     span, share = partial.shape
     return pl.pallas_call(
         last_out_kernel,
@@ -493,8 +485,8 @@
         out_specs=any_spec(),
         scratch_shapes=[pltpu.VMEM((span, share), jnp.bfloat16), pltpu.SemaphoreType.DMA((4,))],
         compiler_params=pltpu.CompilerParams(vmem_limit_bytes=8 * MIB),
-        cost_estimate=cost(512 * 768 * 768 * 2, 5 * MIB),
-    )(where, same, cross, held, near(weight), near(partial), residual_a, residual_b, near(gate), far(fresh))
+        cost_estimate=cost(1, 1),
+    )(where, same, cross, held, near(weight), near(partial), near(kept), residual, near(gate), far(fresh))
 
 
 def on_device(hidden, levels, frame_counts, mod_weight, qkv_weight, out_weight, fresh):
@@ -517,16 +509,16 @@
     frame_counts = frame_counts.astype(jnp.int32)
 
     twin_weight = twin(qkv_weight)
-    mine, share_a, share_b, far_mine = slices(where, hidden, out_weight, members)
+    mine, far_same, far_cross = slices(where, hidden, out_weight, members)
     second = route(mine, target=lambda s, y, k: (s ^ 1, y ^ k, k))
 
     payload = modulate(where, embed_levels(levels, mod_weight.shape[0]), mod_weight)
     mod_rows = lax.all_to_all(payload, "queue", 0, 0, tiled=True)[:, 0, :]
 
     first = twin(after(second, mod_rows))
-    w_far = route(after(far_mine, mod_rows), target=lambda s, y, k: (s ^ 1, 1 - y, k))
-    residual_a = route(after(share_a, mod_rows), target=lambda s, y, k: (s - 1, y, k))
-    kv, k, v, normed, q_weight, twin_mine = keys_values(where, mod_rows, hidden, first, second, qkv_weight, twin_weight, out_weight)
+    w_far = route(after(far_same, mod_rows), target=lambda s, y, k: (s ^ 1, 1 - y, k))
+    w_far_twin = route(after(far_cross, mod_rows), target=lambda s, y, k: (s ^ 1, 1 - y, 1 - k))
+    kv, k, v, normed, q_weight, twin_mine, share_states = keys_values(where, mod_rows, hidden, first, second, qkv_weight, twin_weight, out_weight)
 
     def remote_target(s, y, k):
         back = (s % 2 == 0) == (k == 0)
@@ -536,24 +528,25 @@
     k_twin, v_twin = twin(k), twin(v)
     query = queries(after(normed, kv), q_weight)
     w_twin = twin(twin_mine)
-    o, m, l = local_attention(after(where, residual_a), frame_counts, query, kv, k_twin, v_twin)
-    w_far_twin = twin(after(w_far, o))
-    residual_b = route(after(share_b, o), target=lambda s, y, k: (s - 1, y, k))
-    attn = remote_attention(where, frame_counts, query, kv_remote, o, m, l)
+    o, m, l = local_attention(after(where, w_far_twin), frame_counts, query, kv, k_twin, v_twin)
+    residual = route(
+        after(share_states, o),
+        target=lambda s, y, k: (s - 1, y, 0) if k == 0 else ((s - 2, y, 1) if s % 2 else None),
+    )
+    attn = remote_attention(after(where, w_far), frame_counts, query, kv_remote, o, m, l)
 
     def goal(s, y, k):
         if k == 0:
             return (s - 1, y, 0)
         return (s if s % 2 == 0 else s - 2, y, 1)
 
-    attn = after(attn, residual_b)
     same = route(attn, target=lambda s, y, k: None if s % 2 == 0 and k == 1 else goal(s, y, k))
     cross = route(attn, target=lambda s, y, k: goal(s, 1 - y, k))
     twin_attn = twin(attn)
     weight, gate = tail_inputs(where, mod_rows, out_weight, w_twin, w_far, w_far_twin)
-    same, cross, _ = lax.optimization_barrier((same, cross, weight))
+    same, cross, residual, _ = lax.optimization_barrier((same, cross, residual, weight))
     partial = first_out(where, same, cross, attn, weight)
-    return last_out(where, twin(same), twin(cross), twin_attn, weight, partial, residual_a, residual_b, gate, fresh)
+    return last_out(where, twin(same), twin(cross), twin_attn, weight, partial, share_states, residual, gate, fresh)
 
 
 def solution(mesh):

time: 97.1 us -> 88.3 us (0.909); the launches traced: 96.8 us -> 86.7 us
  waiting for transfers between devices: 25.5 us -> 11.9 us
  starting transfers between devices: 25.2 us -> 28.9 us
    ppermute x16 -> x15, waiting for transfers between devices: 25.5 us -> 11.9 us  [routed(): return lax.ppermute(array, BOTH, pairs)]
    ppermute x16 -> x15, starting transfers between devices: 25.2 us -> 28.9 us  [routed(): return lax.ppermute(array, BOTH, pairs)]
  transfers between devices with their start and end apart: 16 -> 15, of which waited for: 4 -> 4; matrix products, arithmetic and copies ran while one was open for 0% -> 1% of each run, Pallas kernels for 27% -> 30%
where the time goes in v4:
time: 88.3 us; the launch traced here: 86.7 us
  starting transfers between devices  28.9 us (33%)
  Pallas kernels  27.9 us (32%)
  blocking collectives  17.1 us (19%)
  waiting for transfers between devices  11.9 us (13%)
    ppermute x15, starting transfers between devices, routed(): return lax.ppermute(array, BOTH, pairs)  28.9 us
    all_to_all x1, blocking collectives, on_device(): mod_rows = lax.all_to_all(payload, 'queue', 0, 0, tiled=True)[:, 0, :]  17.1 us
    ppermute x15, waiting for transfers between devices, routed(): return lax.ppermute(array, BOTH, pairs)  11.9 us
    pallas_call x1, Pallas kernels, local_attention(): pl.pallas_call(local_kernel, out_shape=(part,) * 3, in_specs=[smem_spec()...  6.51 us
    pallas_call x1, Pallas kernels, keys_values(): pl.pallas_call(kv_kernel, out_shape=(near_out((rows, 2 * each)), near_out...  5.95 us
    pallas_call x1, Pallas kernels, remote_attention(): pl.pallas_call(remote_kernel, out_shape=near_out((span, 3 * PAIR)), in_sp...  5.28 us
    pallas_call x1, Pallas kernels, slices(): pl.pallas_call(slices_kernel, out_shape=(near_out((rows // 2, width)), ne...  2.32 us
    pallas_call x1, Pallas kernels, last_out(): pl.pallas_call(last_out_kernel, out_shape=jax.ShapeDtypeStruct((span, sha...  2.21 us
  transfers between devices with their start and end apart: 15, of which 4 were waited for; matrix products, arithmetic and copies ran while one was open for 1% of the time, Pallas kernels for 30%

profile of v4, /device:TPU:111, one launch (start us, length us, event | category | flops | bytes accessed | tf_op | source)
XLA Modules:
  0.0 86.7 jit_solution(7408920946939869285)
XLA Ops:
  0.8 2.3 %shard_map.73 = (bf16[256,3072]{1,0:T(8,128)(2,1)S(1)}, bf16[384,768]{1,0:T(8,128)(2,1)S(1)}, bf16[384,768]{1,0:T(8,128)(2,1)S(1)}) custom-call(s32[7]{0:T(128)S(1)} %stack.35.where_ref, bf16[512,3072]{1,0:T(8,128)(2,1)} %hidden.3, bf16[384,3072]{1,0:T(8,128)(2,1)} %out_weight.5), custom_call_target="tpu_custom_call" | custom-call | bytes 4194304 | tf_op jit(solution)/shard_map/pallas_call | solution.py:102
  3.1 1.4 %collective-permute-start.1 = (bf16[256,3072]{1,0:T(8,128)(2,1)S(1)}, bf16[256,3072]{1,0:T(8,128)(2,1)S(1)}, u32[]{:S(2)}, u32[]{:S(2)}) collective-permute-start(bf16[256,3072]{1,0:T(8,128)(2,1)S(1)} %get-tuple-element.33), channel_id=1, source_target_pairs={{0,4},{1,7},{2,6},{3,5},{4,0},{5,3},{6,2},{7,1},{8,12},{9,15},{10,... | collective-permute-start | bytes 4718600 | tf_op jit(solution)/shard_map/ppermute | solution.py:35
  4.9 0.8 shard_map.74
  5.7 17.1 %all_to_all.5 = f32[64,1,384]{2,1,0:T(1,128)S(1)} all-to-all(f32[64,1,384]{2,1,0:T(1,128)S(1)} %shard_map.74), channel_id=1, replica_groups=mesh['queue'=64,'heads'=4] {'queue'}, dimensions={0} | all-to-all | bytes 196608 | tf_op jit(solution)/shard_map/all_to_all | solution.py:516
  22.8 2.0 %collective-permute-start.2 = (bf16[256,3072]{1,0:T(8,128)(2,1)S(1)}, bf16[256,3072]{1,0:T(8,128)(2,1)S(1)}, u32[]{:S(2)}, u32[]{:S(2)}) collective-permute-start(bf16[256,3072]{1,0:T(8,128)(2,1)S(1)} %collective-permute-done.1.second), channel_id=1, source_target_pairs={{0,1},{1,0},{2,3},{3,2},{4,5},{5,4},{6,7},{7,6},{8,9},{9,8},{10,11... | collective-permute-start | bytes 4718600 | tf_op jit(solution)/shard_map/ppermute | solution.py:35
  24.8 1.3 %collective-permute-start.5 = (bf16[384,768]{1,0:T(8,128)(2,1)S(1)}, bf16[384,768]{1,0:T(8,128)(2,1)S(1)}, u32[]{:S(2)}, u32[]{:S(2)}) collective-permute-start(bf16[384,768]{1,0:T(8,128)(2,1)S(1)} %get-tuple-element.40), channel_id=1, source_target_pairs={{0,7},{1,6},{2,5},{3,4},{4,3},{5,2},{6,1},{7,0},{8,15},{9,14},{10,... | collective-permute-start | bytes 1769480 | tf_op jit(solution)/shard_map/ppermute | solution.py:35
  26.1 1.8 %collective-permute-done.2.first = bf16[256,3072]{1,0:T(8,128)(2,1)S(1)} collective-permute-done((bf16[256,3072]{1,0:T(8,128)(2,1)S(1)}, bf16[256,3072]{1,0:T(8,128)(2,1)S(1)}, u32[]{:S(2)}, u32[]{:S(2)}) %collective-permute-start.2) | collective-permute-done | bytes 1572896 | tf_op jit(solution)/shard_map/ppermute | solution.py:35
  27.8 6.0 %shard_map.75 = (bf16[512,768]{1,0:T(8,128)(2,1)S(1)}, bf16[512,384]{1,0:T(8,128)(2,1)S(1)}, bf16[512,384]{1,0:T(8,128)(2,1)S(1)}, bf16[512,3072]{1,0:T(8,128)(2...) custom-call(s32[7]{0:T(128)S(1)} %stack.35.where_ref, ...), custom_call_target="tpu_custom_call" | custom-call | flops 1 | bytes 1 | tf_op jit(solution)/shard_map/pallas_call | solution.py:242
  33.8 2.0 %collective-permute-start.6 = (bf16[512,384]{1,0:T(8,128)(2,1)S(1)}, bf16[512,384]{1,0:T(8,128)(2,1)S(1)}, u32[]{:S(2)}, u32[]{:S(2)}) collective-permute-start(bf16[512,384]{1,0:T(8,128)(2,1)S(1)} %get-tuple-element.42), channel_id=1, source_target_pairs={{0,1},{1,0},{2,3},{3,2},{4,5},{5,4},{6,7},{7,6},{8,9},{9,8},{10,11... | collective-permute-start | bytes 1179656 | tf_op jit(solution)/shard_map/ppermute | solution.py:35
  35.9 2.7 %collective-permute-start.4 = (bf16[512,768]{1,0:T(8,128)(2,1)S(1)}, bf16[512,768]{1,0:T(8,128)(2,1)S(1)}, u32[]{:S(2)}, u32[]{:S(2)}) collective-permute-start(bf16[512,768]{1,0:T(8,128)(2,1)S(1)} %get-tuple-element.36.own_ref), channel_id=1, source_target_pairs={{1,8},{3,10},{4,13},{6,15},{8,1},{9,16},{10,3},{11,18},{12,21},{13... | collective-permute-start | bytes 2359304 | tf_op jit(solution)/shard_map/ppermute | solution.py:35
  38.6 3.8 %collective-permute-start = (bf16[384,768]{1,0:T(8,128)(2,1)S(1)}, bf16[384,768]{1,0:T(8,128)(2,1)S(1)}, u32[]{:S(2)}, u32[]{:S(2)}) collective-permute-start(bf16[384,768]{1,0:T(8,128)(2,1)S(1)} %get-tuple-element.31), channel_id=1, source_target_pairs={{0,6},{1,7},{2,4},{3,5},{4,2},{5,3},{6,0},{7,1},{8,14},{9,15},{10,... | collective-permute-start | bytes 1769480 | tf_op jit(solution)/shard_map/ppermute | solution.py:35
  42.4 1.8 %shard_map.76.q_ref = bf16[512,384]{1,0:T(8,128)(2,1)S(1)} custom-call(bf16[512,3072]{1,0:T(8,128)(2,1)S(1)} %get-tuple-element.37.normed, bf16[3072,384]{1,0:T(8,128)(2,1)S(1)} %get-tuple-element.38.weight), custom_call_target="tpu_custom_call" | custom-call | flops 1 | bytes 1 | tf_op jit(solution)/shard_map/pallas_call | solution.py:272
  44.2 6.5 %shard_map.77 = (f32[512,384]{1,0:T(8,128)S(1)}, f32[512,384]{1,0:T(8,128)S(1)}, f32[512,384]{1,0:T(8,128)S(1)}) custom-call(s32[7]{0:T(128)S(1)} %stack.35.where_ref, s32[64]{0:T(128)S(1)} %copy-done.1, bf16[512,384]{1,0:T(8,128)(2,1)S(1)} %shard_map.76.q_ref, bf16[512,768]{1,0:T(8,128)(2,1)S(1)} %get-tuple-element.36.own_ref, ...), custom_call_target="tpu_custom_call" | custom-call | flops 3221225472 | bytes 3145728 | tf_op jit(solution)/shard_map/pallas_call | solution.py:331
  50.7 1.9 %collective-permute-start.10 = (bf16[512,768]{1,0:T(8,128)(2,1)S(1)}, bf16[512,768]{1,0:T(8,128)(2,1)S(1)}, u32[]{:S(2)}, u32[]{:S(2)}) collective-permute-start(bf16[512,768]{1,0:T(8,128)(2,1)S(1)} %get-tuple-element.48.kept), channel_id=1, source_target_pairs={{4,0},{6,2},{8,4},{10,6},{12,8},{13,5},{14,10},{15,7},{16,12},{18,... | collective-permute-start | bytes 2359304 | tf_op jit(solution)/shard_map/ppermute | solution.py:35
  52.7 2.3 %collective-permute-start.11 = (bf16[384,768]{1,0:T(8,128)(2,1)S(1)}, bf16[384,768]{1,0:T(8,128)(2,1)S(1)}, u32[]{:S(2)}, u32[]{:S(2)}) collective-permute-start(bf16[384,768]{1,0:T(8,128)(2,1)S(1)} %get-tuple-element.49), channel_id=1, source_target_pairs={{0,1},{1,0},{2,3},{3,2},{4,5},{5,4},{6,7},{7,6},{8,9},{9,8},{10,11... | collective-permute-start | bytes 1769480 | tf_op jit(solution)/shard_map/ppermute | solution.py:35
  55.6 5.3 %shard_map.78.held = bf16[512,384]{1,0:T(8,128)(2,1)S(1)} custom-call(s32[7]{0:T(128)S(1)} %stack.35.where_ref, s32[64]{0:T(128)S(1)} %copy-done.1, bf16[512,384]{1,0:T(8,128)(2,1)S(1)} %shard_map.76.q_ref, bf16[512,768]{1,0:T(8,128)(2,1)S(1)} %collective-permute-done.4.kv_ref, f32[512,384]{1,0:T(8,128)S(1)} %get-tuple-element.44.o_ref, ...), custom_call_target="tpu_custom_call" | custom-call | flops 1 | bytes 1 | tf_op jit(solution)/shard_map/pallas_call | solution.py:371
  60.9 2.5 %collective-permute-start.9 = (bf16[512,384]{1,0:T(8,128)(2,1)S(1)}, bf16[512,384]{1,0:T(8,128)(2,1)S(1)}, u32[]{:S(2)}, u32[]{:S(2)}) collective-permute-start(bf16[512,384]{1,0:T(8,128)(2,1)S(1)} %shard_map.78.held), channel_id=1, source_target_pairs={{1,3},{3,1},{4,2},{6,0},{8,6},{9,11},{10,4},{11,9},{12,10},{13,7},... | collective-permute-start | bytes 1179656 | tf_op jit(solution)/shard_map/ppermute | solution.py:35
  63.4 1.9 %collective-permute-start.8 = (bf16[512,384]{1,0:T(8,128)(2,1)S(1)}, bf16[512,384]{1,0:T(8,128)(2,1)S(1)}, u32[]{:S(2)}, u32[]{:S(2)}) collective-permute-start(bf16[512,384]{1,0:T(8,128)(2,1)S(1)} %shard_map.78.held), channel_id=1, source_target_pairs={{4,0},{6,2},{8,4},{10,6},{12,8},{13,5},{14,10},{15,7},{16,12},{18,... | collective-permute-start | bytes 1179656 | tf_op jit(solution)/shard_map/ppermute | solution.py:35
  65.3 1.7 %shard_map.79 = (bf16[1536,768]{1,0:T(8,128)(2,1)S(1)}, f32[1,768]{1,0:T(1,128)S(1)}) custom-call(s32[7]{0:T(128)S(1)} %stack.35.where_ref, f32[64,384]{1,0:T(8,128)S(1)} %bitcast.12, bf16[384,3072]{1,0:T(8,128)(2,1)} %out_weight.5, bf16[384,768]{1,0:T(8,128)(2,1)S(1)} %collective-permute-done.11.w_twin, bf16[384,768]{1,0:T(8,128)(2,1)S(1)} %collective-permute-done.w_far, ...), custom_call_target="tpu_custom_call" | custom-call | flops 1 | bytes 1 | tf_op jit(solution)/shard_map/pallas_call | solution.py:411
  67.0 3.4 %collective-permute-start.14 = (bf16[512,384]{1,0:T(8,128)(2,1)S(1)}, bf16[512,384]{1,0:T(8,128)(2,1)S(1)}, u32[]{:S(2)}, u32[]{:S(2)}) collective-permute-start(bf16[512,384]{1,0:T(8,128)(2,1)S(1)} %shard_map.78.held), channel_id=1, source_target_pairs={{0,1},{1,0},{2,3},{3,2},{4,5},{5,4},{6,7},{7,6},{8,9},{9,8},{10,11... | collective-permute-start | bytes 1179656 | tf_op jit(solution)/shard_map/ppermute | solution.py:35
  70.4 9.0 %collective-permute-done.9.cross = bf16[512,384]{1,0:T(8,128)(2,1)S(1)} collective-permute-done((bf16[512,384]{1,0:T(8,128)(2,1)S(1)}, bf16[512,384]{1,0:T(8,128)(2,1)S(1)}, u32[]{:S(2)}, u32[]{:S(2)}) %collective-permute-start.9) | collective-permute-done | bytes 393248 | tf_op jit(solution)/shard_map/ppermute | solution.py:35
  79.4 3.0 %collective-permute-start.12 = (bf16[512,384]{1,0:T(8,128)(2,1)S(1)}, bf16[512,384]{1,0:T(8,128)(2,1)S(1)}, u32[]{:S(2)}, u32[]{:S(2)}) collective-permute-start(bf16[512,384]{1,0:T(8,128)(2,1)S(1)} %collective-permute-done.8.same), channel_id=1, source_target_pairs={{0,1},{1,0},{2,3},{3,2},{4,5},{5,4},{6,7},{7,6},{8,9},{9,8},{10,11... | collective-permute-start | bytes 1179656 | tf_op jit(solution)/shard_map/ppermute | solution.py:35
  82.4 1.3 %shard_map.80.partial = f32[512,768]{1,0:T(8,128)S(1)} custom-call(s32[7]{0:T(128)S(1)} %stack.35.where_ref, bf16[512,384]{1,0:T(8,128)(2,1)S(1)} %collective-permute-done.8.same, bf16[512,384]{1,0:T(8,128)(2,1)S(1)} %collective-permute-done.9.cross, bf16[512,384]{1,0:T(8,128)(2,1)S(1)} %shard_map.78.held, bf16[1536,768]{1,0:T(8,128)(2,1)S(1)} %get-tuple-element.50.weight), custom_call_target="tpu_custom_call" | custom-call | flops 1 | bytes 1 | tf_op jit(solution)/shard_map/pallas_call | solution.py:430
  84.3 2.2 %shard_map.81 = bf16[512,768]{1,0:T(8,128)(2,1)} custom-call(s32[7]{0:T(128)S(1)} %stack.35.where_ref, bf16[512,384]{1,0:T(8,128)(2,1)S(1)} %collective-permute-done.12.same, bf16[512,384]{1,0:T(8,128)(2,1)S(1)} %collective-permute-done.13.cross, bf16[512,384]{1,0:T(8,128)(2,1)S(1)} %collective-permute-done.14.held, ...), custom_call_target="tpu_custom_call" | custom-call | flops 1 | bytes 1 | tf_op jit(solution)/shard_map/pallas_call | solution.py:481
  (28 shorter events, 2.4 us)
Async XLA Ops:
  0.0 27.8 %collective-permute-start.3 = (bf16[3,3072,384]{2,1,0:T(8,128)(2,1)}, bf16[3,3072,384]{2,1,0:T(8,128)(2,1)}, u32[]{:S(2)}, u32[]{:S(2)}) collective-permute-start(bf16[3,3072,384]{2,1,0:T(8,128)(2,1)} %own_weight.1), channel_id=1, source_target_pairs={{0,1},{1,0},{2,3},{3,2},{4,5},{5,4},{6,7},{7,6},{8,9},{9,8},{10,11... | collective-permute-start | bytes 21233672 | tf_op jit(solution)/shard_map/ppermute | solution.py:35
  0.8 3.7 %copy-start.2 = (s32[64]{0:T(128)S(1)}, s32[64]{0:T(128)}, u32[]{:S(2)}) copy-start(s32[64]{0:T(128)} %param.8) | copy-start | bytes 772
  0.8 4.1 %copy-start = (bf16[512,144]{0,1:T(8,128)(2,1)S(1)}, bf16[512,144]{0,1:T(8,128)(2,1)}, u32[]{:S(2)}) copy-start(bf16[512,144]{0,1:T(8,128)(2,1)} %param.10) | copy-start | bytes 442372
  3.1 19.7 %collective-permute-start.1 = (bf16[256,3072]{1,0:T(8,128)(2,1)S(1)}, bf16[256,3072]{1,0:T(8,128)(2,1)S(1)}, u32[]{:S(2)}, u32[]{:S(2)}) collective-permute-start(bf16[256,3072]{1,0:T(8,128)(2,1)S(1)} %get-tuple-element.33), channel_id=1, source_target_pairs={{0,4},{1,7},{2,6},{3,5},{4,0},{5,3},{6,2},{7,1},{8,12},{9,15},{10,... | collective-permute-start | bytes 4718600 | tf_op jit(solution)/shard_map/ppermute | solution.py:35
  22.8 5.0 %collective-permute-start.2 = (bf16[256,3072]{1,0:T(8,128)(2,1)S(1)}, bf16[256,3072]{1,0:T(8,128)(2,1)S(1)}, u32[]{:S(2)}, u32[]{:S(2)}) collective-permute-start(bf16[256,3072]{1,0:T(8,128)(2,1)S(1)} %collective-permute-done.1.second), channel_id=1, source_target_pairs={{0,1},{1,0},{2,3},{3,2},{4,5},{5,4},{6,7},{7,6},{8,9},{9,8},{10,11... | collective-permute-start | bytes 4718600 | tf_op jit(solution)/shard_map/ppermute | solution.py:35
  24.8 17.6 %collective-permute-start.5 = (bf16[384,768]{1,0:T(8,128)(2,1)S(1)}, bf16[384,768]{1,0:T(8,128)(2,1)S(1)}, u32[]{:S(2)}, u32[]{:S(2)}) collective-permute-start(bf16[384,768]{1,0:T(8,128)(2,1)S(1)} %get-tuple-element.40), channel_id=1, source_target_pairs={{0,7},{1,6},{2,5},{3,4},{4,3},{5,2},{6,1},{7,0},{8,15},{9,14},{10,... | collective-permute-start | bytes 1769480 | tf_op jit(solution)/shard_map/ppermute | solution.py:35
  33.8 10.4 %collective-permute-start.6 = (bf16[512,384]{1,0:T(8,128)(2,1)S(1)}, bf16[512,384]{1,0:T(8,128)(2,1)S(1)}, u32[]{:S(2)}, u32[]{:S(2)}) collective-permute-start(bf16[512,384]{1,0:T(8,128)(2,1)S(1)} %get-tuple-element.42), channel_id=1, source_target_pairs={{0,1},{1,0},{2,3},{3,2},{4,5},{5,4},{6,7},{7,6},{8,9},{9,8},{10,11... | collective-permute-start | bytes 1179656 | tf_op jit(solution)/shard_map/ppermute | solution.py:35
  35.8 8.4 %collective-permute-start.7 = (bf16[512,384]{1,0:T(8,128)(2,1)S(1)}, bf16[512,384]{1,0:T(8,128)(2,1)S(1)}, u32[]{:S(2)}, u32[]{:S(2)}) collective-permute-start(bf16[512,384]{1,0:T(8,128)(2,1)S(1)} %get-tuple-element.43), channel_id=1, source_target_pairs={{0,1},{1,0},{2,3},{3,2},{4,5},{5,4},{6,7},{7,6},{8,9},{9,8},{10,11... | collective-permute-start | bytes 1179656 | tf_op jit(solution)/shard_map/ppermute | solution.py:35
  35.9 19.8 %collective-permute-start.4 = (bf16[512,768]{1,0:T(8,128)(2,1)S(1)}, bf16[512,768]{1,0:T(8,128)(2,1)S(1)}, u32[]{:S(2)}, u32[]{:S(2)}) collective-permute-start(bf16[512,768]{1,0:T(8,128)(2,1)S(1)} %get-tuple-element.36.own_ref), channel_id=1, source_target_pairs={{1,8},{3,10},{4,13},{6,15},{8,1},{9,16},{10,3},{11,18},{12,21},{13... | collective-permute-start | bytes 2359304 | tf_op jit(solution)/shard_map/ppermute | solution.py:35
  38.6 17.0 %collective-permute-start = (bf16[384,768]{1,0:T(8,128)(2,1)S(1)}, bf16[384,768]{1,0:T(8,128)(2,1)S(1)}, u32[]{:S(2)}, u32[]{:S(2)}) collective-permute-start(bf16[384,768]{1,0:T(8,128)(2,1)S(1)} %get-tuple-element.31), channel_id=1, source_target_pairs={{0,6},{1,7},{2,4},{3,5},{4,2},{5,3},{6,0},{7,1},{8,14},{9,15},{10,... | collective-permute-start | bytes 1769480 | tf_op jit(solution)/shard_map/ppermute | solution.py:35
  42.4 1.8 %copy-start.1 = (s32[64]{0:T(128)S(1)}, s32[64]{0:T(128)}, u32[]{:S(2)}) copy-start(s32[64]{0:T(128)} %counts_ref.3) | copy-start | bytes 772
  50.7 28.6 %collective-permute-start.10 = (bf16[512,768]{1,0:T(8,128)(2,1)S(1)}, bf16[512,768]{1,0:T(8,128)(2,1)S(1)}, u32[]{:S(2)}, u32[]{:S(2)}) collective-permute-start(bf16[512,768]{1,0:T(8,128)(2,1)S(1)} %get-tuple-element.48.kept), channel_id=1, source_target_pairs={{4,0},{6,2},{8,4},{10,6},{12,8},{13,5},{14,10},{15,7},{16,12},{18,... | collective-permute-start | bytes 2359304 | tf_op jit(solution)/shard_map/ppermute | solution.py:35
  52.7 12.6 %collective-permute-start.11 = (bf16[384,768]{1,0:T(8,128)(2,1)S(1)}, bf16[384,768]{1,0:T(8,128)(2,1)S(1)}, u32[]{:S(2)}, u32[]{:S(2)}) collective-permute-start(bf16[384,768]{1,0:T(8,128)(2,1)S(1)} %get-tuple-element.49), channel_id=1, source_target_pairs={{0,1},{1,0},{2,3},{3,2},{4,5},{5,4},{6,7},{7,6},{8,9},{9,8},{10,11... | collective-permute-start | bytes 1769480 | tf_op jit(solution)/shard_map/ppermute | solution.py:35
  60.9 18.5 %collective-permute-start.9 = (bf16[512,384]{1,0:T(8,128)(2,1)S(1)}, bf16[512,384]{1,0:T(8,128)(2,1)S(1)}, u32[]{:S(2)}, u32[]{:S(2)}) collective-permute-start(bf16[512,384]{1,0:T(8,128)(2,1)S(1)} %shard_map.78.held), channel_id=1, source_target_pairs={{1,3},{3,1},{4,2},{6,0},{8,6},{9,11},{10,4},{11,9},{12,10},{13,7},... | collective-permute-start | bytes 1179656 | tf_op jit(solution)/shard_map/ppermute | solution.py:35
  63.4 16.0 %collective-permute-start.8 = (bf16[512,384]{1,0:T(8,128)(2,1)S(1)}, bf16[512,384]{1,0:T(8,128)(2,1)S(1)}, u32[]{:S(2)}, u32[]{:S(2)}) collective-permute-start(bf16[512,384]{1,0:T(8,128)(2,1)S(1)} %shard_map.78.held), channel_id=1, source_target_pairs={{4,0},{6,2},{8,4},{10,6},{12,8},{13,5},{14,10},{15,7},{16,12},{18,... | collective-permute-start | bytes 1179656 | tf_op jit(solution)/shard_map/ppermute | solution.py:35
  67.0 16.7 %collective-permute-start.14 = (bf16[512,384]{1,0:T(8,128)(2,1)S(1)}, bf16[512,384]{1,0:T(8,128)(2,1)S(1)}, u32[]{:S(2)}, u32[]{:S(2)}) collective-permute-start(bf16[512,384]{1,0:T(8,128)(2,1)S(1)} %shard_map.78.held), channel_id=1, source_target_pairs={{0,1},{1,0},{2,3},{3,2},{4,5},{5,4},{6,7},{7,6},{8,9},{9,8},{10,11... | collective-permute-start | bytes 1179656 | tf_op jit(solution)/shard_map/ppermute | solution.py:35
  79.4 4.3 %collective-permute-start.12 = (bf16[512,384]{1,0:T(8,128)(2,1)S(1)}, bf16[512,384]{1,0:T(8,128)(2,1)S(1)}, u32[]{:S(2)}, u32[]{:S(2)}) collective-permute-start(bf16[512,384]{1,0:T(8,128)(2,1)S(1)} %collective-permute-done.8.same), channel_id=1, source_target_pairs={{0,1},{1,0},{2,3},{3,2},{4,5},{5,4},{6,7},{7,6},{8,9},{9,8},{10,11... | collective-permute-start | bytes 1179656 | tf_op jit(solution)/shard_map/ppermute | solution.py:35
  82.4 1.9 %collective-permute-start.13 = (bf16[512,384]{1,0:T(8,128)(2,1)S(1)}, bf16[512,384]{1,0:T(8,128)(2,1)S(1)}, u32[]{:S(2)}, u32[]{:S(2)}) collective-permute-start(bf16[512,384]{1,0:T(8,128)(2,1)S(1)} %collective-permute-done.9.cross), channel_id=1, source_target_pairs={{0,1},{1,0},{2,3},{3,2},{4,5},{5,4},{6,7},{7,6},{8,9},{9,8},{10,11... | collective-permute-start | bytes 1179656 | tf_op jit(solution)/shard_map/ppermute | solution.py:35

commit v5 on v4

--- a/solution.py
+++ b/solution.py
@@ -202,12 +202,10 @@
 
     start(core == 0, from_own)
     start(core == 1, from_pair)
-    start(core == parity, sum(weights_from(own_weight), []))
-    start(core != parity, sum(weights_from(twin_weight), []))
+    start(core == parity, sum(weights_from(own_weight)[:2], []))
+    start(core != parity, sum(weights_from(twin_weight)[:2], []))
     beside = where_ref[2] * 2 + 1 - core
     asides = copies_of(out_weight.at[:, lanes_at(beside, twin_out.shape[1])], twin_out, w_sems, 2, 6)
-    for copy in asides:
-        copy.start()
     spread(rows_ref, 0, flat)
     scale, shift = 1.0 + flat[:, width : 2 * width], flat[:, :width]
 
@@ -228,6 +226,10 @@
     keys, values, queries = weights_from(own_weight)
     for copy in keys + values:
         copy.wait()
+    start(core == parity, weights_from(own_weight)[2])
+    start(core != parity, weights_from(twin_weight)[2])
+    for copy in asides:
+        copy.start()
     kv = jnp.dot(states_ref[...], weight[...], preferred_element_type=jnp.float32).astype(jnp.bfloat16)
     kv_ref[...] = kv
     k_ref[...] = kv[:, :each]
@@ -284,13 +286,65 @@
     return jnp.where(inside, counts_ref[jnp.where(inside, at, 0)], 0)
 
 
-def bias_of(counts, span):
-    lane = lax.broadcasted_iota(jnp.int32, (1, span), 1)
-    return jnp.concatenate([jnp.where(lane < c * P_SIZE, 0.0, NEG) for c in counts], axis=1)
+LOG2E = math.log2(math.e)
 
 
 def scores_of(query, keys):
     return lax.dot_general(query, keys, (((1,), (1,)), ((), ())), preferred_element_type=jnp.float32)
+
+
+def dead_rows(span, count):
+    row = lax.broadcasted_iota(jnp.int32, (span, PAIR), 0)
+    return jnp.where(row < count * P_SIZE, 0.0, NEG).astype(jnp.bfloat16)
+
+
+def two_heads(keys, values, dead):
+    low = low_lanes(keys.shape)
+    lane = lax.broadcasted_iota(jnp.int32, keys.shape, 1)
+    zero, one = jnp.zeros_like(keys), jnp.ones_like(values)
+    return (
+        (jnp.where(low, keys, jnp.where(lane == HD, dead, zero)), jnp.where(low, values, one)),
+        (jnp.where(low, jnp.where(lane == 0, dead, zero), keys), jnp.where(low, one, values)),
+    )
+
+
+def two_queries(query):
+    low = low_lanes(query.shape)
+    lane = lax.broadcasted_iota(jnp.int32, query.shape, 1)
+    zero, one = jnp.zeros_like(query), jnp.ones_like(query)
+    return (
+        jnp.where(low, query, jnp.where(lane == HD, one, zero)),
+        jnp.where(low, jnp.where(lane == 0, one, zero), query),
+    )
+
+
+def attend(query_of, pairs, blocks, before_of, finish):
+    units = [(pair, rows) for pair in range(len(pairs)) for rows in blocks]
+
+    def scores(unit):
+        pair, rows = unit
+        return [scores_of(q, keys) for q, (keys, _) in zip(two_queries(query_of(pair, rows)), pairs[pair])]
+
+    following = scores(units[0])
+    for index, (pair, rows) in enumerate(units):
+        current = following
+        if index + 1 < len(units):
+            following = scores(units[index + 1])
+        peaks, numers = [], []
+        for head in range(2):
+            peak = jnp.max(current[head], axis=1, keepdims=True)
+            before = before_of(pair, rows, head)
+            peak = peak if before is None else jnp.maximum(peak, before)
+            probs = jnp.exp2((current[head] - peak) * LOG2E).astype(jnp.bfloat16)
+            peaks.append(peak)
+            numers.append(jnp.dot(probs, pairs[pair][head][1], preferred_element_type=jnp.float32))
+        low = low_lanes(numers[0].shape)
+        total = pltpu.roll(jnp.where(low, numers[1], numers[0]), HD, 1)
+        finish(pair, rows, jnp.where(low, *numers), jnp.where(low, *peaks), total)
+
+
+def pair_lanes(pair):
+    return slice(pair * PAIR, (pair + 1) * PAIR)
 
 
 def local_kernel(where_ref, counts_ref, q_ref, own_ref, k_twin, v_twin, o_ref, m_ref, l_ref):
@@ -298,31 +352,30 @@
     tile = 256
     core, slot = where_ref[1], where_ref[6]
     partner = slot + 1 - 2 * where_ref[4]
-    counts = [
-        count_at(counts_ref, jnp.where(core == 0, slot, partner)),
-        count_at(counts_ref, jnp.where(core == 0, partner, slot)),
+    own_count = count_at(counts_ref, jnp.where(core == 0, slot, partner))
+    twin_count = count_at(counts_ref, jnp.where(core == 0, partner, slot))
+    dead = jnp.concatenate([dead_rows(span, own_count), dead_rows(span, twin_count)], axis=0)
+    pairs = [
+        two_heads(
+            jnp.concatenate([own_ref[:, pair_lanes(pair)], k_twin[:, pair_lanes(pair)]], axis=0),
+            jnp.concatenate([own_ref[:, pair_lanes(3 + pair)], v_twin[:, pair_lanes(pair)]], axis=0),
+            dead,
+        )
+        for pair in range(3)
     ]
-    bias = bias_of(counts, span)
-    low = low_lanes((tile, PAIR))
-    for index in range(3):
-        lanes = slice(index * PAIR, (index + 1) * PAIR)
-        values_at = slice((3 + index) * PAIR, (4 + index) * PAIR)
-        keys = jnp.concatenate([own_ref[:, lanes], k_twin[:, lanes]], axis=0)
-        values = jnp.concatenate([own_ref[:, values_at], v_twin[:, lanes]], axis=0)
-        for start in range(0, span, tile):
-            rows = pl.ds(start, tile)
-            query = q_ref[rows, lanes]
-            zero = jnp.zeros_like(query)
-            outs = []
-            for masked in (jnp.where(low, query, zero), jnp.where(low, zero, query)):
-                scores = scores_of(masked, keys) + bias
-                peak = jnp.max(scores, axis=1, keepdims=True)
-                probs = jnp.exp(scores - peak)
-                total = jnp.sum(probs, axis=1, keepdims=True)
-                numer = jnp.dot(probs.astype(jnp.bfloat16), values, preferred_element_type=jnp.float32)
-                outs.append((numer, peak, total))
-            for ref, a, b in zip((o_ref, m_ref, l_ref), *outs):
-                ref[rows, lanes] = jnp.where(low, a, b)
+
+    def finish(pair, rows, numer, peak, total):
+        o_ref[rows, pair_lanes(pair)] = numer
+        m_ref[rows, pair_lanes(pair)] = peak
+        l_ref[rows, pair_lanes(pair)] = total
+
+    attend(
+        lambda pair, rows: q_ref[rows, pair_lanes(pair)],
+        pairs,
+        [pl.ds(start, tile) for start in range(0, span, tile)],
+        lambda pair, rows, head: None,
+        finish,
+    )
 
 
 def local_attention(where, counts, query, own, k_twin, v_twin):
@@ -343,27 +396,29 @@
     tile = 256
     core, slot = where_ref[1], where_ref[6]
     step = 1 - 2 * where_ref[4]
-    bias = bias_of([count_at(counts_ref, jnp.where(core == 0, slot - step, slot + 2 * step))], span)
-    low = low_lanes((tile, PAIR))
-    for index in range(3):
-        lanes = slice(index * PAIR, (index + 1) * PAIR)
-        keys, values = kv_ref[:, lanes], kv_ref[:, (3 + index) * PAIR : (4 + index) * PAIR]
-        for start in range(0, span, tile):
-            rows = pl.ds(start, tile)
-            query = q_ref[rows, lanes]
-            zero = jnp.zeros_like(query)
-            outs = []
-            for head, masked in enumerate((jnp.where(low, query, zero), jnp.where(low, zero, query))):
-                at = index * PAIR + head * HD
-                before = m_ref[rows, at : at + 1]
-                scores = scores_of(masked, keys) + bias
-                peak = jnp.maximum(jnp.max(scores, axis=1, keepdims=True), before)
-                probs = jnp.exp(scores - peak)
-                fade = jnp.exp(before - peak)
-                total = jnp.sum(probs, axis=1, keepdims=True) + fade * l_ref[rows, at : at + 1]
-                numer = jnp.dot(probs.astype(jnp.bfloat16), values, preferred_element_type=jnp.float32)
-                outs.append((numer + fade * o_ref[rows, lanes]) / total)
-            piece_ref[rows, lanes] = jnp.where(low, *outs).astype(jnp.bfloat16)
+    count = count_at(counts_ref, jnp.where(core == 0, slot - step, slot + 2 * step))
+    dead = dead_rows(span, count)
+    pairs = [
+        two_heads(kv_ref[:, pair_lanes(pair)], kv_ref[:, pair_lanes(3 + pair)], dead) for pair in range(3)
+    ]
+
+    def before(pair, rows, head):
+        at = pair * PAIR + head * HD
+        return m_ref[rows, at : at + 1]
+
+    def finish(pair, rows, numer, peak, total):
+        lanes = pair_lanes(pair)
+        fade = jnp.exp2((m_ref[rows, lanes] - peak) * LOG2E)
+        attn = (numer + fade * o_ref[rows, lanes]) / (total + fade * l_ref[rows, lanes])
+        piece_ref[rows, lanes] = attn.astype(jnp.bfloat16)
+
+    attend(
+        lambda pair, rows: q_ref[rows, pair_lanes(pair)],
+        pairs,
+        [pl.ds(start, tile) for start in range(0, span, tile)],
+        before,
+        finish,
+    )
 
 
 def remote_attention(where, counts, query, kv, o, m, l):

time: 88.3 us -> 86.8 us (0.983)
  Pallas kernels: 27.9 us -> 24.5 us
  waiting for transfers between devices: 11.9 us -> 13.9 us
    ppermute x15, waiting for transfers between devices: 11.9 us -> 13.9 us  [routed(): return lax.ppermute(array, BOTH, pairs)]
    pallas_call x1, Pallas kernels: 6.51 us -> 4.7 us  [local_attention(): pl.pallas_call(local_kernel, out_shape=(part,) * 3, in_specs=[smem_spec()...]
    pallas_call x1, Pallas kernels: 5.28 us -> 3.73 us  [remote_attention(): pl.pallas_call(remote_kernel, out_shape=near_out((span, 3 * PAIR)), in_sp...]
  transfers between devices with their start and end apart: 15 -> 15, of which waited for: 4 -> 4; matrix products, arithmetic and copies ran while one was open for 1% -> 1% of each run, Pallas kernels for 30% -> 26%
where the time goes in v5:
time: 86.8 us; the launch traced here: 85.1 us
  starting transfers between devices  28.8 us (33%)
  Pallas kernels  24.5 us (28%)
  blocking collectives  17.1 us (20%)
  waiting for transfers between devices  13.9 us (16%)
    ppermute x15, starting transfers between devices, routed(): return lax.ppermute(array, BOTH, pairs)  28.8 us
    all_to_all x1, blocking collectives, on_device(): mod_rows = lax.all_to_all(payload, 'queue', 0, 0, tiled=True)[:, 0, :]  17.1 us
    ppermute x15, waiting for transfers between devices, routed(): return lax.ppermute(array, BOTH, pairs)  13.9 us
    pallas_call x1, Pallas kernels, keys_values(): pl.pallas_call(kv_kernel, out_shape=(near_out((rows, 2 * each)), near_out...  5.95 us
    pallas_call x1, Pallas kernels, local_attention(): pl.pallas_call(local_kernel, out_shape=(part,) * 3, in_specs=[smem_spec()...  4.7 us
    pallas_call x1, Pallas kernels, remote_attention(): pl.pallas_call(remote_kernel, out_shape=near_out((span, 3 * PAIR)), in_sp...  3.73 us
    pallas_call x1, Pallas kernels, slices(): pl.pallas_call(slices_kernel, out_shape=(near_out((rows // 2, width)), ne...  2.32 us
    pallas_call x1, Pallas kernels, last_out(): pl.pallas_call(last_out_kernel, out_shape=jax.ShapeDtypeStruct((span, sha...  2.2 us
  transfers between devices with their start and end apart: 15, of which 4 were waited for; matrix products, arithmetic and copies ran while one was open for 1% of the time, Pallas kernels for 26%

profile of v5, /device:TPU:111, one launch (start us, length us, event | category | flops | bytes accessed | tf_op | source)
XLA Modules:
  0.0 85.1 jit_solution(7715825769574496481)
XLA Ops:
  0.8 2.3 %shard_map.73 = (bf16[256,3072]{1,0:T(8,128)(2,1)S(1)}, bf16[384,768]{1,0:T(8,128)(2,1)S(1)}, bf16[384,768]{1,0:T(8,128)(2,1)S(1)}) custom-call(s32[7]{0:T(128)S(1)} %stack.35.where_ref, bf16[512,3072]{1,0:T(8,128)(2,1)} %hidden.3, bf16[384,3072]{1,0:T(8,128)(2,1)} %out_weight.5), custom_call_target="tpu_custom_call" | custom-call | bytes 4194304 | tf_op jit(solution)/shard_map/pallas_call | solution.py:102
  3.1 1.4 %collective-permute-start.1 = (bf16[256,3072]{1,0:T(8,128)(2,1)S(1)}, bf16[256,3072]{1,0:T(8,128)(2,1)S(1)}, u32[]{:S(2)}, u32[]{:S(2)}) collective-permute-start(bf16[256,3072]{1,0:T(8,128)(2,1)S(1)} %get-tuple-element.33), channel_id=1, source_target_pairs={{0,4},{1,7},{2,6},{3,5},{4,0},{5,3},{6,2},{7,1},{8,12},{9,15},{10,... | collective-permute-start | bytes 4718600 | tf_op jit(solution)/shard_map/ppermute | solution.py:35
  5.7 17.1 %all_to_all.5 = f32[64,1,384]{2,1,0:T(1,128)S(1)} all-to-all(f32[64,1,384]{2,1,0:T(1,128)S(1)} %shard_map.74), channel_id=1, replica_groups=mesh['queue'=64,'heads'=4] {'queue'}, dimensions={0} | all-to-all | bytes 196608 | tf_op jit(solution)/shard_map/all_to_all | solution.py:571
  22.8 2.0 %collective-permute-start.2 = (bf16[256,3072]{1,0:T(8,128)(2,1)S(1)}, bf16[256,3072]{1,0:T(8,128)(2,1)S(1)}, u32[]{:S(2)}, u32[]{:S(2)}) collective-permute-start(bf16[256,3072]{1,0:T(8,128)(2,1)S(1)} %collective-permute-done.1.second), channel_id=1, source_target_pairs={{0,1},{1,0},{2,3},{3,2},{4,5},{5,4},{6,7},{7,6},{8,9},{9,8},{10,11... | collective-permute-start | bytes 4718600 | tf_op jit(solution)/shard_map/ppermute | solution.py:35
  24.8 1.3 %collective-permute-start.5 = (bf16[384,768]{1,0:T(8,128)(2,1)S(1)}, bf16[384,768]{1,0:T(8,128)(2,1)S(1)}, u32[]{:S(2)}, u32[]{:S(2)}) collective-permute-start(bf16[384,768]{1,0:T(8,128)(2,1)S(1)} %get-tuple-element.40), channel_id=1, source_target_pairs={{0,7},{1,6},{2,5},{3,4},{4,3},{5,2},{6,1},{7,0},{8,15},{9,14},{10,... | collective-permute-start | bytes 1769480 | tf_op jit(solution)/shard_map/ppermute | solution.py:35
  26.1 1.8 %collective-permute-done.2.first = bf16[256,3072]{1,0:T(8,128)(2,1)S(1)} collective-permute-done((bf16[256,3072]{1,0:T(8,128)(2,1)S(1)}, bf16[256,3072]{1,0:T(8,128)(2,1)S(1)}, u32[]{:S(2)}, u32[]{:S(2)}) %collective-permute-start.2) | collective-permute-done | bytes 1572896 | tf_op jit(solution)/shard_map/ppermute | solution.py:35
  27.8 6.0 %shard_map.75 = (bf16[512,768]{1,0:T(8,128)(2,1)S(1)}, bf16[512,384]{1,0:T(8,128)(2,1)S(1)}, bf16[512,384]{1,0:T(8,128)(2,1)S(1)}, bf16[512,3072]{1,0:T(8,128)(2...) custom-call(s32[7]{0:T(128)S(1)} %stack.35.where_ref, ...), custom_call_target="tpu_custom_call" | custom-call | flops 1 | bytes 1 | tf_op jit(solution)/shard_map/pallas_call | solution.py:244
  33.8 2.0 %collective-permute-start.6 = (bf16[512,384]{1,0:T(8,128)(2,1)S(1)}, bf16[512,384]{1,0:T(8,128)(2,1)S(1)}, u32[]{:S(2)}, u32[]{:S(2)}) collective-permute-start(bf16[512,384]{1,0:T(8,128)(2,1)S(1)} %get-tuple-element.42), channel_id=1, source_target_pairs={{0,1},{1,0},{2,3},{3,2},{4,5},{5,4},{6,7},{7,6},{8,9},{9,8},{10,11... | collective-permute-start | bytes 1179656 | tf_op jit(solution)/shard_map/ppermute | solution.py:35
  35.9 2.7 %collective-permute-start.4 = (bf16[512,768]{1,0:T(8,128)(2,1)S(1)}, bf16[512,768]{1,0:T(8,128)(2,1)S(1)}, u32[]{:S(2)}, u32[]{:S(2)}) collective-permute-start(bf16[512,768]{1,0:T(8,128)(2,1)S(1)} %get-tuple-element.36.own_ref), channel_id=1, source_target_pairs={{1,8},{3,10},{4,13},{6,15},{8,1},{9,16},{10,3},{11,18},{12,21},{13... | collective-permute-start | bytes 2359304 | tf_op jit(solution)/shard_map/ppermute | solution.py:35
  38.6 3.8 %collective-permute-start = (bf16[384,768]{1,0:T(8,128)(2,1)S(1)}, bf16[384,768]{1,0:T(8,128)(2,1)S(1)}, u32[]{:S(2)}, u32[]{:S(2)}) collective-permute-start(bf16[384,768]{1,0:T(8,128)(2,1)S(1)} %get-tuple-element.31), channel_id=1, source_target_pairs={{0,6},{1,7},{2,4},{3,5},{4,2},{5,3},{6,0},{7,1},{8,14},{9,15},{10,... | collective-permute-start | bytes 1769480 | tf_op jit(solution)/shard_map/ppermute | solution.py:35
  42.4 1.8 %shard_map.76.q_ref = bf16[512,384]{1,0:T(8,128)(2,1)S(1)} custom-call(bf16[512,3072]{1,0:T(8,128)(2,1)S(1)} %get-tuple-element.37.normed, bf16[3072,384]{1,0:T(8,128)(2,1)S(1)} %get-tuple-element.38.weight), custom_call_target="tpu_custom_call" | custom-call | flops 1 | bytes 1 | tf_op jit(solution)/shard_map/pallas_call | solution.py:274
  44.2 4.7 %shard_map.77 = (f32[512,384]{1,0:T(8,128)S(1)}, f32[512,384]{1,0:T(8,128)S(1)}, f32[512,384]{1,0:T(8,128)S(1)}) custom-call(s32[7]{0:T(128)S(1)} %stack.35.where_ref, s32[64]{0:T(128)S(1)} %copy-done.1, bf16[512,384]{1,0:T(8,128)(2,1)S(1)} %shard_map.76.q_ref, bf16[512,768]{1,0:T(8,128)(2,1)S(1)} %get-tuple-element.36.own_ref, ...), custom_call_target="tpu_custom_call" | custom-call | flops 3221225472 | bytes 3145728 | tf_op jit(solution)/shard_map/pallas_call | solution.py:384
  48.9 1.9 %collective-permute-start.10 = (bf16[512,768]{1,0:T(8,128)(2,1)S(1)}, bf16[512,768]{1,0:T(8,128)(2,1)S(1)}, u32[]{:S(2)}, u32[]{:S(2)}) collective-permute-start(bf16[512,768]{1,0:T(8,128)(2,1)S(1)} %get-tuple-element.48.kept), channel_id=1, source_target_pairs={{4,0},{6,2},{8,4},{10,6},{12,8},{13,5},{14,10},{15,7},{16,12},{18,... | collective-permute-start | bytes 2359304 | tf_op jit(solution)/shard_map/ppermute | solution.py:35
  50.8 2.4 %collective-permute-start.11 = (bf16[384,768]{1,0:T(8,128)(2,1)S(1)}, bf16[384,768]{1,0:T(8,128)(2,1)S(1)}, u32[]{:S(2)}, u32[]{:S(2)}) collective-permute-start(bf16[384,768]{1,0:T(8,128)(2,1)S(1)} %get-tuple-element.49), channel_id=1, source_target_pairs={{0,1},{1,0},{2,3},{3,2},{4,5},{5,4},{6,7},{7,6},{8,9},{9,8},{10,11... | collective-permute-start | bytes 1769480 | tf_op jit(solution)/shard_map/ppermute | solution.py:35
  53.2 2.4 %collective-permute-done.w_far = bf16[384,768]{1,0:T(8,128)(2,1)S(1)} collective-permute-done((bf16[384,768]{1,0:T(8,128)(2,1)S(1)}, bf16[384,768]{1,0:T(8,128)(2,1)S(1)}, u32[]{:S(2)}, u32[]{:S(2)}) %collective-permute-start) | collective-permute-done | bytes 589856 | tf_op jit(solution)/shard_map/ppermute | solution.py:35
  55.6 3.7 %shard_map.78.held = bf16[512,384]{1,0:T(8,128)(2,1)S(1)} custom-call(s32[7]{0:T(128)S(1)} %stack.35.where_ref, s32[64]{0:T(128)S(1)} %copy-done.1, bf16[512,384]{1,0:T(8,128)(2,1)S(1)} %shard_map.76.q_ref, bf16[512,768]{1,0:T(8,128)(2,1)S(1)} %collective-permute-done.4.kv_ref, f32[512,384]{1,0:T(8,128)S(1)} %get-tuple-element.44.o_ref, ...), custom_call_target="tpu_custom_call" | custom-call | flops 1 | bytes 1 | tf_op jit(solution)/shard_map/pallas_call | solution.py:426
  59.3 2.5 %collective-permute-start.9 = (bf16[512,384]{1,0:T(8,128)(2,1)S(1)}, bf16[512,384]{1,0:T(8,128)(2,1)S(1)}, u32[]{:S(2)}, u32[]{:S(2)}) collective-permute-start(bf16[512,384]{1,0:T(8,128)(2,1)S(1)} %shard_map.78.held), channel_id=1, source_target_pairs={{1,3},{3,1},{4,2},{6,0},{8,6},{9,11},{10,4},{11,9},{12,10},{13,7},... | collective-permute-start | bytes 1179656 | tf_op jit(solution)/shard_map/ppermute | solution.py:35
  61.8 1.9 %collective-permute-start.8 = (bf16[512,384]{1,0:T(8,128)(2,1)S(1)}, bf16[512,384]{1,0:T(8,128)(2,1)S(1)}, u32[]{:S(2)}, u32[]{:S(2)}) collective-permute-start(bf16[512,384]{1,0:T(8,128)(2,1)S(1)} %shard_map.78.held), channel_id=1, source_target_pairs={{4,0},{6,2},{8,4},{10,6},{12,8},{13,5},{14,10},{15,7},{16,12},{18,... | collective-permute-start | bytes 1179656 | tf_op jit(solution)/shard_map/ppermute | solution.py:35
  63.8 1.7 %shard_map.79 = (bf16[1536,768]{1,0:T(8,128)(2,1)S(1)}, f32[1,768]{1,0:T(1,128)S(1)}) custom-call(s32[7]{0:T(128)S(1)} %stack.35.where_ref, f32[64,384]{1,0:T(8,128)S(1)} %bitcast.12, bf16[384,3072]{1,0:T(8,128)(2,1)} %out_weight.5, bf16[384,768]{1,0:T(8,128)(2,1)S(1)} %collective-permute-done.11.w_twin, bf16[384,768]{1,0:T(8,128)(2,1)S(1)} %collective-permute-done.w_far, ...), custom_call_target="tpu_custom_call" | custom-call | flops 1 | bytes 1 | tf_op jit(solution)/shard_map/pallas_call | solution.py:466
  65.5 3.2 %collective-permute-start.14 = (bf16[512,384]{1,0:T(8,128)(2,1)S(1)}, bf16[512,384]{1,0:T(8,128)(2,1)S(1)}, u32[]{:S(2)}, u32[]{:S(2)}) collective-permute-start(bf16[512,384]{1,0:T(8,128)(2,1)S(1)} %shard_map.78.held), channel_id=1, source_target_pairs={{0,1},{1,0},{2,3},{3,2},{4,5},{5,4},{6,7},{7,6},{8,9},{9,8},{10,11... | collective-permute-start | bytes 1179656 | tf_op jit(solution)/shard_map/ppermute | solution.py:35
  68.6 9.2 %collective-permute-done.9.cross = bf16[512,384]{1,0:T(8,128)(2,1)S(1)} collective-permute-done((bf16[512,384]{1,0:T(8,128)(2,1)S(1)}, bf16[512,384]{1,0:T(8,128)(2,1)S(1)}, u32[]{:S(2)}, u32[]{:S(2)}) %collective-permute-start.9) | collective-permute-done | bytes 393248 | tf_op jit(solution)/shard_map/ppermute | solution.py:35
  77.8 3.0 %collective-permute-start.12 = (bf16[512,384]{1,0:T(8,128)(2,1)S(1)}, bf16[512,384]{1,0:T(8,128)(2,1)S(1)}, u32[]{:S(2)}, u32[]{:S(2)}) collective-permute-start(bf16[512,384]{1,0:T(8,128)(2,1)S(1)} %collective-permute-done.8.same), channel_id=1, source_target_pairs={{0,1},{1,0},{2,3},{3,2},{4,5},{5,4},{6,7},{7,6},{8,9},{9,8},{10,11... | collective-permute-start | bytes 1179656 | tf_op jit(solution)/shard_map/ppermute | solution.py:35
  80.8 1.3 %shard_map.80.partial = f32[512,768]{1,0:T(8,128)S(1)} custom-call(s32[7]{0:T(128)S(1)} %stack.35.where_ref, bf16[512,384]{1,0:T(8,128)(2,1)S(1)} %collective-permute-done.8.same, bf16[512,384]{1,0:T(8,128)(2,1)S(1)} %collective-permute-done.9.cross, bf16[512,384]{1,0:T(8,128)(2,1)S(1)} %shard_map.78.held, bf16[1536,768]{1,0:T(8,128)(2,1)S(1)} %get-tuple-element.50.weight), custom_call_target="tpu_custom_call" | custom-call | flops 1 | bytes 1 | tf_op jit(solution)/shard_map/pallas_call | solution.py:485
  82.7 2.2 %shard_map.81 = bf16[512,768]{1,0:T(8,128)(2,1)} custom-call(s32[7]{0:T(128)S(1)} %stack.35.where_ref, bf16[512,384]{1,0:T(8,128)(2,1)S(1)} %collective-permute-done.12.same, bf16[512,384]{1,0:T(8,128)(2,1)S(1)} %collective-permute-done.13.cross, bf16[512,384]{1,0:T(8,128)(2,1)S(1)} %collective-permute-done.14.held, ...), custom_call_target="tpu_custom_call" | custom-call | flops 1 | bytes 1 | tf_op jit(solution)/shard_map/pallas_call | solution.py:536
  (28 shorter events, 2.6 us)
Async XLA Ops:
  0.0 27.8 %collective-permute-start.3 = (bf16[3,3072,384]{2,1,0:T(8,128)(2,1)}, bf16[3,3072,384]{2,1,0:T(8,128)(2,1)}, u32[]{:S(2)}, u32[]{:S(2)}) collective-permute-start(bf16[3,3072,384]{2,1,0:T(8,128)(2,1)} %own_weight.1), channel_id=1, source_target_pairs={{0,1},{1,0},{2,3},{3,2},{4,5},{5,4},{6,7},{7,6},{8,9},{9,8},{10,11... | collective-permute-start | bytes 21233672 | tf_op jit(solution)/shard_map/ppermute | solution.py:35
  0.8 3.7 %copy-start.2 = (s32[64]{0:T(128)S(1)}, s32[64]{0:T(128)}, u32[]{:S(2)}) copy-start(s32[64]{0:T(128)} %param.8) | copy-start | bytes 772
  0.8 4.1 %copy-start = (bf16[512,144]{0,1:T(8,128)(2,1)S(1)}, bf16[512,144]{0,1:T(8,128)(2,1)}, u32[]{:S(2)}) copy-start(bf16[512,144]{0,1:T(8,128)(2,1)} %param.10) | copy-start | bytes 442372
  3.1 19.7 %collective-permute-start.1 = (bf16[256,3072]{1,0:T(8,128)(2,1)S(1)}, bf16[256,3072]{1,0:T(8,128)(2,1)S(1)}, u32[]{:S(2)}, u32[]{:S(2)}) collective-permute-start(bf16[256,3072]{1,0:T(8,128)(2,1)S(1)} %get-tuple-element.33), channel_id=1, source_target_pairs={{0,4},{1,7},{2,6},{3,5},{4,0},{5,3},{6,2},{7,1},{8,12},{9,15},{10,... | collective-permute-start | bytes 4718600 | tf_op jit(solution)/shard_map/ppermute | solution.py:35
  22.8 5.0 %collective-permute-start.2 = (bf16[256,3072]{1,0:T(8,128)(2,1)S(1)}, bf16[256,3072]{1,0:T(8,128)(2,1)S(1)}, u32[]{:S(2)}, u32[]{:S(2)}) collective-permute-start(bf16[256,3072]{1,0:T(8,128)(2,1)S(1)} %collective-permute-done.1.second), channel_id=1, source_target_pairs={{0,1},{1,0},{2,3},{3,2},{4,5},{5,4},{6,7},{7,6},{8,9},{9,8},{10,11... | collective-permute-start | bytes 4718600 | tf_op jit(solution)/shard_map/ppermute | solution.py:35
  24.8 17.6 %collective-permute-start.5 = (bf16[384,768]{1,0:T(8,128)(2,1)S(1)}, bf16[384,768]{1,0:T(8,128)(2,1)S(1)}, u32[]{:S(2)}, u32[]{:S(2)}) collective-permute-start(bf16[384,768]{1,0:T(8,128)(2,1)S(1)} %get-tuple-element.40), channel_id=1, source_target_pairs={{0,7},{1,6},{2,5},{3,4},{4,3},{5,2},{6,1},{7,0},{8,15},{9,14},{10,... | collective-permute-start | bytes 1769480 | tf_op jit(solution)/shard_map/ppermute | solution.py:35
  33.8 10.4 %collective-permute-start.6 = (bf16[512,384]{1,0:T(8,128)(2,1)S(1)}, bf16[512,384]{1,0:T(8,128)(2,1)S(1)}, u32[]{:S(2)}, u32[]{:S(2)}) collective-permute-start(bf16[512,384]{1,0:T(8,128)(2,1)S(1)} %get-tuple-element.42), channel_id=1, source_target_pairs={{0,1},{1,0},{2,3},{3,2},{4,5},{5,4},{6,7},{7,6},{8,9},{9,8},{10,11... | collective-permute-start | bytes 1179656 | tf_op jit(solution)/shard_map/ppermute | solution.py:35
  35.8 8.4 %collective-permute-start.7 = (bf16[512,384]{1,0:T(8,128)(2,1)S(1)}, bf16[512,384]{1,0:T(8,128)(2,1)S(1)}, u32[]{:S(2)}, u32[]{:S(2)}) collective-permute-start(bf16[512,384]{1,0:T(8,128)(2,1)S(1)} %get-tuple-element.43), channel_id=1, source_target_pairs={{0,1},{1,0},{2,3},{3,2},{4,5},{5,4},{6,7},{7,6},{8,9},{9,8},{10,11... | collective-permute-start | bytes 1179656 | tf_op jit(solution)/shard_map/ppermute | solution.py:35
  35.9 19.7 %collective-permute-start.4 = (bf16[512,768]{1,0:T(8,128)(2,1)S(1)}, bf16[512,768]{1,0:T(8,128)(2,1)S(1)}, u32[]{:S(2)}, u32[]{:S(2)}) collective-permute-start(bf16[512,768]{1,0:T(8,128)(2,1)S(1)} %get-tuple-element.36.own_ref), channel_id=1, source_target_pairs={{1,8},{3,10},{4,13},{6,15},{8,1},{9,16},{10,3},{11,18},{12,21},{13... | collective-permute-start | bytes 2359304 | tf_op jit(solution)/shard_map/ppermute | solution.py:35
  38.6 17.0 %collective-permute-start = (bf16[384,768]{1,0:T(8,128)(2,1)S(1)}, bf16[384,768]{1,0:T(8,128)(2,1)S(1)}, u32[]{:S(2)}, u32[]{:S(2)}) collective-permute-start(bf16[384,768]{1,0:T(8,128)(2,1)S(1)} %get-tuple-element.31), channel_id=1, source_target_pairs={{0,6},{1,7},{2,4},{3,5},{4,2},{5,3},{6,0},{7,1},{8,14},{9,15},{10,... | collective-permute-start | bytes 1769480 | tf_op jit(solution)/shard_map/ppermute | solution.py:35
  42.4 1.8 %copy-start.1 = (s32[64]{0:T(128)S(1)}, s32[64]{0:T(128)}, u32[]{:S(2)}) copy-start(s32[64]{0:T(128)} %counts_ref.3) | copy-start | bytes 772
  48.9 28.9 %collective-permute-start.10 = (bf16[512,768]{1,0:T(8,128)(2,1)S(1)}, bf16[512,768]{1,0:T(8,128)(2,1)S(1)}, u32[]{:S(2)}, u32[]{:S(2)}) collective-permute-start(bf16[512,768]{1,0:T(8,128)(2,1)S(1)} %get-tuple-element.48.kept), channel_id=1, source_target_pairs={{4,0},{6,2},{8,4},{10,6},{12,8},{13,5},{14,10},{15,7},{16,12},{18,... | collective-permute-start | bytes 2359304 | tf_op jit(solution)/shard_map/ppermute | solution.py:35
  50.8 12.9 %collective-permute-start.11 = (bf16[384,768]{1,0:T(8,128)(2,1)S(1)}, bf16[384,768]{1,0:T(8,128)(2,1)S(1)}, u32[]{:S(2)}, u32[]{:S(2)}) collective-permute-start(bf16[384,768]{1,0:T(8,128)(2,1)S(1)} %get-tuple-element.49), channel_id=1, source_target_pairs={{0,1},{1,0},{2,3},{3,2},{4,5},{5,4},{6,7},{7,6},{8,9},{9,8},{10,11... | collective-permute-start | bytes 1769480 | tf_op jit(solution)/shard_map/ppermute | solution.py:35
  59.3 18.5 %collective-permute-start.9 = (bf16[512,384]{1,0:T(8,128)(2,1)S(1)}, bf16[512,384]{1,0:T(8,128)(2,1)S(1)}, u32[]{:S(2)}, u32[]{:S(2)}) collective-permute-start(bf16[512,384]{1,0:T(8,128)(2,1)S(1)} %shard_map.78.held), channel_id=1, source_target_pairs={{1,3},{3,1},{4,2},{6,0},{8,6},{9,11},{10,4},{11,9},{12,10},{13,7},... | collective-permute-start | bytes 1179656 | tf_op jit(solution)/shard_map/ppermute | solution.py:35
  61.8 16.0 %collective-permute-start.8 = (bf16[512,384]{1,0:T(8,128)(2,1)S(1)}, bf16[512,384]{1,0:T(8,128)(2,1)S(1)}, u32[]{:S(2)}, u32[]{:S(2)}) collective-permute-start(bf16[512,384]{1,0:T(8,128)(2,1)S(1)} %shard_map.78.held), channel_id=1, source_target_pairs={{4,0},{6,2},{8,4},{10,6},{12,8},{13,5},{14,10},{15,7},{16,12},{18,... | collective-permute-start | bytes 1179656 | tf_op jit(solution)/shard_map/ppermute | solution.py:35
  65.5 16.7 %collective-permute-start.14 = (bf16[512,384]{1,0:T(8,128)(2,1)S(1)}, bf16[512,384]{1,0:T(8,128)(2,1)S(1)}, u32[]{:S(2)}, u32[]{:S(2)}) collective-permute-start(bf16[512,384]{1,0:T(8,128)(2,1)S(1)} %shard_map.78.held), channel_id=1, source_target_pairs={{0,1},{1,0},{2,3},{3,2},{4,5},{5,4},{6,7},{7,6},{8,9},{9,8},{10,11... | collective-permute-start | bytes 1179656 | tf_op jit(solution)/shard_map/ppermute | solution.py:35
  77.8 4.3 %collective-permute-start.12 = (bf16[512,384]{1,0:T(8,128)(2,1)S(1)}, bf16[512,384]{1,0:T(8,128)(2,1)S(1)}, u32[]{:S(2)}, u32[]{:S(2)}) collective-permute-start(bf16[512,384]{1,0:T(8,128)(2,1)S(1)} %collective-permute-done.8.same), channel_id=1, source_target_pairs={{0,1},{1,0},{2,3},{3,2},{4,5},{5,4},{6,7},{7,6},{8,9},{9,8},{10,11... | collective-permute-start | bytes 1179656 | tf_op jit(solution)/shard_map/ppermute | solution.py:35
  80.8 1.9 %collective-permute-start.13 = (bf16[512,384]{1,0:T(8,128)(2,1)S(1)}, bf16[512,384]{1,0:T(8,128)(2,1)S(1)}, u32[]{:S(2)}, u32[]{:S(2)}) collective-permute-start(bf16[512,384]{1,0:T(8,128)(2,1)S(1)} %collective-permute-done.9.cross), channel_id=1, source_target_pairs={{0,1},{1,0},{2,3},{3,2},{4,5},{5,4},{6,7},{7,6},{8,9},{9,8},{10,11... | collective-permute-start | bytes 1179656 | tf_op jit(solution)/shard_map/ppermute | solution.py:35

commit v6 on v5

--- a/solution.py
+++ b/solution.py
@@ -81,14 +81,12 @@
     return pl.ds(pl.multiple_of(index * size, size), size)
 
 
-def slices_kernel(where_ref, hidden, out_weight, mine, far_same, far_cross, sems):
+def slices_kernel(where_ref, hidden, out_weight, mine, far_out, sems):
     core, y_hi = where_ref[1], where_ref[2]
-    half, width = mine.shape[0], far_same.shape[1]
-    away = (1 - y_hi) * 2
+    half, width = mine.shape[0], far_out.shape[1]
     copies = (
         copies_of(hidden.at[lanes_at(core, half), :], mine, sems, 4)
-        + copies_of(out_weight.at[:, lanes_at(away + core, width)], far_same, sems, 2, 4)
-        + copies_of(out_weight.at[:, lanes_at(away + 1 - core, width)], far_cross, sems, 2, 6)
+        + copies_of(out_weight.at[:, lanes_at(1 - y_hi, width)], far_out, sems, 4, 4)
     )
     for copy in copies:
         copy.start()
@@ -103,11 +101,10 @@
         slices_kernel,
         out_shape=(
             near_out((rows // 2, width)),
-            near_out((depth, share)),
-            near_out((depth, share)),
+            near_out((depth, 2 * share)),
         ),
         in_specs=[smem_spec(), any_spec(), any_spec()],
-        out_specs=(vmem_spec(),) * 3,
+        out_specs=(vmem_spec(),) * 2,
         scratch_shapes=[pltpu.SemaphoreType.DMA((8,))],
         compiler_params=pltpu.CompilerParams(vmem_limit_bytes=2 * MIB),
         cost_estimate=cost(0, 4 * MIB),
@@ -209,8 +206,8 @@
     spread(rows_ref, 0, flat)
     scale, shift = 1.0 + flat[:, width : 2 * width], flat[:, :width]
 
-    def normalise(first_row):
-        for start in range(first_row, first_row + half, NORM_ROWS):
+    def normalise(first_row, count):
+        for start in range(first_row, first_row + count, NORM_ROWS):
             block = pl.ds(start, NORM_ROWS)
             states = states_ref[block, :].astype(jnp.float32)
             mean = jnp.mean(states, axis=1, keepdims=True)
@@ -218,11 +215,12 @@
             var = jnp.mean(centred * centred, axis=1, keepdims=True)
             states_ref[block, :] = (centred * lax.rsqrt(var + 1e-05) * scale + shift).astype(jnp.bfloat16)
 
-    for copy in from_own:
+    step = rows // len(from_own)
+    for index, copy in enumerate(from_own):
         copy.wait()
-    share_ref[...] = states_ref[:, lanes_at(where_ref[0], share_ref.shape[1])]
-    normalise(0)
-    normalise(half)
+        block = pl.ds(index * step, step)
+        share_ref[block, :] = states_ref[block, lanes_at(where_ref[0], share_ref.shape[1])]
+        normalise(index * step, step)
     keys, values, queries = weights_from(own_weight)
     for copy in keys + values:
         copy.wait()
@@ -387,7 +385,7 @@
         in_specs=[smem_spec()] * 2 + [vmem_spec()] * 4,
         out_specs=(vmem_spec(),) * 3,
         compiler_params=pltpu.CompilerParams(vmem_limit_bytes=16 * MIB),
-        cost_estimate=cost(8 * 6 * span * span * 256, 3 * MIB),
+        cost_estimate=cost(1, 1),
     )(where, counts, near(query), near(own), k_twin, v_twin)
 
 
@@ -441,12 +439,12 @@
     width = flat.shape[1] // 3
     block = out_weight.shape[0]
     local = jnp.where(core == 0, 1 - parity, parity)
-    whole, own = pl.ds(0, share), lanes_at(member, share)
+    whole, mine, own = pl.ds(0, share), lanes_at(core, share), lanes_at(member, share)
     copies = []
     for source, lanes, far_half, y_lo in (
         (out_weight, own, 0, core),
         (w_twin, whole, 0, 1 - core),
-        (w_far, whole, 1, core),
+        (w_far, mine, 1, core),
         (w_far_twin, whole, 1, 1 - core),
     ):
         base = jnp.where(local == y_lo, 0, 2 * block) + far_half * block
@@ -458,6 +456,27 @@
     gate[...] = flat[:, pl.ds(pl.multiple_of(2 * width + member * share, PAIR), share)]
     for copy in copies:
         copy.wait()
+
+
+def columns_kernel(where_ref, source, out, sems):
+    copies = copies_of(source.at[:, lanes_at(1 - where_ref[1], out.shape[1])], out, sems, 4)
+    for copy in copies:
+        copy.start()
+    for copy in copies:
+        copy.wait()
+
+
+def columns_of_twin(where, blocks):
+    rows, width = blocks.shape
+    return pl.pallas_call(
+        columns_kernel,
+        out_shape=near_out((rows, width // 2)),
+        in_specs=[smem_spec(), any_spec()],
+        out_specs=vmem_spec(),
+        scratch_shapes=[pltpu.SemaphoreType.DMA((4,))],
+        compiler_params=pltpu.CompilerParams(vmem_limit_bytes=2 * MIB),
+        cost_estimate=cost(1, 1),
+    )(where, blocks)
 
 
 def tail_inputs(where, mod_rows, out_weight, w_twin, w_far, w_far_twin):
@@ -564,15 +583,14 @@
     frame_counts = frame_counts.astype(jnp.int32)
 
     twin_weight = twin(qkv_weight)
-    mine, far_same, far_cross = slices(where, hidden, out_weight, members)
+    mine, far_mine = slices(where, hidden, out_weight, members)
     second = route(mine, target=lambda s, y, k: (s ^ 1, y ^ k, k))
 
     payload = modulate(where, embed_levels(levels, mod_weight.shape[0]), mod_weight)
     mod_rows = lax.all_to_all(payload, "queue", 0, 0, tiled=True)[:, 0, :]
 
     first = twin(after(second, mod_rows))
-    w_far = route(after(far_same, mod_rows), target=lambda s, y, k: (s ^ 1, 1 - y, k))
-    w_far_twin = route(after(far_cross, mod_rows), target=lambda s, y, k: (s ^ 1, 1 - y, 1 - k))
+    w_far = route(after(far_mine, mod_rows), target=lambda s, y, k: (s ^ 1, 1 - y, k))
     kv, k, v, normed, q_weight, twin_mine, share_states = keys_values(where, mod_rows, hidden, first, second, qkv_weight, twin_weight, out_weight)
 
     def remote_target(s, y, k):
@@ -582,13 +600,12 @@
     kv_remote = route(kv, target=remote_target)
     k_twin, v_twin = twin(k), twin(v)
     query = queries(after(normed, kv), q_weight)
-    w_twin = twin(twin_mine)
-    o, m, l = local_attention(after(where, w_far_twin), frame_counts, query, kv, k_twin, v_twin)
+    o, m, l = local_attention(where, frame_counts, query, kv, k_twin, v_twin)
     residual = route(
         after(share_states, o),
         target=lambda s, y, k: (s - 1, y, 0) if k == 0 else ((s - 2, y, 1) if s % 2 else None),
     )
-    attn = remote_attention(after(where, w_far), frame_counts, query, kv_remote, o, m, l)
+    attn = remote_attention(where, frame_counts, query, kv_remote, o, m, l)
 
     def goal(s, y, k):
         if k == 0:
@@ -598,6 +615,8 @@
     same = route(attn, target=lambda s, y, k: None if s % 2 == 0 and k == 1 else goal(s, y, k))
     cross = route(attn, target=lambda s, y, k: goal(s, 1 - y, k))
     twin_attn = twin(attn)
+    w_far_twin = twin(columns_of_twin(after(where, attn), w_far))
+    w_twin = twin(after(twin_mine, attn))
     weight, gate = tail_inputs(where, mod_rows, out_weight, w_twin, w_far, w_far_twin)
     same, cross, residual, _ = lax.optimization_barrier((same, cross, residual, weight))
     partial = first_out(where, same, cross, attn, weight)

time: 86.8 us -> 83.2 us (0.959)
  starting transfers between devices: 28.8 us -> 26.1 us
  waiting for transfers between devices: 13.9 us -> 13 us
    ppermute x15, starting transfers between devices: 28.8 us -> 26.1 us  [routed(): return lax.ppermute(array, BOTH, pairs)]
    ppermute x15, waiting for transfers between devices: 13.9 us -> 13 us  [routed(): return lax.ppermute(array, BOTH, pairs)]
  transfers between devices with their start and end apart: 15 -> 15, of which waited for: 4 -> 5; matrix products, arithmetic and copies ran while one was open for 1% -> 1% of each run, Pallas kernels for 26% -> 28%
where the time goes in v6:
time: 83.2 us; the launch traced here: 82.2 us
  starting transfers between devices  26.1 us (31%)
  Pallas kernels  25.2 us (30%)
  blocking collectives  17.1 us (21%)
  waiting for transfers between devices  13 us (16%)
    ppermute x15, starting transfers between devices, routed(): return lax.ppermute(array, BOTH, pairs)  26.1 us
    all_to_all x1, blocking collectives, on_device(): mod_rows = lax.all_to_all(payload, 'queue', 0, 0, tiled=True)[:, 0, :]  17.1 us
    ppermute x15, waiting for transfers between devices, routed(): return lax.ppermute(array, BOTH, pairs)  13 us
    pallas_call x1, Pallas kernels, keys_values(): pl.pallas_call(kv_kernel, out_shape=(near_out((rows, 2 * each)), near_out...  5.96 us
    pallas_call x1, Pallas kernels, local_attention(): pl.pallas_call(local_kernel, out_shape=(part,) * 3, in_specs=[smem_spec()...  4.69 us
    pallas_call x1, Pallas kernels, remote_attention(): pl.pallas_call(remote_kernel, out_shape=near_out((span, 3 * PAIR)), in_sp...  3.75 us
    pallas_call x1, Pallas kernels, slices(): pl.pallas_call(slices_kernel, out_shape=(near_out((rows // 2, width)), ne...  2.32 us
    pallas_call x1, Pallas kernels, last_out(): pl.pallas_call(last_out_kernel, out_shape=jax.ShapeDtypeStruct((span, sha...  2.22 us
  transfers between devices with their start and end apart: 15, of which 5 were waited for; matrix products, arithmetic and copies ran while one was open for 1% of the time, Pallas kernels for 28%

profile of v6, /device:TPU:111, one launch (start us, length us, event | category | flops | bytes accessed | tf_op | source)
XLA Modules:
  0.0 82.2 jit_solution(8535550856420666687)
XLA Ops:
  0.8 2.3 %shard_map.74 = (bf16[256,3072]{1,0:T(8,128)(2,1)S(1)}, bf16[384,1536]{1,0:T(8,128)(2,1)S(1)}) custom-call(s32[7]{0:T(128)S(1)} %stack.35.where_ref, bf16[512,3072]{1,0:T(8,128)(2,1)} %hidden.3, bf16[384,3072]{1,0:T(8,128)(2,1)} %out_weight.5), custom_call_target="tpu_custom_call" | custom-call | bytes 4194304 | tf_op jit(solution)/shard_map/pallas_call | solution.py:100
  3.1 1.4 %collective-permute-start = (bf16[256,3072]{1,0:T(8,128)(2,1)S(1)}, bf16[256,3072]{1,0:T(8,128)(2,1)S(1)}, u32[]{:S(2)}, u32[]{:S(2)}) collective-permute-start(bf16[256,3072]{1,0:T(8,128)(2,1)S(1)} %get-tuple-element.28), channel_id=1, source_target_pairs={{0,4},{1,7},{2,6},{3,5},{4,0},{5,3},{6,2},{7,1},{8,12},{9,15},{10,... | collective-permute-start | bytes 4718600 | tf_op jit(solution)/shard_map/ppermute | solution.py:35
  4.9 0.8 shard_map.73
  5.7 17.1 %all_to_all.5 = f32[64,1,384]{2,1,0:T(1,128)S(1)} all-to-all(f32[64,1,384]{2,1,0:T(1,128)S(1)} %shard_map.73), channel_id=1, replica_groups=mesh['queue'=64,'heads'=4] {'queue'}, dimensions={0} | all-to-all | bytes 196608 | tf_op jit(solution)/shard_map/all_to_all | solution.py:590
  22.8 2.0 %collective-permute-start.1 = (bf16[256,3072]{1,0:T(8,128)(2,1)S(1)}, bf16[256,3072]{1,0:T(8,128)(2,1)S(1)}, u32[]{:S(2)}, u32[]{:S(2)}) collective-permute-start(bf16[256,3072]{1,0:T(8,128)(2,1)S(1)} %collective-permute-done.second), channel_id=1, source_target_pairs={{0,1},{1,0},{2,3},{3,2},{4,5},{5,4},{6,7},{7,6},{8,9},{9,8},{10,11... | collective-permute-start | bytes 4718600 | tf_op jit(solution)/shard_map/ppermute | solution.py:35
  24.8 1.3 %collective-permute-start.10 = (bf16[384,1536]{1,0:T(8,128)(2,1)S(1)}, bf16[384,1536]{1,0:T(8,128)(2,1)S(1)}, u32[]{:S(2)}, u32[]{:S(2)}) collective-permute-start(bf16[384,1536]{1,0:T(8,128)(2,1)S(1)} %get-tuple-element.44), channel_id=1, source_target_pairs={{0,6},{1,7},{2,4},{3,5},{4,2},{5,3},{6,0},{7,1},{8,14},{9,15},{10,... | collective-permute-start | bytes 3538952 | tf_op jit(solution)/shard_map/ppermute | solution.py:35
  26.1 1.7 %collective-permute-done.1.first = bf16[256,3072]{1,0:T(8,128)(2,1)S(1)} collective-permute-done((bf16[256,3072]{1,0:T(8,128)(2,1)S(1)}, bf16[256,3072]{1,0:T(8,128)(2,1)S(1)}, u32[]{:S(2)}, u32[]{:S(2)}) %collective-permute-start.1) | collective-permute-done | bytes 1572896 | tf_op jit(solution)/shard_map/ppermute | solution.py:35
  27.8 6.0 %shard_map.75 = (bf16[512,768]{1,0:T(8,128)(2,1)S(1)}, bf16[512,384]{1,0:T(8,128)(2,1)S(1)}, bf16[512,384]{1,0:T(8,128)(2,1)S(1)}, bf16[512,3072]{1,0:T(8,128)(2...) custom-call(s32[7]{0:T(128)S(1)} %stack.35.where_ref, ...), custom_call_target="tpu_custom_call" | custom-call | flops 1 | bytes 1 | tf_op jit(solution)/shard_map/pallas_call | solution.py:242
  33.8 3.5 %collective-permute-start.3 = (bf16[512,768]{1,0:T(8,128)(2,1)S(1)}, bf16[512,768]{1,0:T(8,128)(2,1)S(1)}, u32[]{:S(2)}, u32[]{:S(2)}) collective-permute-start(bf16[512,768]{1,0:T(8,128)(2,1)S(1)} %get-tuple-element.31.own_ref), channel_id=1, source_target_pairs={{1,8},{3,10},{4,13},{6,15},{8,1},{9,16},{10,3},{11,18},{12,21},{13... | collective-permute-start | bytes 2359304 | tf_op jit(solution)/shard_map/ppermute | solution.py:35
  37.3 1.6 %collective-permute-start.4 = (bf16[512,384]{1,0:T(8,128)(2,1)S(1)}, bf16[512,384]{1,0:T(8,128)(2,1)S(1)}, u32[]{:S(2)}, u32[]{:S(2)}) collective-permute-start(bf16[512,384]{1,0:T(8,128)(2,1)S(1)} %get-tuple-element.34), channel_id=1, source_target_pairs={{0,1},{1,0},{2,3},{3,2},{4,5},{5,4},{6,7},{7,6},{8,9},{9,8},{10,11... | collective-permute-start | bytes 1179656 | tf_op jit(solution)/shard_map/ppermute | solution.py:35
  39.2 1.8 %shard_map.76.q_ref = bf16[512,384]{1,0:T(8,128)(2,1)S(1)} custom-call(bf16[512,3072]{1,0:T(8,128)(2,1)S(1)} %get-tuple-element.32.normed, bf16[3072,384]{1,0:T(8,128)(2,1)S(1)} %get-tuple-element.33.weight), custom_call_target="tpu_custom_call" | custom-call | flops 1 | bytes 1 | tf_op jit(solution)/shard_map/pallas_call | solution.py:272
  41.1 4.7 %shard_map.77 = (f32[512,384]{1,0:T(8,128)S(1)}, f32[512,384]{1,0:T(8,128)S(1)}, f32[512,384]{1,0:T(8,128)S(1)}) custom-call(s32[7]{0:T(128)S(1)} %stack.35.where_ref, s32[64]{0:T(128)S(1)} %copy-done.1, bf16[512,384]{1,0:T(8,128)(2,1)S(1)} %shard_map.76.q_ref, bf16[512,768]{1,0:T(8,128)(2,1)S(1)} %get-tuple-element.31.own_ref, ...), custom_call_target="tpu_custom_call" | custom-call | flops 1 | bytes 1 | tf_op jit(solution)/shard_map/pallas_call | solution.py:382
  45.8 1.9 %collective-permute-start.8 = (bf16[512,768]{1,0:T(8,128)(2,1)S(1)}, bf16[512,768]{1,0:T(8,128)(2,1)S(1)}, u32[]{:S(2)}, u32[]{:S(2)}) collective-permute-start(bf16[512,768]{1,0:T(8,128)(2,1)S(1)} %get-tuple-element.40.kept), channel_id=1, source_target_pairs={{4,0},{6,2},{8,4},{10,6},{12,8},{13,5},{14,10},{15,7},{16,12},{18,... | collective-permute-start | bytes 2359304 | tf_op jit(solution)/shard_map/ppermute | solution.py:35
  47.7 3.7 %shard_map.78.held = bf16[512,384]{1,0:T(8,128)(2,1)S(1)} custom-call(s32[7]{0:T(128)S(1)} %stack.35.where_ref, s32[64]{0:T(128)S(1)} %copy-done.1, bf16[512,384]{1,0:T(8,128)(2,1)S(1)} %shard_map.76.q_ref, bf16[512,768]{1,0:T(8,128)(2,1)S(1)} %collective-permute-done.3.kv_ref, f32[512,384]{1,0:T(8,128)S(1)} %get-tuple-element.36.o_ref, ...), custom_call_target="tpu_custom_call" | custom-call | flops 1 | bytes 1 | tf_op jit(solution)/shard_map/pallas_call | solution.py:424
  51.5 0.9 %collective-permute-done.10.source.w_far = bf16[384,1536]{1,0:T(8,128)(2,1)S(1)} collective-permute-done((bf16[384,1536]{1,0:T(8,128)(2,1)S(1)}, bf16[384,1536]{1,0:T(8,128)(2,1)S(1)}, u32[]{:S(2)}, u32[]{:S(2)}) %collective-permute-start.10) | collective-permute-done | bytes 1179680 | tf_op jit(solution)/shard_map/ppermute | solution.py:35
  53.0 3.2 %collective-permute-start.11 = (bf16[384,768]{1,0:T(8,128)(2,1)S(1)}, bf16[384,768]{1,0:T(8,128)(2,1)S(1)}, u32[]{:S(2)}, u32[]{:S(2)}) collective-permute-start(bf16[384,768]{1,0:T(8,128)(2,1)S(1)} %shard_map.79), channel_id=1, source_target_pairs={{0,1},{1,0},{2,3},{3,2},{4,5},{5,4},{6,7},{7,6},{8,9},{9,8},{10,11... | collective-permute-start | bytes 1769480 | tf_op jit(solution)/shard_map/ppermute | solution.py:35
  56.2 3.2 %collective-permute-start.7 = (bf16[512,384]{1,0:T(8,128)(2,1)S(1)}, bf16[512,384]{1,0:T(8,128)(2,1)S(1)}, u32[]{:S(2)}, u32[]{:S(2)}) collective-permute-start(bf16[512,384]{1,0:T(8,128)(2,1)S(1)} %shard_map.78.held), channel_id=1, source_target_pairs={{1,3},{3,1},{4,2},{6,0},{8,6},{9,11},{10,4},{11,9},{12,10},{13,7},... | collective-permute-start | bytes 1179656 | tf_op jit(solution)/shard_map/ppermute | solution.py:35
  59.4 2.2 %collective-permute-start.6 = (bf16[512,384]{1,0:T(8,128)(2,1)S(1)}, bf16[512,384]{1,0:T(8,128)(2,1)S(1)}, u32[]{:S(2)}, u32[]{:S(2)}) collective-permute-start(bf16[512,384]{1,0:T(8,128)(2,1)S(1)} %shard_map.78.held), channel_id=1, source_target_pairs={{4,0},{6,2},{8,4},{10,6},{12,8},{13,5},{14,10},{15,7},{16,12},{18,... | collective-permute-start | bytes 1179656 | tf_op jit(solution)/shard_map/ppermute | solution.py:35
  61.6 1.7 %collective-permute-start.14 = (bf16[512,384]{1,0:T(8,128)(2,1)S(1)}, bf16[512,384]{1,0:T(8,128)(2,1)S(1)}, u32[]{:S(2)}, u32[]{:S(2)}) collective-permute-start(bf16[512,384]{1,0:T(8,128)(2,1)S(1)} %shard_map.78.held), channel_id=1, source_target_pairs={{0,1},{1,0},{2,3},{3,2},{4,5},{5,4},{6,7},{7,6},{8,9},{9,8},{10,11... | collective-permute-start | bytes 1179656 | tf_op jit(solution)/shard_map/ppermute | solution.py:35
  63.3 1.7 %shard_map.80 = (bf16[1536,768]{1,0:T(8,128)(2,1)S(1)}, f32[1,768]{1,0:T(1,128)S(1)}) custom-call(s32[7]{0:T(128)S(1)} %stack.35.where_ref, f32[64,384]{1,0:T(8,128)S(1)} %bitcast.12, bf16[384,3072]{1,0:T(8,128)(2,1)} %out_weight.5, bf16[384,768]{1,0:T(8,128)(2,1)S(1)} %collective-permute-done.9.w_twin, ...), custom_call_target="tpu_custom_call" | custom-call | flops 1 | bytes 1 | tf_op jit(solution)/shard_map/pallas_call | solution.py:485
  65.0 9.0 %collective-permute-done.7.cross = bf16[512,384]{1,0:T(8,128)(2,1)S(1)} collective-permute-done((bf16[512,384]{1,0:T(8,128)(2,1)S(1)}, bf16[512,384]{1,0:T(8,128)(2,1)S(1)}, u32[]{:S(2)}, u32[]{:S(2)}) %collective-permute-start.7) | collective-permute-done | bytes 393248 | tf_op jit(solution)/shard_map/ppermute | solution.py:35
  74.8 3.1 %collective-permute-start.12 = (bf16[512,384]{1,0:T(8,128)(2,1)S(1)}, bf16[512,384]{1,0:T(8,128)(2,1)S(1)}, u32[]{:S(2)}, u32[]{:S(2)}) collective-permute-start(bf16[512,384]{1,0:T(8,128)(2,1)S(1)} %collective-permute-done.6.same), channel_id=1, source_target_pairs={{0,1},{1,0},{2,3},{3,2},{4,5},{5,4},{6,7},{7,6},{8,9},{9,8},{10,11... | collective-permute-start | bytes 1179656 | tf_op jit(solution)/shard_map/ppermute | solution.py:35
  77.9 1.3 %shard_map.81.partial = f32[512,768]{1,0:T(8,128)S(1)} custom-call(s32[7]{0:T(128)S(1)} %stack.35.where_ref, bf16[512,384]{1,0:T(8,128)(2,1)S(1)} %collective-permute-done.6.same, bf16[512,384]{1,0:T(8,128)(2,1)S(1)} %collective-permute-done.7.cross, bf16[512,384]{1,0:T(8,128)(2,1)S(1)} %shard_map.78.held, bf16[1536,768]{1,0:T(8,128)(2,1)S(1)} %get-tuple-element.46.weight), custom_call_target="tpu_custom_call" | custom-call | flops 1 | bytes 1 | tf_op jit(solution)/shard_map/pallas_call | solution.py:504
  79.8 2.2 %shard_map.82 = bf16[512,768]{1,0:T(8,128)(2,1)} custom-call(s32[7]{0:T(128)S(1)} %stack.35.where_ref, bf16[512,384]{1,0:T(8,128)(2,1)S(1)} %collective-permute-done.12.same, bf16[512,384]{1,0:T(8,128)(2,1)S(1)} %collective-permute-done.13.cross, bf16[512,384]{1,0:T(8,128)(2,1)S(1)} %collective-permute-done.14.held, ...), custom_call_target="tpu_custom_call" | custom-call | flops 1 | bytes 1 | tf_op jit(solution)/shard_map/pallas_call | solution.py:555
  (29 shorter events, 3.5 us)
Async XLA Ops:
  0.0 27.8 %collective-permute-start.2 = (bf16[3,3072,384]{2,1,0:T(8,128)(2,1)}, bf16[3,3072,384]{2,1,0:T(8,128)(2,1)}, u32[]{:S(2)}, u32[]{:S(2)}) collective-permute-start(bf16[3,3072,384]{2,1,0:T(8,128)(2,1)} %own_weight.1), channel_id=1, source_target_pairs={{0,1},{1,0},{2,3},{3,2},{4,5},{5,4},{6,7},{7,6},{8,9},{9,8},{10,11... | collective-permute-start | bytes 21233672 | tf_op jit(solution)/shard_map/ppermute | solution.py:35
  0.8 3.7 %copy-start.2 = (s32[64]{0:T(128)S(1)}, s32[64]{0:T(128)}, u32[]{:S(2)}) copy-start(s32[64]{0:T(128)} %param.8) | copy-start | bytes 772
  0.8 4.1 %copy-start = (bf16[512,144]{0,1:T(8,128)(2,1)S(1)}, bf16[512,144]{0,1:T(8,128)(2,1)}, u32[]{:S(2)}) copy-start(bf16[512,144]{0,1:T(8,128)(2,1)} %param.10) | copy-start | bytes 442372
  3.1 19.7 %collective-permute-start = (bf16[256,3072]{1,0:T(8,128)(2,1)S(1)}, bf16[256,3072]{1,0:T(8,128)(2,1)S(1)}, u32[]{:S(2)}, u32[]{:S(2)}) collective-permute-start(bf16[256,3072]{1,0:T(8,128)(2,1)S(1)} %get-tuple-element.28), channel_id=1, source_target_pairs={{0,4},{1,7},{2,6},{3,5},{4,0},{5,3},{6,2},{7,1},{8,12},{9,15},{10,... | collective-permute-start | bytes 4718600 | tf_op jit(solution)/shard_map/ppermute | solution.py:35
  22.8 5.0 %collective-permute-start.1 = (bf16[256,3072]{1,0:T(8,128)(2,1)S(1)}, bf16[256,3072]{1,0:T(8,128)(2,1)S(1)}, u32[]{:S(2)}, u32[]{:S(2)}) collective-permute-start(bf16[256,3072]{1,0:T(8,128)(2,1)S(1)} %collective-permute-done.second), channel_id=1, source_target_pairs={{0,1},{1,0},{2,3},{3,2},{4,5},{5,4},{6,7},{7,6},{8,9},{9,8},{10,11... | collective-permute-start | bytes 4718600 | tf_op jit(solution)/shard_map/ppermute | solution.py:35
  24.8 27.5 %collective-permute-start.10 = (bf16[384,1536]{1,0:T(8,128)(2,1)S(1)}, bf16[384,1536]{1,0:T(8,128)(2,1)S(1)}, u32[]{:S(2)}, u32[]{:S(2)}) collective-permute-start(bf16[384,1536]{1,0:T(8,128)(2,1)S(1)} %get-tuple-element.44), channel_id=1, source_target_pairs={{0,6},{1,7},{2,4},{3,5},{4,2},{5,3},{6,0},{7,1},{8,14},{9,15},{10,... | collective-permute-start | bytes 3538952 | tf_op jit(solution)/shard_map/ppermute | solution.py:35
  33.8 13.9 %collective-permute-start.3 = (bf16[512,768]{1,0:T(8,128)(2,1)S(1)}, bf16[512,768]{1,0:T(8,128)(2,1)S(1)}, u32[]{:S(2)}, u32[]{:S(2)}) collective-permute-start(bf16[512,768]{1,0:T(8,128)(2,1)S(1)} %get-tuple-element.31.own_ref), channel_id=1, source_target_pairs={{1,8},{3,10},{4,13},{6,15},{8,1},{9,16},{10,3},{11,18},{12,21},{13... | collective-permute-start | bytes 2359304 | tf_op jit(solution)/shard_map/ppermute | solution.py:35
  37.3 3.7 %collective-permute-start.4 = (bf16[512,384]{1,0:T(8,128)(2,1)S(1)}, bf16[512,384]{1,0:T(8,128)(2,1)S(1)}, u32[]{:S(2)}, u32[]{:S(2)}) collective-permute-start(bf16[512,384]{1,0:T(8,128)(2,1)S(1)} %get-tuple-element.34), channel_id=1, source_target_pairs={{0,1},{1,0},{2,3},{3,2},{4,5},{5,4},{6,7},{7,6},{8,9},{9,8},{10,11... | collective-permute-start | bytes 1179656 | tf_op jit(solution)/shard_map/ppermute | solution.py:35
  39.0 2.1 %collective-permute-start.5 = (bf16[512,384]{1,0:T(8,128)(2,1)S(1)}, bf16[512,384]{1,0:T(8,128)(2,1)S(1)}, u32[]{:S(2)}, u32[]{:S(2)}) collective-permute-start(bf16[512,384]{1,0:T(8,128)(2,1)S(1)} %get-tuple-element.35), channel_id=1, source_target_pairs={{0,1},{1,0},{2,3},{3,2},{4,5},{5,4},{6,7},{7,6},{8,9},{9,8},{10,11... | collective-permute-start | bytes 1179656 | tf_op jit(solution)/shard_map/ppermute | solution.py:35
  39.2 1.8 %copy-start.1 = (s32[64]{0:T(128)S(1)}, s32[64]{0:T(128)}, u32[]{:S(2)}) copy-start(s32[64]{0:T(128)} %counts_ref.3) | copy-start | bytes 772
  45.8 29.0 %collective-permute-start.8 = (bf16[512,768]{1,0:T(8,128)(2,1)S(1)}, bf16[512,768]{1,0:T(8,128)(2,1)S(1)}, u32[]{:S(2)}, u32[]{:S(2)}) collective-permute-start(bf16[512,768]{1,0:T(8,128)(2,1)S(1)} %get-tuple-element.40.kept), channel_id=1, source_target_pairs={{4,0},{6,2},{8,4},{10,6},{12,8},{13,5},{14,10},{15,7},{16,12},{18,... | collective-permute-start | bytes 2359304 | tf_op jit(solution)/shard_map/ppermute | solution.py:35
  53.0 8.6 %collective-permute-start.11 = (bf16[384,768]{1,0:T(8,128)(2,1)S(1)}, bf16[384,768]{1,0:T(8,128)(2,1)S(1)}, u32[]{:S(2)}, u32[]{:S(2)}) collective-permute-start(bf16[384,768]{1,0:T(8,128)(2,1)S(1)} %shard_map.79), channel_id=1, source_target_pairs={{0,1},{1,0},{2,3},{3,2},{4,5},{5,4},{6,7},{7,6},{8,9},{9,8},{10,11... | collective-permute-start | bytes 1769480 | tf_op jit(solution)/shard_map/ppermute | solution.py:35
  56.1 7.2 %collective-permute-start.9 = (bf16[384,768]{1,0:T(8,128)(2,1)S(1)}, bf16[384,768]{1,0:T(8,128)(2,1)S(1)}, u32[]{:S(2)}, u32[]{:S(2)}) collective-permute-start(bf16[384,768]{1,0:T(8,128)(2,1)S(1)} %get-tuple-element.42), channel_id=1, source_target_pairs={{0,1},{1,0},{2,3},{3,2},{4,5},{5,4},{6,7},{7,6},{8,9},{9,8},{10,11... | collective-permute-start | bytes 1769480 | tf_op jit(solution)/shard_map/ppermute | solution.py:35
  56.2 17.8 %collective-permute-start.7 = (bf16[512,384]{1,0:T(8,128)(2,1)S(1)}, bf16[512,384]{1,0:T(8,128)(2,1)S(1)}, u32[]{:S(2)}, u32[]{:S(2)}) collective-permute-start(bf16[512,384]{1,0:T(8,128)(2,1)S(1)} %shard_map.78.held), channel_id=1, source_target_pairs={{1,3},{3,1},{4,2},{6,0},{8,6},{9,11},{10,4},{11,9},{12,10},{13,7},... | collective-permute-start | bytes 1179656 | tf_op jit(solution)/shard_map/ppermute | solution.py:35
  59.4 15.4 %collective-permute-start.6 = (bf16[512,384]{1,0:T(8,128)(2,1)S(1)}, bf16[512,384]{1,0:T(8,128)(2,1)S(1)}, u32[]{:S(2)}, u32[]{:S(2)}) collective-permute-start(bf16[512,384]{1,0:T(8,128)(2,1)S(1)} %shard_map.78.held), channel_id=1, source_target_pairs={{4,0},{6,2},{8,4},{10,6},{12,8},{13,5},{14,10},{15,7},{16,12},{18,... | collective-permute-start | bytes 1179656 | tf_op jit(solution)/shard_map/ppermute | solution.py:35
  61.6 17.6 %collective-permute-start.14 = (bf16[512,384]{1,0:T(8,128)(2,1)S(1)}, bf16[512,384]{1,0:T(8,128)(2,1)S(1)}, u32[]{:S(2)}, u32[]{:S(2)}) collective-permute-start(bf16[512,384]{1,0:T(8,128)(2,1)S(1)} %shard_map.78.held), channel_id=1, source_target_pairs={{0,1},{1,0},{2,3},{3,2},{4,5},{5,4},{6,7},{7,6},{8,9},{9,8},{10,11... | collective-permute-start | bytes 1179656 | tf_op jit(solution)/shard_map/ppermute | solution.py:35
  74.8 4.4 %collective-permute-start.12 = (bf16[512,384]{1,0:T(8,128)(2,1)S(1)}, bf16[512,384]{1,0:T(8,128)(2,1)S(1)}, u32[]{:S(2)}, u32[]{:S(2)}) collective-permute-start(bf16[512,384]{1,0:T(8,128)(2,1)S(1)} %collective-permute-done.6.same), channel_id=1, source_target_pairs={{0,1},{1,0},{2,3},{3,2},{4,5},{5,4},{6,7},{7,6},{8,9},{9,8},{10,11... | collective-permute-start | bytes 1179656 | tf_op jit(solution)/shard_map/ppermute | solution.py:35
  77.9 1.9 %collective-permute-start.13 = (bf16[512,384]{1,0:T(8,128)(2,1)S(1)}, bf16[512,384]{1,0:T(8,128)(2,1)S(1)}, u32[]{:S(2)}, u32[]{:S(2)}) collective-permute-start(bf16[512,384]{1,0:T(8,128)(2,1)S(1)} %collective-permute-done.7.cross), channel_id=1, source_target_pairs={{0,1},{1,0},{2,3},{3,2},{4,5},{5,4},{6,7},{7,6},{8,9},{9,8},{10,11... | collective-permute-start | bytes 1179656 | tf_op jit(solution)/shard_map/ppermute | solution.py:35

commit v7 on v6

--- a/solution.py
+++ b/solution.py
@@ -49,6 +49,11 @@
     ]
 
 
+def place():
+    slot, member = lax.axis_index("queue"), lax.axis_index("heads")
+    return member, member & 1, member >> 1, slot & 1, slot
+
+
 def any_spec():
     return pl.BlockSpec(memory_space=pl.ANY)
 
@@ -81,8 +86,8 @@
     return pl.ds(pl.multiple_of(index * size, size), size)
 
 
-def slices_kernel(where_ref, hidden, out_weight, mine, far_out, sems):
-    core, y_hi = where_ref[1], where_ref[2]
+def slices_kernel(hidden, out_weight, mine, far_out, sems):
+    _, core, y_hi, _, _ = place()
     half, width = mine.shape[0], far_out.shape[1]
     copies = (
         copies_of(hidden.at[lanes_at(core, half), :], mine, sems, 4)
@@ -94,7 +99,7 @@
         copy.wait()
 
 
-def slices(where, hidden, out_weight, members):
+def slices(hidden, out_weight, members):
     rows, width = hidden.shape
     share, depth = width // members, out_weight.shape[0]
     return pl.pallas_call(
@@ -103,18 +108,18 @@
             near_out((rows // 2, width)),
             near_out((depth, 2 * share)),
         ),
-        in_specs=[smem_spec(), any_spec(), any_spec()],
+        in_specs=[any_spec(), any_spec()],
         out_specs=(vmem_spec(),) * 2,
         scratch_shapes=[pltpu.SemaphoreType.DMA((8,))],
         compiler_params=pltpu.CompilerParams(vmem_limit_bytes=2 * MIB),
         cost_estimate=cost(0, 4 * MIB),
-    )(where, far(hidden), far(out_weight))
+    )(far(hidden), far(out_weight))
 
 
 ROW = 384
 
 
-def modulate_kernel(where_ref, emb_ref, mod_ref, payload, rows_ref):
+def modulate_kernel(emb_ref, mod_ref, payload, rows_ref):
     rows_ref[...] = jnp.zeros_like(rows_ref)
     columns = mod_ref.shape[0]
     rows_ref[:, :columns] = lax.dot_general(
@@ -125,21 +130,21 @@
     even = lax.broadcasted_iota(jnp.int32, rows.shape, 0) % 2 == 0
     following = pltpu.roll(rows, slots - 1, 0)
     partner = jnp.where(even, following, pltpu.roll(rows, 1, 0))
-    joined = jnp.where(where_ref[1] == 0, rows, partner) + pltpu.roll(following, columns, 1)
+    joined = jnp.where(place()[1] == 0, rows, partner) + pltpu.roll(following, columns, 1)
     for slot in range(slots):
         payload[slot] = joined[slot : slot + 1, :]
 
 
-def modulate(where, emb, mod_weight):
+def modulate(emb, mod_weight):
     return pl.pallas_call(
         modulate_kernel,
         out_shape=jax.ShapeDtypeStruct((emb.shape[0], 1, ROW), jnp.float32),
-        in_specs=[smem_spec(), vmem_spec(), vmem_spec()],
+        in_specs=[vmem_spec(), vmem_spec()],
         out_specs=vmem_spec(),
         scratch_shapes=[pltpu.VMEM((emb.shape[0], ROW), jnp.float32)],
         compiler_params=pltpu.CompilerParams(vmem_limit_bytes=2 * MIB),
         cost_estimate=cost(10**7, MIB),
-    )(where, emb, mod_weight.T)
+    )(emb, mod_weight.T)
 
 
 NORM_ROWS = 16
@@ -168,11 +173,11 @@
 
 
 def kv_kernel(
-    where_ref, rows_ref, hidden, first, second, own_weight, twin_weight, out_weight, kv_ref, k_ref, v_ref, states_ref, q_weight,
-    twin_out, share_ref,
+    counts_ref, rows_ref, hidden, first, second, own_weight, twin_weight, out_weight, kv_ref, k_ref, v_ref, states_ref, q_weight,
+    twin_out, share_ref, dead_ref,
     flat, weight, x_sems, w_sems,
 ):
-    core, parity = where_ref[1], where_ref[4]
+    member, core, y_hi, parity, slot = place()
     rows, width = states_ref.shape
     half = rows // 2
     each = q_weight.shape[1]
@@ -201,9 +206,13 @@
     start(core == 1, from_pair)
     start(core == parity, sum(weights_from(own_weight)[:2], []))
     start(core != parity, sum(weights_from(twin_weight)[:2], []))
-    beside = where_ref[2] * 2 + 1 - core
+    beside = y_hi * 2 + 1 - core
     asides = copies_of(out_weight.at[:, lanes_at(beside, twin_out.shape[1])], twin_out, w_sems, 2, 6)
     spread(rows_ref, 0, flat)
+    step = 1 - 2 * parity
+    mine = slot + core * step
+    for index, stretch in enumerate((mine, slot + (1 - core) * step, jnp.where(core == 0, slot - step, slot + 2 * step))):
+        dead_ref[pl.ds(index * rows, rows), :] = dead_rows(rows, count_at(counts_ref, stretch))
     scale, shift = 1.0 + flat[:, width : 2 * width], flat[:, :width]
 
     def normalise(first_row, count):
@@ -215,12 +224,12 @@
             var = jnp.mean(centred * centred, axis=1, keepdims=True)
             states_ref[block, :] = (centred * lax.rsqrt(var + 1e-05) * scale + shift).astype(jnp.bfloat16)
 
-    step = rows // len(from_own)
+    chunk = rows // len(from_own)
     for index, copy in enumerate(from_own):
         copy.wait()
-        block = pl.ds(index * step, step)
-        share_ref[block, :] = states_ref[block, lanes_at(where_ref[0], share_ref.shape[1])]
-        normalise(index * step, step)
+        block = pl.ds(index * chunk, chunk)
+        share_ref[block, :] = states_ref[block, lanes_at(member, share_ref.shape[1])]
+        normalise(index * chunk, chunk)
     keys, values, queries = weights_from(own_weight)
     for copy in keys + values:
         copy.wait()
@@ -236,7 +245,7 @@
         copy.wait()
 
 
-def keys_values(where, mod_rows, hidden, first, second, own_weight, twin_weight, out_weight):
+def keys_values(counts, mod_rows, hidden, first, second, own_weight, twin_weight, out_weight):
     rows, width = hidden.shape
     each = own_weight.shape[2]
     return pl.pallas_call(
@@ -249,9 +258,10 @@
             near_out((width, each)),
             near_out((out_weight.shape[0], width // 4)),
             near_out((rows, width // 4)),
+            near_out((3 * rows, PAIR)),
         ),
         in_specs=[smem_spec(), vmem_spec()] + [any_spec()] * 6,
-        out_specs=(vmem_spec(),) * 7,
+        out_specs=(vmem_spec(),) * 8,
         scratch_shapes=[
             pltpu.VMEM((1, 3 * width), jnp.float32),
             pltpu.VMEM((width, 2 * each), jnp.bfloat16),
@@ -260,7 +270,7 @@
         ],
         compiler_params=pltpu.CompilerParams(vmem_limit_bytes=24 * MIB),
         cost_estimate=cost(1, 1),
-    )(where, mod_rows, far(hidden), first, second, far(own_weight), twin_weight, far(out_weight))
+    )(counts, mod_rows, far(hidden), first, second, far(own_weight), twin_weight, far(out_weight))
 
 
 def query_kernel(normed, weight, query_ref):
@@ -345,14 +355,10 @@
     return slice(pair * PAIR, (pair + 1) * PAIR)
 
 
-def local_kernel(where_ref, counts_ref, q_ref, own_ref, k_twin, v_twin, o_ref, m_ref, l_ref):
+def local_kernel(dead_ref, q_ref, own_ref, k_twin, v_twin, o_ref, m_ref, l_ref):
     span = own_ref.shape[0]
     tile = 256
-    core, slot = where_ref[1], where_ref[6]
-    partner = slot + 1 - 2 * where_ref[4]
-    own_count = count_at(counts_ref, jnp.where(core == 0, slot, partner))
-    twin_count = count_at(counts_ref, jnp.where(core == 0, partner, slot))
-    dead = jnp.concatenate([dead_rows(span, own_count), dead_rows(span, twin_count)], axis=0)
+    dead = dead_ref[: 2 * span, :]
     pairs = [
         two_heads(
             jnp.concatenate([own_ref[:, pair_lanes(pair)], k_twin[:, pair_lanes(pair)]], axis=0),
@@ -376,26 +382,23 @@
     )
 
 
-def local_attention(where, counts, query, own, k_twin, v_twin):
+def local_attention(dead, query, own, k_twin, v_twin):
     span = query.shape[0]
     part = near_out((span, 3 * PAIR), jnp.float32)
     return pl.pallas_call(
         local_kernel,
         out_shape=(part,) * 3,
-        in_specs=[smem_spec()] * 2 + [vmem_spec()] * 4,
+        in_specs=[vmem_spec()] * 5,
         out_specs=(vmem_spec(),) * 3,
         compiler_params=pltpu.CompilerParams(vmem_limit_bytes=16 * MIB),
         cost_estimate=cost(1, 1),
-    )(where, counts, near(query), near(own), k_twin, v_twin)
-
-
-def remote_kernel(where_ref, counts_ref, q_ref, kv_ref, o_ref, m_ref, l_ref, piece_ref):
+    )(near(dead), near(query), near(own), k_twin, v_twin)
+
+
+def remote_kernel(dead_ref, q_ref, kv_ref, o_ref, m_ref, l_ref, piece_ref):
     span = kv_ref.shape[0]
     tile = 256
-    core, slot = where_ref[1], where_ref[6]
-    step = 1 - 2 * where_ref[4]
-    count = count_at(counts_ref, jnp.where(core == 0, slot - step, slot + 2 * step))
-    dead = dead_rows(span, count)
+    dead = dead_ref[2 * span :, :]
     pairs = [
         two_heads(kv_ref[:, pair_lanes(pair)], kv_ref[:, pair_lanes(3 + pair)], dead) for pair in range(3)
     ]
@@ -419,22 +422,22 @@
     )
 
 
-def remote_attention(where, counts, query, kv, o, m, l):
+def remote_attention(dead, query, kv, o, m, l):
     span = query.shape[0]
     return pl.pallas_call(
         remote_kernel,
         out_shape=near_out((span, 3 * PAIR)),
-        in_specs=[smem_spec()] * 2 + [vmem_spec()] * 5,
+        in_specs=[vmem_spec()] * 6,
         out_specs=vmem_spec(),
         compiler_params=pltpu.CompilerParams(vmem_limit_bytes=16 * MIB),
         cost_estimate=cost(1, 1),
-    )(where, counts, near(query), kv, near(o), near(m), near(l))
+    )(near(dead), near(query), kv, near(o), near(m), near(l))
 
 
 def tail_kernel(
-    where_ref, rows_ref, out_weight, w_twin, w_far, w_far_twin, gathered, gate, flat, sems,
+    rows_ref, out_weight, w_twin, w_far, w_far_twin, gathered, gate, flat, sems,
 ):
-    member, core, parity = where_ref[0], where_ref[1], where_ref[4]
+    member, core, _, parity, _ = place()
     share = gathered.shape[1]
     width = flat.shape[1] // 3
     block = out_weight.shape[0]
@@ -458,68 +461,70 @@
         copy.wait()
 
 
-def columns_kernel(where_ref, source, out, sems):
-    copies = copies_of(source.at[:, lanes_at(1 - where_ref[1], out.shape[1])], out, sems, 4)
+def columns_kernel(source, out, sems):
+    copies = copies_of(source.at[:, lanes_at(1 - place()[1], out.shape[1])], out, sems, 4)
     for copy in copies:
         copy.start()
     for copy in copies:
         copy.wait()
 
 
-def columns_of_twin(where, blocks):
+def columns_of_twin(blocks):
     rows, width = blocks.shape
     return pl.pallas_call(
         columns_kernel,
         out_shape=near_out((rows, width // 2)),
-        in_specs=[smem_spec(), any_spec()],
+        in_specs=[any_spec()],
         out_specs=vmem_spec(),
         scratch_shapes=[pltpu.SemaphoreType.DMA((4,))],
         compiler_params=pltpu.CompilerParams(vmem_limit_bytes=2 * MIB),
         cost_estimate=cost(1, 1),
-    )(where, blocks)
-
-
-def tail_inputs(where, mod_rows, out_weight, w_twin, w_far, w_far_twin):
+    )(blocks)
+
+
+def tail_inputs(mod_rows, out_weight, w_twin, w_far, w_far_twin):
     block, share = w_twin.shape
     width = out_weight.shape[1]
     return pl.pallas_call(
         tail_kernel,
         out_shape=(near_out((4 * block, share)), near_out((1, share), jnp.float32)),
-        in_specs=[smem_spec(), vmem_spec()] + [any_spec()] * 4,
+        in_specs=[vmem_spec()] + [any_spec()] * 4,
         out_specs=(vmem_spec(),) * 2,
         scratch_shapes=[pltpu.VMEM((1, 3 * width), jnp.float32), pltpu.SemaphoreType.DMA((8,))],
         compiler_params=pltpu.CompilerParams(vmem_limit_bytes=2 * MIB),
         cost_estimate=cost(1, 1),
-    )(where, mod_rows, far(out_weight), w_twin, w_far, w_far_twin)
-
-
-def first_out_kernel(where_ref, same, cross, held, weight, partial):
-    here = (where_ref[4] == 0) & (where_ref[1] == 1)
+    )(mod_rows, far(out_weight), w_twin, w_far, w_far_twin)
+
+
+def first_out_kernel(same, cross, held, weight, partial):
+    _, core, _, parity, _ = place()
+    here = (parity == 0) & (core == 1)
     attn = jnp.concatenate([jnp.where(here, held[...], same[...]), cross[...]], axis=1)
     partial[...] = jnp.dot(attn, weight[: attn.shape[1], :], preferred_element_type=jnp.float32)
 
 
-def first_out(where, same, cross, held, weight):
+def first_out(same, cross, held, weight):
     span, share = same.shape[0], weight.shape[1]
     return pl.pallas_call(
         first_out_kernel,
         out_shape=near_out((span, share), jnp.float32),
-        in_specs=[smem_spec()] + [vmem_spec()] * 4,
+        in_specs=[vmem_spec()] * 4,
         out_specs=vmem_spec(),
         compiler_params=pltpu.CompilerParams(vmem_limit_bytes=8 * MIB),
         cost_estimate=cost(1, 1),
-    )(where, same, cross, near(held), near(weight))
+    )(same, cross, near(held), near(weight))
 
 
 TILE = 128
 
 
 def last_out_kernel(
-    where_ref, same, cross, held, weight, partial, kept, residual, gate, fresh, out, ready, sems
+    same, cross, held, weight, partial, kept, residual, gate, fresh, out, ready, sems
 ):
-    here = (where_ref[4] == 0) & (where_ref[1] == 0)
-    holds = (where_ref[4] == 0) & (where_ref[1] == 1)
-    last = where_ref[5] == 1
+    _, core, _, parity, slot = place()
+    here = (parity == 0) & (core == 0)
+    holds = (parity == 0) & (core == 1)
+    last = slot == lax.axis_size("queue") - 1
     span = partial.shape[0]
     tiles = span // TILE
 
@@ -550,48 +555,38 @@
             copy.wait()
 
 
-def last_out(where, same, cross, held, weight, partial, kept, residual, gate, fresh):
+def last_out(same, cross, held, weight, partial, kept, residual, gate, fresh):
     span, share = partial.shape
     return pl.pallas_call(
         last_out_kernel,
         out_shape=jax.ShapeDtypeStruct((span, share), jnp.bfloat16),
-        in_specs=[smem_spec()] + [vmem_spec()] * 8 + [any_spec()],
+        in_specs=[vmem_spec()] * 8 + [any_spec()],
         out_specs=any_spec(),
         scratch_shapes=[pltpu.VMEM((span, share), jnp.bfloat16), pltpu.SemaphoreType.DMA((4,))],
         compiler_params=pltpu.CompilerParams(vmem_limit_bytes=8 * MIB),
         cost_estimate=cost(1, 1),
-    )(where, same, cross, held, near(weight), near(partial), near(kept), residual, near(gate), far(fresh))
+    )(same, cross, held, near(weight), near(partial), near(kept), residual, near(gate), far(fresh))
 
 
 def on_device(hidden, levels, frame_counts, mod_weight, qkv_weight, out_weight, fresh):
-    rows, width = hidden.shape
-    slot = lax.axis_index("queue")
     queue_len = lax.axis_size("queue")
-    member = lax.axis_index("heads")
     members = lax.axis_size("heads")
-    share = width // members
-    parity, core, y_hi = slot % 2, member % 2, member // 2
-    z_half = (slot // 8) % 2
-    half = rows // 2
     route = functools.partial(routed, queue_len=queue_len, members=members)
     twin = lambda a: route(a, target=lambda s, y, k: (s, y, 1 - k))
 
-    where = jnp.stack(
-        [member, core, y_hi, z_half, parity, (slot == queue_len - 1).astype(jnp.int32), slot]
-    ).astype(jnp.int32)
     after = lambda a, *b: lax.optimization_barrier((a, *b))[0]
     frame_counts = frame_counts.astype(jnp.int32)
 
     twin_weight = twin(qkv_weight)
-    mine, far_mine = slices(where, hidden, out_weight, members)
+    mine, far_mine = slices(hidden, out_weight, members)
     second = route(mine, target=lambda s, y, k: (s ^ 1, y ^ k, k))
 
-    payload = modulate(where, embed_levels(levels, mod_weight.shape[0]), mod_weight)
+    payload = modulate(embed_levels(levels, mod_weight.shape[0]), mod_weight)
     mod_rows = lax.all_to_all(payload, "queue", 0, 0, tiled=True)[:, 0, :]
 
     first = twin(after(second, mod_rows))
     w_far = route(after(far_mine, mod_rows), target=lambda s, y, k: (s ^ 1, 1 - y, k))
-    kv, k, v, normed, q_weight, twin_mine, share_states = keys_values(where, mod_rows, hidden, first, second, qkv_weight, twin_weight, out_weight)
+    kv, k, v, normed, q_weight, twin_mine, share_states, dead = keys_values(frame_counts, mod_rows, hidden, first, second, qkv_weight, twin_weight, out_weight)
 
     def remote_target(s, y, k):
         back = (s % 2 == 0) == (k == 0)
@@ -600,12 +595,12 @@
     kv_remote = route(kv, target=remote_target)
     k_twin, v_twin = twin(k), twin(v)
     query = queries(after(normed, kv), q_weight)
-    o, m, l = local_attention(where, frame_counts, query, kv, k_twin, v_twin)
+    o, m, l = local_attention(dead, query, kv, k_twin, v_twin)
     residual = route(
         after(share_states, o),
         target=lambda s, y, k: (s - 1, y, 0) if k == 0 else ((s - 2, y, 1) if s % 2 else None),
     )
-    attn = remote_attention(where, frame_counts, query, kv_remote, o, m, l)
+    attn = remote_attention(dead, query, kv_remote, o, m, l)
 
     def goal(s, y, k):
         if k == 0:
@@ -615,12 +610,12 @@
     same = route(attn, target=lambda s, y, k: None if s % 2 == 0 and k == 1 else goal(s, y, k))
     cross = route(attn, target=lambda s, y, k: goal(s, 1 - y, k))
     twin_attn = twin(attn)
-    w_far_twin = twin(columns_of_twin(after(where, attn), w_far))
+    w_far_twin = twin(columns_of_twin(after(w_far, attn)))
     w_twin = twin(after(twin_mine, attn))
-    weight, gate = tail_inputs(where, mod_rows, out_weight, w_twin, w_far, w_far_twin)
+    weight, gate = tail_inputs(mod_rows, out_weight, w_twin, w_far, w_far_twin)
     same, cross, residual, _ = lax.optimization_barrier((same, cross, residual, weight))
-    partial = first_out(where, same, cross, attn, weight)
-    return last_out(where, twin(same), twin(cross), twin_attn, weight, partial, share_states, residual, gate, fresh)
+    partial = first_out(same, cross, attn, weight)
+    return last_out(twin(same), twin(cross), twin_attn, weight, partial, share_states, residual, gate, fresh)
 
 
 def solution(mesh):

time: 83.2 us -> 81 us (0.974)
  Pallas kernels: 25.2 us -> 20.8 us
  waiting for transfers between devices: 13 us -> 15.4 us
    ppermute x15, waiting for transfers between devices: 13 us -> 15.4 us  [routed(): return lax.ppermute(array, BOTH, pairs)]
  transfers between devices with their start and end apart: 15 -> 15, of which waited for: 5 -> 8; matrix products, arithmetic and copies ran while one was open for 1% -> 0% of each run, Pallas kernels for 28% -> 24%
where the time goes in v7:
time: 81 us; the launch traced here: 80.3 us
  starting transfers between devices  26.3 us (32%)
  Pallas kernels  20.8 us (26%)
  blocking collectives  17.1 us (21%)
  waiting for transfers between devices  15.4 us (19%)
    ppermute x15, starting transfers between devices, routed(): return lax.ppermute(array, BOTH, pairs)  26.3 us
    all_to_all x1, blocking collectives, on_device(): mod_rows = lax.all_to_all(payload, 'queue', 0, 0, tiled=True)[:, 0, :]  17.1 us
    ppermute x15, waiting for transfers between devices, routed(): return lax.ppermute(array, BOTH, pairs)  15.4 us
    pallas_call x1, Pallas kernels, keys_values(): pl.pallas_call(kv_kernel, out_shape=(near_out((rows, 2 * each)), near_out...  6.07 us
    pallas_call x1, Pallas kernels, local_attention(): pl.pallas_call(local_kernel, out_shape=(part,) * 3, in_specs=[vmem_spec()...  4.2 us
    pallas_call x1, Pallas kernels, remote_attention(): pl.pallas_call(remote_kernel, out_shape=near_out((span, 3 * PAIR)), in_sp...  3.05 us
    pallas_call x1, Pallas kernels, queries(): pl.pallas_call(query_kernel, out_shape=near_out((normed.shape[0], weight....  1.79 us
    pallas_call x1, Pallas kernels, slices(): pl.pallas_call(slices_kernel, out_shape=(near_out((rows // 2, width)), ne...  1.77 us
  transfers between devices with their start and end apart: 15, of which 8 were waited for; matrix products, arithmetic and copies ran while one was open for 0% of the time, Pallas kernels for 24%

profile of v7, /device:TPU:111, one launch (start us, length us, event | category | flops | bytes accessed | tf_op | source)
XLA Modules:
  0.0 80.3 jit_solution(16160474631482536711)
XLA Ops:
  0.8 1.8 %shard_map.74 = (bf16[256,3072]{1,0:T(8,128)(2,1)S(1)}, bf16[384,1536]{1,0:T(8,128)(2,1)S(1)}) custom-call(bf16[512,3072]{1,0:T(8,128)(2,1)} %hidden.3, bf16[384,3072]{1,0:T(8,128)(2,1)} %out_weight.5), custom_call_target="tpu_custom_call" | custom-call | bytes 4194304 | tf_op jit(solution)/shard_map/pallas_call | solution.py:105
  2.5 1.4 %collective-permute-start = (bf16[256,3072]{1,0:T(8,128)(2,1)S(1)}, bf16[256,3072]{1,0:T(8,128)(2,1)S(1)}, u32[]{:S(2)}, u32[]{:S(2)}) collective-permute-start(bf16[256,3072]{1,0:T(8,128)(2,1)S(1)} %get-tuple-element.29), channel_id=1, source_target_pairs={{0,4},{1,7},{2,6},{3,5},{4,0},{5,3},{6,2},{7,1},{8,12},{9,15},{10,... | collective-permute-start | bytes 4718600 | tf_op jit(solution)/shard_map/ppermute | solution.py:35
  4.6 17.1 %all_to_all.5 = f32[64,1,384]{2,1,0:T(1,128)S(1)} all-to-all(f32[64,1,384]{2,1,0:T(1,128)S(1)} %shard_map.73), channel_id=1, replica_groups=mesh['queue'=64,'heads'=4] {'queue'}, dimensions={0} | all-to-all | bytes 196608 | tf_op jit(solution)/shard_map/all_to_all | solution.py:585
  22.2 2.1 %collective-permute-start.1 = (bf16[256,3072]{1,0:T(8,128)(2,1)S(1)}, bf16[256,3072]{1,0:T(8,128)(2,1)S(1)}, u32[]{:S(2)}, u32[]{:S(2)}) collective-permute-start(bf16[256,3072]{1,0:T(8,128)(2,1)S(1)} %collective-permute-done.second), channel_id=1, source_target_pairs={{0,1},{1,0},{2,3},{3,2},{4,5},{5,4},{6,7},{7,6},{8,9},{9,8},{10,11... | collective-permute-start | bytes 4718600 | tf_op jit(solution)/shard_map/ppermute | solution.py:35
  24.3 1.3 %collective-permute-start.10 = (bf16[384,1536]{1,0:T(8,128)(2,1)S(1)}, bf16[384,1536]{1,0:T(8,128)(2,1)S(1)}, u32[]{:S(2)}, u32[]{:S(2)}) collective-permute-start(bf16[384,1536]{1,0:T(8,128)(2,1)S(1)} %get-tuple-element.46), channel_id=1, source_target_pairs={{0,6},{1,7},{2,4},{3,5},{4,2},{5,3},{6,0},{7,1},{8,14},{9,15},{10,... | collective-permute-start | bytes 3538952 | tf_op jit(solution)/shard_map/ppermute | solution.py:35
  25.6 1.7 %collective-permute-done.1.first = bf16[256,3072]{1,0:T(8,128)(2,1)S(1)} collective-permute-done((bf16[256,3072]{1,0:T(8,128)(2,1)S(1)}, bf16[256,3072]{1,0:T(8,128)(2,1)S(1)}, u32[]{:S(2)}, u32[]{:S(2)}) %collective-permute-start.1) | collective-permute-done | bytes 1572896 | tf_op jit(solution)/shard_map/ppermute | solution.py:35
  27.3 6.1 %shard_map.75 = (bf16[512,768]{1,0:T(8,128)(2,1)S(1)}, bf16[512,384]{1,0:T(8,128)(2,1)S(1)}, bf16[512,384]{1,0:T(8,128)(2,1)S(1)}, bf16[512,3072]{1,0:T(8,128)(2...) custom-call(s32[64]{0:T(128)S(1)} %copy-done.1, ...), custom_call_target="tpu_custom_call" | custom-call | flops 1 | bytes 1 | tf_op jit(solution)/shard_map/pallas_call | solution.py:251
  33.4 3.9 %collective-permute-start.3 = (bf16[512,768]{1,0:T(8,128)(2,1)S(1)}, bf16[512,768]{1,0:T(8,128)(2,1)S(1)}, u32[]{:S(2)}, u32[]{:S(2)}) collective-permute-start(bf16[512,768]{1,0:T(8,128)(2,1)S(1)} %get-tuple-element.33.own_ref), channel_id=1, source_target_pairs={{1,8},{3,10},{4,13},{6,15},{8,1},{9,16},{10,3},{11,18},{12,21},{13... | collective-permute-start | bytes 2359304 | tf_op jit(solution)/shard_map/ppermute | solution.py:35
  37.3 1.3 %collective-permute-start.4 = (bf16[512,384]{1,0:T(8,128)(2,1)S(1)}, bf16[512,384]{1,0:T(8,128)(2,1)S(1)}, u32[]{:S(2)}, u32[]{:S(2)}) collective-permute-start(bf16[512,384]{1,0:T(8,128)(2,1)S(1)} %get-tuple-element.36), channel_id=1, source_target_pairs={{0,1},{1,0},{2,3},{3,2},{4,5},{5,4},{6,7},{7,6},{8,9},{9,8},{10,11... | collective-permute-start | bytes 1179656 | tf_op jit(solution)/shard_map/ppermute | solution.py:35
  38.8 1.8 %shard_map.76.q_ref = bf16[512,384]{1,0:T(8,128)(2,1)S(1)} custom-call(bf16[512,3072]{1,0:T(8,128)(2,1)S(1)} %get-tuple-element.34.normed, bf16[3072,384]{1,0:T(8,128)(2,1)S(1)} %get-tuple-element.35.weight), custom_call_target="tpu_custom_call" | custom-call | flops 1 | bytes 1 | tf_op jit(solution)/shard_map/pallas_call | solution.py:282
  40.6 4.2 %shard_map.77 = (f32[512,384]{1,0:T(8,128)S(1)}, f32[512,384]{1,0:T(8,128)S(1)}, f32[512,384]{1,0:T(8,128)S(1)}) custom-call(bf16[1536,128]{1,0:T(8,128)(2,1)S(1)} %get-tuple-element.31.dead_ref, bf16[512,384]{1,0:T(8,128)(2,1)S(1)} %shard_map.76.q_ref, bf16[512,768]{1,0:T(8,128)(2,1)S(1)} %get-tuple-element.33.own_ref, ...), custom_call_target="tpu_custom_call" | custom-call | flops 1 | bytes 1 | tf_op jit(solution)/shard_map/pallas_call | solution.py:388
  44.8 1.9 %collective-permute-start.8 = (bf16[512,768]{1,0:T(8,128)(2,1)S(1)}, bf16[512,768]{1,0:T(8,128)(2,1)S(1)}, u32[]{:S(2)}, u32[]{:S(2)}) collective-permute-start(bf16[512,768]{1,0:T(8,128)(2,1)S(1)} %get-tuple-element.42.kept), channel_id=1, source_target_pairs={{4,0},{6,2},{8,4},{10,6},{12,8},{13,5},{14,10},{15,7},{16,12},{18,... | collective-permute-start | bytes 2359304 | tf_op jit(solution)/shard_map/ppermute | solution.py:35
  47.2 3.0 %shard_map.78.held = bf16[512,384]{1,0:T(8,128)(2,1)S(1)} custom-call(bf16[1536,128]{1,0:T(8,128)(2,1)S(1)} %get-tuple-element.31.dead_ref, bf16[512,384]{1,0:T(8,128)(2,1)S(1)} %shard_map.76.q_ref, bf16[512,768]{1,0:T(8,128)(2,1)S(1)} %collective-permute-done.3.kv_ref, f32[512,384]{1,0:T(8,128)S(1)} %get-tuple-element.38.o_ref, ...), custom_call_target="tpu_custom_call" | custom-call | flops 1 | bytes 1 | tf_op jit(solution)/shard_map/pallas_call | solution.py:427
  50.3 1.5 %collective-permute-done.10.source.w_far = bf16[384,1536]{1,0:T(8,128)(2,1)S(1)} collective-permute-done((bf16[384,1536]{1,0:T(8,128)(2,1)S(1)}, bf16[384,1536]{1,0:T(8,128)(2,1)S(1)}, u32[]{:S(2)}, u32[]{:S(2)}) %collective-permute-start.10) | collective-permute-done | bytes 1179680 | tf_op jit(solution)/shard_map/ppermute | solution.py:35
  51.9 2.9 %collective-permute-start.11 = (bf16[384,768]{1,0:T(8,128)(2,1)S(1)}, bf16[384,768]{1,0:T(8,128)(2,1)S(1)}, u32[]{:S(2)}, u32[]{:S(2)}) collective-permute-start(bf16[384,768]{1,0:T(8,128)(2,1)S(1)} %shard_map.79), channel_id=1, source_target_pairs={{0,1},{1,0},{2,3},{3,2},{4,5},{5,4},{6,7},{7,6},{8,9},{9,8},{10,11... | collective-permute-start | bytes 1769480 | tf_op jit(solution)/shard_map/ppermute | solution.py:35
  54.9 3.4 %collective-permute-start.7 = (bf16[512,384]{1,0:T(8,128)(2,1)S(1)}, bf16[512,384]{1,0:T(8,128)(2,1)S(1)}, u32[]{:S(2)}, u32[]{:S(2)}) collective-permute-start(bf16[512,384]{1,0:T(8,128)(2,1)S(1)} %shard_map.78.held), channel_id=1, source_target_pairs={{1,3},{3,1},{4,2},{6,0},{8,6},{9,11},{10,4},{11,9},{12,10},{13,7},... | collective-permute-start | bytes 1179656 | tf_op jit(solution)/shard_map/ppermute | solution.py:35
  58.4 2.2 %collective-permute-start.6 = (bf16[512,384]{1,0:T(8,128)(2,1)S(1)}, bf16[512,384]{1,0:T(8,128)(2,1)S(1)}, u32[]{:S(2)}, u32[]{:S(2)}) collective-permute-start(bf16[512,384]{1,0:T(8,128)(2,1)S(1)} %shard_map.78.held), channel_id=1, source_target_pairs={{4,0},{6,2},{8,4},{10,6},{12,8},{13,5},{14,10},{15,7},{16,12},{18,... | collective-permute-start | bytes 1179656 | tf_op jit(solution)/shard_map/ppermute | solution.py:35
  60.5 1.7 %collective-permute-start.14 = (bf16[512,384]{1,0:T(8,128)(2,1)S(1)}, bf16[512,384]{1,0:T(8,128)(2,1)S(1)}, u32[]{:S(2)}, u32[]{:S(2)}) collective-permute-start(bf16[512,384]{1,0:T(8,128)(2,1)S(1)} %shard_map.78.held), channel_id=1, source_target_pairs={{0,1},{1,0},{2,3},{3,2},{4,5},{5,4},{6,7},{7,6},{8,9},{9,8},{10,11... | collective-permute-start | bytes 1179656 | tf_op jit(solution)/shard_map/ppermute | solution.py:35
  62.2 1.1 %shard_map.80 = (bf16[1536,768]{1,0:T(8,128)(2,1)S(1)}, f32[1,768]{1,0:T(1,128)S(1)}) custom-call(f32[64,384]{1,0:T(8,128)S(1)} %bitcast.5, bf16[384,3072]{1,0:T(8,128)(2,1)} %out_weight.5, bf16[384,768]{1,0:T(8,128)(2,1)S(1)} %collective-permute-done.9.w_twin, bf16[384,1536]{1,0:T(8,128)(2,1)S(1)} %collective-permute-done.10.source.w_far, ...), custom_call_target="tpu_custom_call" | custom-call | flops 1 | bytes 1 | tf_op jit(solution)/shard_map/pallas_call | solution.py:488
  63.4 9.4 %collective-permute-done.7.cross = bf16[512,384]{1,0:T(8,128)(2,1)S(1)} collective-permute-done((bf16[512,384]{1,0:T(8,128)(2,1)S(1)}, bf16[512,384]{1,0:T(8,128)(2,1)S(1)}, u32[]{:S(2)}, u32[]{:S(2)}) %collective-permute-start.7) | collective-permute-done | bytes 393248 | tf_op jit(solution)/shard_map/ppermute | solution.py:35
  72.7 0.8 collective-permute-done.6.same
  73.5 3.1 %collective-permute-start.12 = (bf16[512,384]{1,0:T(8,128)(2,1)S(1)}, bf16[512,384]{1,0:T(8,128)(2,1)S(1)}, u32[]{:S(2)}, u32[]{:S(2)}) collective-permute-start(bf16[512,384]{1,0:T(8,128)(2,1)S(1)} %collective-permute-done.6.same), channel_id=1, source_target_pairs={{0,1},{1,0},{2,3},{3,2},{4,5},{5,4},{6,7},{7,6},{8,9},{9,8},{10,11... | collective-permute-start | bytes 1179656 | tf_op jit(solution)/shard_map/ppermute | solution.py:35
  76.6 0.8 %shard_map.81.partial = f32[512,768]{1,0:T(8,128)S(1)} custom-call(bf16[512,384]{1,0:T(8,128)(2,1)S(1)} %collective-permute-done.6.same, bf16[512,384]{1,0:T(8,128)(2,1)S(1)} %collective-permute-done.7.cross, bf16[512,384]{1,0:T(8,128)(2,1)S(1)} %shard_map.78.held, bf16[1536,768]{1,0:T(8,128)(2,1)S(1)} %get-tuple-element.48.weight), custom_call_target="tpu_custom_call" | custom-call | flops 1 | bytes 1 | tf_op jit(solution)/shard_map/pallas_call | solution.py:508
  78.5 1.6 %shard_map.82 = bf16[512,768]{1,0:T(8,128)(2,1)} custom-call(bf16[512,384]{1,0:T(8,128)(2,1)S(1)} %collective-permute-done.12.same, bf16[512,384]{1,0:T(8,128)(2,1)S(1)} %collective-permute-done.13.cross, bf16[512,384]{1,0:T(8,128)(2,1)S(1)} %collective-permute-done.14.held, bf16[1536,768]{1,0:T(8,128)(2,1)S(1)} %get-tuple-element.48.weight, ...), custom_call_target="tpu_custom_call" | custom-call | flops 1 | bytes 1 | tf_op jit(solution)/shard_map/pallas_call | solution.py:560
  (28 shorter events, 3.9 us)
Async XLA Ops:
  0.0 3.9 %copy-start.2 = (s32[64]{0:T(128)S(1)}, s32[64]{0:T(128)}, u32[]{:S(2)}) copy-start(s32[64]{0:T(128)} %param.8) | copy-start | bytes 772
  0.0 4.3 %copy-start = (bf16[512,144]{0,1:T(8,128)(2,1)S(1)}, bf16[512,144]{0,1:T(8,128)(2,1)}, u32[]{:S(2)}) copy-start(bf16[512,144]{0,1:T(8,128)(2,1)} %param.10) | copy-start | bytes 442372
  0.0 27.3 %copy-start.1 = (s32[64]{0:T(128)S(1)}, s32[64]{0:T(128)}, u32[]{:S(2)}) copy-start(s32[64]{0:T(128)} %counts_ref.1) | copy-start | bytes 772
  0.0 27.3 %collective-permute-start.2 = (bf16[3,3072,384]{2,1,0:T(8,128)(2,1)}, bf16[3,3072,384]{2,1,0:T(8,128)(2,1)S(1)}, u32[]{:S(2)}, u32[]{:S(2)}) collective-permute-start(bf16[3,3072,384]{2,1,0:T(8,128)(2,1)} %own_weight.1), channel_id=1, source_target_pairs={{0,1},{1,0},{2,3},{3,2},{4,5},{5,4},{6,7},{7,6},{8,9},{9,8},{10,11... | collective-permute-start | bytes 21233672 | tf_op jit(solution)/shard_map/ppermute | solution.py:35
  2.5 19.6 %collective-permute-start = (bf16[256,3072]{1,0:T(8,128)(2,1)S(1)}, bf16[256,3072]{1,0:T(8,128)(2,1)S(1)}, u32[]{:S(2)}, u32[]{:S(2)}) collective-permute-start(bf16[256,3072]{1,0:T(8,128)(2,1)S(1)} %get-tuple-element.29), channel_id=1, source_target_pairs={{0,4},{1,7},{2,6},{3,5},{4,0},{5,3},{6,2},{7,1},{8,12},{9,15},{10,... | collective-permute-start | bytes 4718600 | tf_op jit(solution)/shard_map/ppermute | solution.py:35
  22.2 5.1 %collective-permute-start.1 = (bf16[256,3072]{1,0:T(8,128)(2,1)S(1)}, bf16[256,3072]{1,0:T(8,128)(2,1)S(1)}, u32[]{:S(2)}, u32[]{:S(2)}) collective-permute-start(bf16[256,3072]{1,0:T(8,128)(2,1)S(1)} %collective-permute-done.second), channel_id=1, source_target_pairs={{0,1},{1,0},{2,3},{3,2},{4,5},{5,4},{6,7},{7,6},{8,9},{9,8},{10,11... | collective-permute-start | bytes 4718600 | tf_op jit(solution)/shard_map/ppermute | solution.py:35
  24.3 27.5 %collective-permute-start.10 = (bf16[384,1536]{1,0:T(8,128)(2,1)S(1)}, bf16[384,1536]{1,0:T(8,128)(2,1)S(1)}, u32[]{:S(2)}, u32[]{:S(2)}) collective-permute-start(bf16[384,1536]{1,0:T(8,128)(2,1)S(1)} %get-tuple-element.46), channel_id=1, source_target_pairs={{0,6},{1,7},{2,4},{3,5},{4,2},{5,3},{6,0},{7,1},{8,14},{9,15},{10,... | collective-permute-start | bytes 3538952 | tf_op jit(solution)/shard_map/ppermute | solution.py:35
  33.4 13.9 %collective-permute-start.3 = (bf16[512,768]{1,0:T(8,128)(2,1)S(1)}, bf16[512,768]{1,0:T(8,128)(2,1)S(1)}, u32[]{:S(2)}, u32[]{:S(2)}) collective-permute-start(bf16[512,768]{1,0:T(8,128)(2,1)S(1)} %get-tuple-element.33.own_ref), channel_id=1, source_target_pairs={{1,8},{3,10},{4,13},{6,15},{8,1},{9,16},{10,3},{11,18},{12,21},{13... | collective-permute-start | bytes 2359304 | tf_op jit(solution)/shard_map/ppermute | solution.py:35
  37.3 3.3 %collective-permute-start.4 = (bf16[512,384]{1,0:T(8,128)(2,1)S(1)}, bf16[512,384]{1,0:T(8,128)(2,1)S(1)}, u32[]{:S(2)}, u32[]{:S(2)}) collective-permute-start(bf16[512,384]{1,0:T(8,128)(2,1)S(1)} %get-tuple-element.36), channel_id=1, source_target_pairs={{0,1},{1,0},{2,3},{3,2},{4,5},{5,4},{6,7},{7,6},{8,9},{9,8},{10,11... | collective-permute-start | bytes 1179656 | tf_op jit(solution)/shard_map/ppermute | solution.py:35
  38.5 2.1 %collective-permute-start.5 = (bf16[512,384]{1,0:T(8,128)(2,1)S(1)}, bf16[512,384]{1,0:T(8,128)(2,1)S(1)}, u32[]{:S(2)}, u32[]{:S(2)}) collective-permute-start(bf16[512,384]{1,0:T(8,128)(2,1)S(1)} %get-tuple-element.37), channel_id=1, source_target_pairs={{0,1},{1,0},{2,3},{3,2},{4,5},{5,4},{6,7},{7,6},{8,9},{9,8},{10,11... | collective-permute-start | bytes 1179656 | tf_op jit(solution)/shard_map/ppermute | solution.py:35
  44.8 28.7 %collective-permute-start.8 = (bf16[512,768]{1,0:T(8,128)(2,1)S(1)}, bf16[512,768]{1,0:T(8,128)(2,1)S(1)}, u32[]{:S(2)}, u32[]{:S(2)}) collective-permute-start(bf16[512,768]{1,0:T(8,128)(2,1)S(1)} %get-tuple-element.42.kept), channel_id=1, source_target_pairs={{4,0},{6,2},{8,4},{10,6},{12,8},{13,5},{14,10},{15,7},{16,12},{18,... | collective-permute-start | bytes 2359304 | tf_op jit(solution)/shard_map/ppermute | solution.py:35
  51.9 8.6 %collective-permute-start.11 = (bf16[384,768]{1,0:T(8,128)(2,1)S(1)}, bf16[384,768]{1,0:T(8,128)(2,1)S(1)}, u32[]{:S(2)}, u32[]{:S(2)}) collective-permute-start(bf16[384,768]{1,0:T(8,128)(2,1)S(1)} %shard_map.79), channel_id=1, source_target_pairs={{0,1},{1,0},{2,3},{3,2},{4,5},{5,4},{6,7},{7,6},{8,9},{9,8},{10,11... | collective-permute-start | bytes 1769480 | tf_op jit(solution)/shard_map/ppermute | solution.py:35
  54.8 7.4 %collective-permute-start.9 = (bf16[384,768]{1,0:T(8,128)(2,1)S(1)}, bf16[384,768]{1,0:T(8,128)(2,1)S(1)}, u32[]{:S(2)}, u32[]{:S(2)}) collective-permute-start(bf16[384,768]{1,0:T(8,128)(2,1)S(1)} %get-tuple-element.44), channel_id=1, source_target_pairs={{0,1},{1,0},{2,3},{3,2},{4,5},{5,4},{6,7},{7,6},{8,9},{9,8},{10,11... | collective-permute-start | bytes 1769480 | tf_op jit(solution)/shard_map/ppermute | solution.py:35
  54.9 17.8 %collective-permute-start.7 = (bf16[512,384]{1,0:T(8,128)(2,1)S(1)}, bf16[512,384]{1,0:T(8,128)(2,1)S(1)}, u32[]{:S(2)}, u32[]{:S(2)}) collective-permute-start(bf16[512,384]{1,0:T(8,128)(2,1)S(1)} %shard_map.78.held), channel_id=1, source_target_pairs={{1,3},{3,1},{4,2},{6,0},{8,6},{9,11},{10,4},{11,9},{12,10},{13,7},... | collective-permute-start | bytes 1179656 | tf_op jit(solution)/shard_map/ppermute | solution.py:35
  58.4 15.2 %collective-permute-start.6 = (bf16[512,384]{1,0:T(8,128)(2,1)S(1)}, bf16[512,384]{1,0:T(8,128)(2,1)S(1)}, u32[]{:S(2)}, u32[]{:S(2)}) collective-permute-start(bf16[512,384]{1,0:T(8,128)(2,1)S(1)} %shard_map.78.held), channel_id=1, source_target_pairs={{4,0},{6,2},{8,4},{10,6},{12,8},{13,5},{14,10},{15,7},{16,12},{18,... | collective-permute-start | bytes 1179656 | tf_op jit(solution)/shard_map/ppermute | solution.py:35
  60.5 16.9 %collective-permute-start.14 = (bf16[512,384]{1,0:T(8,128)(2,1)S(1)}, bf16[512,384]{1,0:T(8,128)(2,1)S(1)}, u32[]{:S(2)}, u32[]{:S(2)}) collective-permute-start(bf16[512,384]{1,0:T(8,128)(2,1)S(1)} %shard_map.78.held), channel_id=1, source_target_pairs={{0,1},{1,0},{2,3},{3,2},{4,5},{5,4},{6,7},{7,6},{8,9},{9,8},{10,11... | collective-permute-start | bytes 1179656 | tf_op jit(solution)/shard_map/ppermute | solution.py:35
  73.5 4.4 %collective-permute-start.12 = (bf16[512,384]{1,0:T(8,128)(2,1)S(1)}, bf16[512,384]{1,0:T(8,128)(2,1)S(1)}, u32[]{:S(2)}, u32[]{:S(2)}) collective-permute-start(bf16[512,384]{1,0:T(8,128)(2,1)S(1)} %collective-permute-done.6.same), channel_id=1, source_target_pairs={{0,1},{1,0},{2,3},{3,2},{4,5},{5,4},{6,7},{7,6},{8,9},{9,8},{10,11... | collective-permute-start | bytes 1179656 | tf_op jit(solution)/shard_map/ppermute | solution.py:35
  76.6 1.9 %collective-permute-start.13 = (bf16[512,384]{1,0:T(8,128)(2,1)S(1)}, bf16[512,384]{1,0:T(8,128)(2,1)S(1)}, u32[]{:S(2)}, u32[]{:S(2)}) collective-permute-start(bf16[512,384]{1,0:T(8,128)(2,1)S(1)} %collective-permute-done.7.cross), channel_id=1, source_target_pairs={{0,1},{1,0},{2,3},{3,2},{4,5},{5,4},{6,7},{7,6},{8,9},{9,8},{10,11... | collective-permute-start | bytes 1179656 | tf_op jit(solution)/shard_map/ppermute | solution.py:35

commit v8 on v7

--- a/solution.py
+++ b/solution.py
@@ -173,11 +173,11 @@
 
 
 def kv_kernel(
-    counts_ref, rows_ref, hidden, first, second, own_weight, twin_weight, out_weight, kv_ref, k_ref, v_ref, states_ref, q_weight,
-    twin_out, share_ref, dead_ref,
+    rows_ref, hidden, first, second, own_weight, twin_weight, out_weight, kv_ref, k_ref, v_ref, states_ref, q_weight,
+    twin_a, twin_b, share_ref,
     flat, weight, x_sems, w_sems,
 ):
-    member, core, y_hi, parity, slot = place()
+    member, core, y_hi, parity, _ = place()
     rows, width = states_ref.shape
     half = rows // 2
     each = q_weight.shape[1]
@@ -207,12 +207,16 @@
     start(core == parity, sum(weights_from(own_weight)[:2], []))
     start(core != parity, sum(weights_from(twin_weight)[:2], []))
     beside = y_hi * 2 + 1 - core
-    asides = copies_of(out_weight.at[:, lanes_at(beside, twin_out.shape[1])], twin_out, w_sems, 2, 6)
+    asides = sum(
+        (
+            copies_of(
+                out_weight.at[lanes_at(index, out.shape[0]), lanes_at(beside, out.shape[1])], out, w_sems, 1, 6 + index
+            )
+            for index, out in enumerate((twin_a, twin_b))
+        ),
+        [],
+    )
     spread(rows_ref, 0, flat)
-    step = 1 - 2 * parity
-    mine = slot + core * step
-    for index, stretch in enumerate((mine, slot + (1 - core) * step, jnp.where(core == 0, slot - step, slot + 2 * step))):
-        dead_ref[pl.ds(index * rows, rows), :] = dead_rows(rows, count_at(counts_ref, stretch))
     scale, shift = 1.0 + flat[:, width : 2 * width], flat[:, :width]
 
     def normalise(first_row, count):
@@ -245,7 +249,7 @@
         copy.wait()
 
 
-def keys_values(counts, mod_rows, hidden, first, second, own_weight, twin_weight, out_weight):
+def keys_values(mod_rows, hidden, first, second, own_weight, twin_weight, out_weight):
     rows, width = hidden.shape
     each = own_weight.shape[2]
     return pl.pallas_call(
@@ -256,11 +260,11 @@
             near_out((rows, each)),
             near_out((rows, width)),
             near_out((width, each)),
-            near_out((out_weight.shape[0], width // 4)),
+            near_out((out_weight.shape[0] // 2, width // 4)),
+            near_out((out_weight.shape[0] // 2, width // 4)),
             near_out((rows, width // 4)),
-            near_out((3 * rows, PAIR)),
         ),
-        in_specs=[smem_spec(), vmem_spec()] + [any_spec()] * 6,
+        in_specs=[vmem_spec()] + [any_spec()] * 6,
         out_specs=(vmem_spec(),) * 8,
         scratch_shapes=[
             pltpu.VMEM((1, 3 * width), jnp.float32),
@@ -270,7 +274,7 @@
         ],
         compiler_params=pltpu.CompilerParams(vmem_limit_bytes=24 * MIB),
         cost_estimate=cost(1, 1),
-    )(counts, mod_rows, far(hidden), first, second, far(own_weight), twin_weight, far(out_weight))
+    )(mod_rows, far(hidden), first, second, far(own_weight), twin_weight, far(out_weight))
 
 
 def query_kernel(normed, weight, query_ref):
@@ -355,6 +359,26 @@
     return slice(pair * PAIR, (pair + 1) * PAIR)
 
 
+def masks_kernel(counts_ref, dead_ref):
+    _, core, _, parity, slot = place()
+    rows = dead_ref.shape[0] // 3
+    step = 1 - 2 * parity
+    stretches = (slot + core * step, slot + (1 - core) * step, jnp.where(core == 0, slot - step, slot + 2 * step))
+    for index, stretch in enumerate(stretches):
+        dead_ref[index * rows : (index + 1) * rows, :] = dead_rows(rows, count_at(counts_ref, stretch))
+
+
+def masks(counts, rows):
+    return pl.pallas_call(
+        masks_kernel,
+        out_shape=near_out((3 * rows, PAIR)),
+        in_specs=[smem_spec()],
+        out_specs=vmem_spec(),
+        compiler_params=pltpu.CompilerParams(vmem_limit_bytes=2 * MIB),
+        cost_estimate=cost(1, 1),
+    )(counts)
+
+
 def local_kernel(dead_ref, q_ref, own_ref, k_twin, v_twin, o_ref, m_ref, l_ref):
     span = own_ref.shape[0]
     tile = 256
@@ -435,7 +459,7 @@
 
 
 def tail_kernel(
-    rows_ref, out_weight, w_twin, w_far, w_far_twin, gathered, gate, flat, sems,
+    rows_ref, out_weight, w_far, twin_a, twin_b, far_a, far_b, gathered, gate, flat, sems,
 ):
     member, core, _, parity, _ = place()
     share = gathered.shape[1]
@@ -444,15 +468,17 @@
     local = jnp.where(core == 0, 1 - parity, parity)
     whole, mine, own = pl.ds(0, share), lanes_at(core, share), lanes_at(member, share)
     copies = []
-    for source, lanes, far_half, y_lo in (
-        (out_weight, own, 0, core),
-        (w_twin, whole, 0, 1 - core),
-        (w_far, mine, 1, core),
-        (w_far_twin, whole, 1, 1 - core),
+    for sources, lanes, far_half, y_lo in (
+        ((out_weight,), own, 0, core),
+        ((twin_a, twin_b), whole, 0, 1 - core),
+        ((w_far,), mine, 1, core),
+        ((far_a, far_b), whole, 1, 1 - core),
     ):
         base = jnp.where(local == y_lo, 0, 2 * block) + far_half * block
-        to = pl.ds(pl.multiple_of(base, block), block)
-        copies += copies_of(source.at[:, lanes], gathered.at[to, :], sems, 2, len(copies))
+        each = block // len(sources)
+        for index, source in enumerate(sources):
+            to = pl.ds(pl.multiple_of(base + index * each, each), each)
+            copies += copies_of(source.at[:, lanes], gathered.at[to, :], sems, 2 // len(sources), len(copies))
     for copy in copies:
         copy.start()
     spread(rows_ref, 1, flat)
@@ -461,8 +487,11 @@
         copy.wait()
 
 
-def columns_kernel(source, out, sems):
-    copies = copies_of(source.at[:, lanes_at(1 - place()[1], out.shape[1])], out, sems, 4)
+def columns_kernel(source, first, second, sems):
+    half, width = first.shape
+    copies = []
+    for index, out in enumerate((first, second)):
+        copies += copies_of(source.at[pl.ds(index * half, half), lanes_at(1 - place()[1], width)], out, sems, 2, 2 * index)
     for copy in copies:
         copy.start()
     for copy in copies:
@@ -473,27 +502,27 @@
     rows, width = blocks.shape
     return pl.pallas_call(
         columns_kernel,
-        out_shape=near_out((rows, width // 2)),
+        out_shape=(near_out((rows // 2, width // 2)),) * 2,
         in_specs=[any_spec()],
-        out_specs=vmem_spec(),
+        out_specs=(vmem_spec(),) * 2,
         scratch_shapes=[pltpu.SemaphoreType.DMA((4,))],
         compiler_params=pltpu.CompilerParams(vmem_limit_bytes=2 * MIB),
         cost_estimate=cost(1, 1),
     )(blocks)
 
 
-def tail_inputs(mod_rows, out_weight, w_twin, w_far, w_far_twin):
-    block, share = w_twin.shape
-    width = out_weight.shape[1]
+def tail_inputs(mod_rows, out_weight, w_far, twin_a, twin_b, far_a, far_b):
+    block, width = out_weight.shape
+    share = twin_a.shape[1]
     return pl.pallas_call(
         tail_kernel,
         out_shape=(near_out((4 * block, share)), near_out((1, share), jnp.float32)),
-        in_specs=[vmem_spec()] + [any_spec()] * 4,
+        in_specs=[vmem_spec()] + [any_spec()] * 6,
         out_specs=(vmem_spec(),) * 2,
         scratch_shapes=[pltpu.VMEM((1, 3 * width), jnp.float32), pltpu.SemaphoreType.DMA((8,))],
         compiler_params=pltpu.CompilerParams(vmem_limit_bytes=2 * MIB),
         cost_estimate=cost(1, 1),
-    )(mod_rows, far(out_weight), w_twin, w_far, w_far_twin)
+    )(mod_rows, far(out_weight), w_far, twin_a, twin_b, far_a, far_b)
 
 
 def first_out_kernel(same, cross, held, weight, partial):
@@ -586,7 +615,8 @@
 
     first = twin(after(second, mod_rows))
     w_far = route(after(far_mine, mod_rows), target=lambda s, y, k: (s ^ 1, 1 - y, k))
-    kv, k, v, normed, q_weight, twin_mine, share_states, dead = keys_values(frame_counts, mod_rows, hidden, first, second, qkv_weight, twin_weight, out_weight)
+    dead = masks(after(frame_counts, mod_rows), hidden.shape[0])
+    kv, k, v, normed, q_weight, twin_a, twin_b, share_states = keys_values(after(mod_rows, dead), hidden, first, second, qkv_weight, twin_weight, out_weight)
 
     def remote_target(s, y, k):
         back = (s % 2 == 0) == (k == 0)
@@ -610,9 +640,9 @@
     same = route(attn, target=lambda s, y, k: None if s % 2 == 0 and k == 1 else goal(s, y, k))
     cross = route(attn, target=lambda s, y, k: goal(s, 1 - y, k))
     twin_attn = twin(attn)
-    w_far_twin = twin(columns_of_twin(after(w_far, attn)))
-    w_twin = twin(after(twin_mine, attn))
-    weight, gate = tail_inputs(mod_rows, out_weight, w_twin, w_far, w_far_twin)
+    blocks = [*columns_of_twin(after(w_far, attn)), after(twin_a, attn), after(twin_b, attn)]
+    far_a, far_b, twin_a, twin_b = [twin(a) for a in blocks]
+    weight, gate = tail_inputs(mod_rows, out_weight, w_far, twin_a, twin_b, far_a, far_b)
     same, cross, residual, _ = lax.optimization_barrier((same, cross, residual, weight))
     partial = first_out(same, cross, attn, weight)
     return last_out(twin(same), twin(cross), twin_attn, weight, partial, share_states, residual, gate, fresh)

time: 81 us -> 79.9 us (0.986)
    ppermute x15 -> x17, waiting for transfers between devices: 15.4 us -> 14.8 us  [routed(): return lax.ppermute(array, BOTH, pairs)]
    ppermute x15 -> x17, starting transfers between devices: 26.3 us -> 26.2 us  [routed(): return lax.ppermute(array, BOTH, pairs)]
  transfers between devices with their start and end apart: 15 -> 17, of which waited for: 8 -> 8; matrix products, arithmetic and copies ran while one was open for 0% -> 0% of each run, Pallas kernels for 24% -> 24%
where the time goes in v8:
time: 79.9 us; the launch traced here: 79.6 us
  starting transfers between devices  26.2 us (33%)
  Pallas kernels  20.7 us (26%)
  blocking collectives  17.1 us (21%)
  waiting for transfers between devices  14.8 us (19%)
    ppermute x17, starting transfers between devices, routed(): return lax.ppermute(array, BOTH, pairs)  26.2 us
    all_to_all x1, blocking collectives, on_device(): mod_rows = lax.all_to_all(payload, 'queue', 0, 0, tiled=True)[:, 0, :]  17.1 us
    ppermute x17, waiting for transfers between devices, routed(): return lax.ppermute(array, BOTH, pairs)  14.8 us
    pallas_call x1, Pallas kernels, keys_values(): pl.pallas_call(kv_kernel, out_shape=(near_out((rows, 2 * each)), near_out...  5.41 us
    pallas_call x1, Pallas kernels, local_attention(): pl.pallas_call(local_kernel, out_shape=(part,) * 3, in_specs=[vmem_spec()...  4.11 us
    pallas_call x1, Pallas kernels, remote_attention(): pl.pallas_call(remote_kernel, out_shape=near_out((span, 3 * PAIR)), in_sp...  3.05 us
    pallas_call x1, Pallas kernels, queries(): pl.pallas_call(query_kernel, out_shape=near_out((normed.shape[0], weight....  1.79 us
    pallas_call x1, Pallas kernels, slices(): pl.pallas_call(slices_kernel, out_shape=(near_out((rows // 2, width)), ne...  1.77 us
  transfers between devices with their start and end apart: 17, of which 8 were waited for; matrix products, arithmetic and copies ran while one was open for 0% of the time, Pallas kernels for 24%

profile of v8, /device:TPU:111, one launch (start us, length us, event | category | flops | bytes accessed | tf_op | source)
XLA Modules:
  0.0 79.6 jit_solution(14980753455053377267)
XLA Ops:
  0.8 1.8 %shard_map.75 = (bf16[256,3072]{1,0:T(8,128)(2,1)S(1)}, bf16[384,1536]{1,0:T(8,128)(2,1)S(1)}) custom-call(bf16[512,3072]{1,0:T(8,128)(2,1)} %hidden.3, bf16[384,3072]{1,0:T(8,128)(2,1)} %out_weight.5), custom_call_target="tpu_custom_call" | custom-call | bytes 4194304 | tf_op jit(solution)/shard_map/pallas_call | solution.py:105
  2.5 1.4 %collective-permute-start = (bf16[256,3072]{1,0:T(8,128)(2,1)S(1)}, bf16[256,3072]{1,0:T(8,128)(2,1)S(1)}, u32[]{:S(2)}, u32[]{:S(2)}) collective-permute-start(bf16[256,3072]{1,0:T(8,128)(2,1)S(1)} %get-tuple-element.36), channel_id=1, source_target_pairs={{0,4},{1,7},{2,6},{3,5},{4,0},{5,3},{6,2},{7,1},{8,12},{9,15},{10,... | collective-permute-start | bytes 4718600 | tf_op jit(solution)/shard_map/ppermute | solution.py:35
  4.6 17.1 %all_to_all.5 = f32[64,1,384]{2,1,0:T(1,128)S(1)} all-to-all(f32[64,1,384]{2,1,0:T(1,128)S(1)} %shard_map.73), channel_id=1, replica_groups=mesh['queue'=64,'heads'=4] {'queue'}, dimensions={0} | all-to-all | bytes 196608 | tf_op jit(solution)/shard_map/all_to_all | solution.py:614
  22.2 2.1 %collective-permute-start.1 = (bf16[256,3072]{1,0:T(8,128)(2,1)S(1)}, bf16[256,3072]{1,0:T(8,128)(2,1)S(1)}, u32[]{:S(2)}, u32[]{:S(2)}) collective-permute-start(bf16[256,3072]{1,0:T(8,128)(2,1)S(1)} %collective-permute-done.second), channel_id=1, source_target_pairs={{0,1},{1,0},{2,3},{3,2},{4,5},{5,4},{6,7},{7,6},{8,9},{9,8},{10,11... | collective-permute-start | bytes 4718600 | tf_op jit(solution)/shard_map/ppermute | solution.py:35
  24.3 1.3 %collective-permute-start.9 = (bf16[384,1536]{1,0:T(8,128)(2,1)S(1)}, bf16[384,1536]{1,0:T(8,128)(2,1)S(1)}, u32[]{:S(2)}, u32[]{:S(2)}) collective-permute-start(bf16[384,1536]{1,0:T(8,128)(2,1)S(1)} %get-tuple-element.50), channel_id=1, source_target_pairs={{0,6},{1,7},{2,4},{3,5},{4,2},{5,3},{6,0},{7,1},{8,14},{9,15},{10,... | collective-permute-start | bytes 3538952 | tf_op jit(solution)/shard_map/ppermute | solution.py:35
  26.3 1.1 %collective-permute-done.1.first = bf16[256,3072]{1,0:T(8,128)(2,1)S(1)} collective-permute-done((bf16[256,3072]{1,0:T(8,128)(2,1)S(1)}, bf16[256,3072]{1,0:T(8,128)(2,1)S(1)}, u32[]{:S(2)}, u32[]{:S(2)}) %collective-permute-start.1) | collective-permute-done | bytes 1572896 | tf_op jit(solution)/shard_map/ppermute | solution.py:35
  27.3 5.4 %shard_map.76 = (bf16[512,768]{1,0:T(8,128)(2,1)S(1)}, bf16[512,384]{1,0:T(8,128)(2,1)S(1)}, bf16[512,384]{1,0:T(8,128)(2,1)S(1)}, bf16[512,3072]{1,0:T(8,128)(2...) custom-call(f32[64,384]{1,0:T(8,128)S(1)} %bitcast.4, ...), custom_call_target="tpu_custom_call" | custom-call | flops 1 | bytes 1 | tf_op jit(solution)/shard_map/pallas_call | solution.py:255
  32.7 4.0 %collective-permute-start.3 = (bf16[512,768]{1,0:T(8,128)(2,1)S(1)}, bf16[512,768]{1,0:T(8,128)(2,1)S(1)}, u32[]{:S(2)}, u32[]{:S(2)}) collective-permute-start(bf16[512,768]{1,0:T(8,128)(2,1)S(1)} %get-tuple-element.39.own_ref), channel_id=1, source_target_pairs={{1,8},{3,10},{4,13},{6,15},{8,1},{9,16},{10,3},{11,18},{12,21},{13... | collective-permute-start | bytes 2359304 | tf_op jit(solution)/shard_map/ppermute | solution.py:35
  36.7 1.2 %collective-permute-start.4 = (bf16[512,384]{1,0:T(8,128)(2,1)S(1)}, bf16[512,384]{1,0:T(8,128)(2,1)S(1)}, u32[]{:S(2)}, u32[]{:S(2)}) collective-permute-start(bf16[512,384]{1,0:T(8,128)(2,1)S(1)} %get-tuple-element.42), channel_id=1, source_target_pairs={{0,1},{1,0},{2,3},{3,2},{4,5},{5,4},{6,7},{7,6},{8,9},{9,8},{10,11... | collective-permute-start | bytes 1179656 | tf_op jit(solution)/shard_map/ppermute | solution.py:35
  38.2 1.8 %shard_map.77.q_ref = bf16[512,384]{1,0:T(8,128)(2,1)S(1)} custom-call(bf16[512,3072]{1,0:T(8,128)(2,1)S(1)} %get-tuple-element.40.normed, bf16[3072,384]{1,0:T(8,128)(2,1)S(1)} %get-tuple-element.41.weight), custom_call_target="tpu_custom_call" | custom-call | flops 1 | bytes 1 | tf_op jit(solution)/shard_map/pallas_call | solution.py:286
  40.0 4.1 %shard_map.78 = (f32[512,384]{1,0:T(8,128)S(1)}, f32[512,384]{1,0:T(8,128)S(1)}, f32[512,384]{1,0:T(8,128)S(1)}) custom-call(bf16[1536,128]{1,0:T(8,128)(2,1)S(1)} %shard_map.74.dead_ref, bf16[512,384]{1,0:T(8,128)(2,1)S(1)} %shard_map.77.q_ref, bf16[512,768]{1,0:T(8,128)(2,1)S(1)} %get-tuple-element.39.own_ref, ...), custom_call_target="tpu_custom_call" | custom-call | flops 1 | bytes 1 | tf_op jit(solution)/shard_map/pallas_call | solution.py:412
  44.1 1.9 %collective-permute-start.8 = (bf16[512,768]{1,0:T(8,128)(2,1)S(1)}, bf16[512,768]{1,0:T(8,128)(2,1)S(1)}, u32[]{:S(2)}, u32[]{:S(2)}) collective-permute-start(bf16[512,768]{1,0:T(8,128)(2,1)S(1)} %get-tuple-element.48.kept), channel_id=1, source_target_pairs={{4,0},{6,2},{8,4},{10,6},{12,8},{13,5},{14,10},{15,7},{16,12},{18,... | collective-permute-start | bytes 2359304 | tf_op jit(solution)/shard_map/ppermute | solution.py:35
  46.7 3.1 %shard_map.79.held = bf16[512,384]{1,0:T(8,128)(2,1)S(1)} custom-call(bf16[1536,128]{1,0:T(8,128)(2,1)S(1)} %shard_map.74.dead_ref, bf16[512,384]{1,0:T(8,128)(2,1)S(1)} %shard_map.77.q_ref, bf16[512,768]{1,0:T(8,128)(2,1)S(1)} %collective-permute-done.3.kv_ref, f32[512,384]{1,0:T(8,128)S(1)} %get-tuple-element.44.o_ref, ...), custom_call_target="tpu_custom_call" | custom-call | flops 1 | bytes 1 | tf_op jit(solution)/shard_map/pallas_call | solution.py:451
  49.7 4.4 %collective-permute-start.10 = (bf16[192,768]{1,0:T(8,128)(2,1)S(1)}, bf16[192,768]{1,0:T(8,128)(2,1)S(1)}, u32[]{:S(2)}, u32[]{:S(2)}) collective-permute-start(bf16[192,768]{1,0:T(8,128)(2,1)S(1)} %get-tuple-element.52), channel_id=1, source_target_pairs={{0,1},{1,0},{2,3},{3,2},{4,5},{5,4},{6,7},{7,6},{8,9},{9,8},{10,11... | collective-permute-start | bytes 884744 | tf_op jit(solution)/shard_map/ppermute | solution.py:35
  54.2 1.9 %collective-permute-start.7 = (bf16[512,384]{1,0:T(8,128)(2,1)S(1)}, bf16[512,384]{1,0:T(8,128)(2,1)S(1)}, u32[]{:S(2)}, u32[]{:S(2)}) collective-permute-start(bf16[512,384]{1,0:T(8,128)(2,1)S(1)} %shard_map.79.held), channel_id=1, source_target_pairs={{1,3},{3,1},{4,2},{6,0},{8,6},{9,11},{10,4},{11,9},{12,10},{13,7},... | collective-permute-start | bytes 1179656 | tf_op jit(solution)/shard_map/ppermute | solution.py:35
  56.2 1.9 %collective-permute-start.6 = (bf16[512,384]{1,0:T(8,128)(2,1)S(1)}, bf16[512,384]{1,0:T(8,128)(2,1)S(1)}, u32[]{:S(2)}, u32[]{:S(2)}) collective-permute-start(bf16[512,384]{1,0:T(8,128)(2,1)S(1)} %shard_map.79.held), channel_id=1, source_target_pairs={{4,0},{6,2},{8,4},{10,6},{12,8},{13,5},{14,10},{15,7},{16,12},{18,... | collective-permute-start | bytes 1179656 | tf_op jit(solution)/shard_map/ppermute | solution.py:35
  58.2 1.5 %collective-permute-start.12 = (bf16[192,768]{1,0:T(8,128)(2,1)S(1)}, bf16[192,768]{1,0:T(8,128)(2,1)S(1)}, u32[]{:S(2)}, u32[]{:S(2)}) collective-permute-start(bf16[192,768]{1,0:T(8,128)(2,1)S(1)} %get-tuple-element.56), channel_id=1, source_target_pairs={{0,1},{1,0},{2,3},{3,2},{4,5},{5,4},{6,7},{7,6},{8,9},{9,8},{10,11... | collective-permute-start | bytes 884744 | tf_op jit(solution)/shard_map/ppermute | solution.py:35
  59.8 1.1 %collective-permute-done.12.far_a = bf16[192,768]{1,0:T(8,128)(2,1)S(1)} collective-permute-done((bf16[192,768]{1,0:T(8,128)(2,1)S(1)}, bf16[192,768]{1,0:T(8,128)(2,1)S(1)}, u32[]{:S(2)}, u32[]{:S(2)}) %collective-permute-start.12) | collective-permute-done | bytes 294944 | tf_op jit(solution)/shard_map/ppermute | solution.py:35
  61.3 1.1 %shard_map.81 = (bf16[1536,768]{1,0:T(8,128)(2,1)S(1)}, f32[1,768]{1,0:T(1,128)S(1)}) custom-call(f32[64,384]{1,0:T(8,128)S(1)} %bitcast.5, bf16[384,3072]{1,0:T(8,128)(2,1)} %out_weight.5, bf16[384,1536]{1,0:T(8,128)(2,1)S(1)} %collective-permute-done.9.source.w_far, bf16[192,768]{1,0:T(8,128)(2,1)S(1)} %collective-permute-done.10.twin_a, ...), custom_call_target="tpu_custom_call" | custom-call | flops 1 | bytes 1 | tf_op jit(solution)/shard_map/pallas_call | solution.py:517
  62.5 9.6 %collective-permute-done.7.cross = bf16[512,384]{1,0:T(8,128)(2,1)S(1)} collective-permute-done((bf16[512,384]{1,0:T(8,128)(2,1)S(1)}, bf16[512,384]{1,0:T(8,128)(2,1)S(1)}, u32[]{:S(2)}, u32[]{:S(2)}) %collective-permute-start.7) | collective-permute-done | bytes 393248 | tf_op jit(solution)/shard_map/ppermute | solution.py:35
  72.0 0.8 collective-permute-done.6.same
  72.8 3.1 %collective-permute-start.14 = (bf16[512,384]{1,0:T(8,128)(2,1)S(1)}, bf16[512,384]{1,0:T(8,128)(2,1)S(1)}, u32[]{:S(2)}, u32[]{:S(2)}) collective-permute-start(bf16[512,384]{1,0:T(8,128)(2,1)S(1)} %collective-permute-done.6.same), channel_id=1, source_target_pairs={{0,1},{1,0},{2,3},{3,2},{4,5},{5,4},{6,7},{7,6},{8,9},{9,8},{10,11... | collective-permute-start | bytes 1179656 | tf_op jit(solution)/shard_map/ppermute | solution.py:35
  75.9 0.8 shard_map.82.partial
  77.8 1.6 %shard_map.83 = bf16[512,768]{1,0:T(8,128)(2,1)} custom-call(bf16[512,384]{1,0:T(8,128)(2,1)S(1)} %collective-permute-done.14.same, bf16[512,384]{1,0:T(8,128)(2,1)S(1)} %collective-permute-done.15.cross, bf16[512,384]{1,0:T(8,128)(2,1)S(1)} %collective-permute-done.16.held, bf16[1536,768]{1,0:T(8,128)(2,1)S(1)} %get-tuple-element.58.weight, ...), custom_call_target="tpu_custom_call" | custom-call | flops 1 | bytes 1 | tf_op jit(solution)/shard_map/pallas_call | solution.py:589
  (33 shorter events, 5.3 us)
Async XLA Ops:
  0.0 3.9 %copy-start.2 = (s32[64]{0:T(128)S(1)}, s32[64]{0:T(128)}, u32[]{:S(2)}) copy-start(s32[64]{0:T(128)} %param.8) | copy-start | bytes 772
  0.0 4.3 %copy-start = (bf16[512,144]{0,1:T(8,128)(2,1)S(1)}, bf16[512,144]{0,1:T(8,128)(2,1)}, u32[]{:S(2)}) copy-start(bf16[512,144]{0,1:T(8,128)(2,1)} %param.10) | copy-start | bytes 442372
  0.0 25.6 %copy-start.1 = (s32[64]{0:T(128)S(1)}, s32[64]{0:T(128)}, u32[]{:S(2)}) copy-start(s32[64]{0:T(128)} %counts_ref) | copy-start | bytes 772
  0.0 27.3 %collective-permute-start.2 = (bf16[3,3072,384]{2,1,0:T(8,128)(2,1)}, bf16[3,3072,384]{2,1,0:T(8,128)(2,1)S(1)}, u32[]{:S(2)}, u32[]{:S(2)}) collective-permute-start(bf16[3,3072,384]{2,1,0:T(8,128)(2,1)} %own_weight.1), channel_id=1, source_target_pairs={{0,1},{1,0},{2,3},{3,2},{4,5},{5,4},{6,7},{7,6},{8,9},{9,8},{10,11... | collective-permute-start | bytes 21233672 | tf_op jit(solution)/shard_map/ppermute | solution.py:35
  2.5 19.6 %collective-permute-start = (bf16[256,3072]{1,0:T(8,128)(2,1)S(1)}, bf16[256,3072]{1,0:T(8,128)(2,1)S(1)}, u32[]{:S(2)}, u32[]{:S(2)}) collective-permute-start(bf16[256,3072]{1,0:T(8,128)(2,1)S(1)} %get-tuple-element.36), channel_id=1, source_target_pairs={{0,4},{1,7},{2,6},{3,5},{4,0},{5,3},{6,2},{7,1},{8,12},{9,15},{10,... | collective-permute-start | bytes 4718600 | tf_op jit(solution)/shard_map/ppermute | solution.py:35
  22.2 5.1 %collective-permute-start.1 = (bf16[256,3072]{1,0:T(8,128)(2,1)S(1)}, bf16[256,3072]{1,0:T(8,128)(2,1)S(1)}, u32[]{:S(2)}, u32[]{:S(2)}) collective-permute-start(bf16[256,3072]{1,0:T(8,128)(2,1)S(1)} %collective-permute-done.second), channel_id=1, source_target_pairs={{0,1},{1,0},{2,3},{3,2},{4,5},{5,4},{6,7},{7,6},{8,9},{9,8},{10,11... | collective-permute-start | bytes 4718600 | tf_op jit(solution)/shard_map/ppermute | solution.py:35
  24.3 31.9 %collective-permute-start.9 = (bf16[384,1536]{1,0:T(8,128)(2,1)S(1)}, bf16[384,1536]{1,0:T(8,128)(2,1)S(1)}, u32[]{:S(2)}, u32[]{:S(2)}) collective-permute-start(bf16[384,1536]{1,0:T(8,128)(2,1)S(1)} %get-tuple-element.50), channel_id=1, source_target_pairs={{0,6},{1,7},{2,4},{3,5},{4,2},{5,3},{6,0},{7,1},{8,14},{9,15},{10,... | collective-permute-start | bytes 3538952 | tf_op jit(solution)/shard_map/ppermute | solution.py:35
  32.7 13.9 %collective-permute-start.3 = (bf16[512,768]{1,0:T(8,128)(2,1)S(1)}, bf16[512,768]{1,0:T(8,128)(2,1)S(1)}, u32[]{:S(2)}, u32[]{:S(2)}) collective-permute-start(bf16[512,768]{1,0:T(8,128)(2,1)S(1)} %get-tuple-element.39.own_ref), channel_id=1, source_target_pairs={{1,8},{3,10},{4,13},{6,15},{8,1},{9,16},{10,3},{11,18},{12,21},{13... | collective-permute-start | bytes 2359304 | tf_op jit(solution)/shard_map/ppermute | solution.py:35
  36.7 3.3 %collective-permute-start.4 = (bf16[512,384]{1,0:T(8,128)(2,1)S(1)}, bf16[512,384]{1,0:T(8,128)(2,1)S(1)}, u32[]{:S(2)}, u32[]{:S(2)}) collective-permute-start(bf16[512,384]{1,0:T(8,128)(2,1)S(1)} %get-tuple-element.42), channel_id=1, source_target_pairs={{0,1},{1,0},{2,3},{3,2},{4,5},{5,4},{6,7},{7,6},{8,9},{9,8},{10,11... | collective-permute-start | bytes 1179656 | tf_op jit(solution)/shard_map/ppermute | solution.py:35
  37.9 2.1 %collective-permute-start.5 = (bf16[512,384]{1,0:T(8,128)(2,1)S(1)}, bf16[512,384]{1,0:T(8,128)(2,1)S(1)}, u32[]{:S(2)}, u32[]{:S(2)}) collective-permute-start(bf16[512,384]{1,0:T(8,128)(2,1)S(1)} %get-tuple-element.43), channel_id=1, source_target_pairs={{0,1},{1,0},{2,3},{3,2},{4,5},{5,4},{6,7},{7,6},{8,9},{9,8},{10,11... | collective-permute-start | bytes 1179656 | tf_op jit(solution)/shard_map/ppermute | solution.py:35
  44.1 28.7 %collective-permute-start.8 = (bf16[512,768]{1,0:T(8,128)(2,1)S(1)}, bf16[512,768]{1,0:T(8,128)(2,1)S(1)}, u32[]{:S(2)}, u32[]{:S(2)}) collective-permute-start(bf16[512,768]{1,0:T(8,128)(2,1)S(1)} %get-tuple-element.48.kept), channel_id=1, source_target_pairs={{4,0},{6,2},{8,4},{10,6},{12,8},{13,5},{14,10},{15,7},{16,12},{18,... | collective-permute-start | bytes 2359304 | tf_op jit(solution)/shard_map/ppermute | solution.py:35
  49.7 8.5 %collective-permute-start.10 = (bf16[192,768]{1,0:T(8,128)(2,1)S(1)}, bf16[192,768]{1,0:T(8,128)(2,1)S(1)}, u32[]{:S(2)}, u32[]{:S(2)}) collective-permute-start(bf16[192,768]{1,0:T(8,128)(2,1)S(1)} %get-tuple-element.52), channel_id=1, source_target_pairs={{0,1},{1,0},{2,3},{3,2},{4,5},{5,4},{6,7},{7,6},{8,9},{9,8},{10,11... | collective-permute-start | bytes 884744 | tf_op jit(solution)/shard_map/ppermute | solution.py:35
  54.1 5.6 %collective-permute-start.11 = (bf16[192,768]{1,0:T(8,128)(2,1)S(1)}, bf16[192,768]{1,0:T(8,128)(2,1)S(1)}, u32[]{:S(2)}, u32[]{:S(2)}) collective-permute-start(bf16[192,768]{1,0:T(8,128)(2,1)S(1)} %get-tuple-element.54), channel_id=1, source_target_pairs={{0,1},{1,0},{2,3},{3,2},{4,5},{5,4},{6,7},{7,6},{8,9},{9,8},{10,11... | collective-permute-start | bytes 884744 | tf_op jit(solution)/shard_map/ppermute | solution.py:35
  54.2 17.8 %collective-permute-start.7 = (bf16[512,384]{1,0:T(8,128)(2,1)S(1)}, bf16[512,384]{1,0:T(8,128)(2,1)S(1)}, u32[]{:S(2)}, u32[]{:S(2)}) collective-permute-start(bf16[512,384]{1,0:T(8,128)(2,1)S(1)} %shard_map.79.held), channel_id=1, source_target_pairs={{1,3},{3,1},{4,2},{6,0},{8,6},{9,11},{10,4},{11,9},{12,10},{13,7},... | collective-permute-start | bytes 1179656 | tf_op jit(solution)/shard_map/ppermute | solution.py:35
  56.2 16.7 %collective-permute-start.6 = (bf16[512,384]{1,0:T(8,128)(2,1)S(1)}, bf16[512,384]{1,0:T(8,128)(2,1)S(1)}, u32[]{:S(2)}, u32[]{:S(2)}) collective-permute-start(bf16[512,384]{1,0:T(8,128)(2,1)S(1)} %shard_map.79.held), channel_id=1, source_target_pairs={{4,0},{6,2},{8,4},{10,6},{12,8},{13,5},{14,10},{15,7},{16,12},{18,... | collective-permute-start | bytes 1179656 | tf_op jit(solution)/shard_map/ppermute | solution.py:35
  58.2 2.7 %collective-permute-start.12 = (bf16[192,768]{1,0:T(8,128)(2,1)S(1)}, bf16[192,768]{1,0:T(8,128)(2,1)S(1)}, u32[]{:S(2)}, u32[]{:S(2)}) collective-permute-start(bf16[192,768]{1,0:T(8,128)(2,1)S(1)} %get-tuple-element.56), channel_id=1, source_target_pairs={{0,1},{1,0},{2,3},{3,2},{4,5},{5,4},{6,7},{7,6},{8,9},{9,8},{10,11... | collective-permute-start | bytes 884744 | tf_op jit(solution)/shard_map/ppermute | solution.py:35
  59.7 1.6 %collective-permute-start.13 = (bf16[192,768]{1,0:T(8,128)(2,1)S(1)}, bf16[192,768]{1,0:T(8,128)(2,1)S(1)}, u32[]{:S(2)}, u32[]{:S(2)}) collective-permute-start(bf16[192,768]{1,0:T(8,128)(2,1)S(1)} %get-tuple-element.57), channel_id=1, source_target_pairs={{0,1},{1,0},{2,3},{3,2},{4,5},{5,4},{6,7},{7,6},{8,9},{9,8},{10,11... | collective-permute-start | bytes 884744 | tf_op jit(solution)/shard_map/ppermute | solution.py:35
  60.9 15.8 %collective-permute-start.16 = (bf16[512,384]{1,0:T(8,128)(2,1)S(1)}, bf16[512,384]{1,0:T(8,128)(2,1)S(1)}, u32[]{:S(2)}, u32[]{:S(2)}) collective-permute-start(bf16[512,384]{1,0:T(8,128)(2,1)S(1)} %shard_map.79.held), channel_id=1, source_target_pairs={{0,1},{1,0},{2,3},{3,2},{4,5},{5,4},{6,7},{7,6},{8,9},{9,8},{10,11... | collective-permute-start | bytes 1179656 | tf_op jit(solution)/shard_map/ppermute | solution.py:35
  72.8 4.4 %collective-permute-start.14 = (bf16[512,384]{1,0:T(8,128)(2,1)S(1)}, bf16[512,384]{1,0:T(8,128)(2,1)S(1)}, u32[]{:S(2)}, u32[]{:S(2)}) collective-permute-start(bf16[512,384]{1,0:T(8,128)(2,1)S(1)} %collective-permute-done.6.same), channel_id=1, source_target_pairs={{0,1},{1,0},{2,3},{3,2},{4,5},{5,4},{6,7},{7,6},{8,9},{9,8},{10,11... | collective-permute-start | bytes 1179656 | tf_op jit(solution)/shard_map/ppermute | solution.py:35
  75.9 1.9 %collective-permute-start.15 = (bf16[512,384]{1,0:T(8,128)(2,1)S(1)}, bf16[512,384]{1,0:T(8,128)(2,1)S(1)}, u32[]{:S(2)}, u32[]{:S(2)}) collective-permute-start(bf16[512,384]{1,0:T(8,128)(2,1)S(1)} %collective-permute-done.7.cross), channel_id=1, source_target_pairs={{0,1},{1,0},{2,3},{3,2},{4,5},{5,4},{6,7},{7,6},{8,9},{9,8},{10,11... | collective-permute-start | bytes 1179656 | tf_op jit(solution)/shard_map/ppermute | solution.py:35

commit v9 on v8

--- a/solution.py
+++ b/solution.py
@@ -643,7 +643,8 @@
     blocks = [*columns_of_twin(after(w_far, attn)), after(twin_a, attn), after(twin_b, attn)]
     far_a, far_b, twin_a, twin_b = [twin(a) for a in blocks]
     weight, gate = tail_inputs(mod_rows, out_weight, w_far, twin_a, twin_b, far_a, far_b)
-    same, cross, residual, _ = lax.optimization_barrier((same, cross, residual, weight))
+    cross, residual, _ = lax.optimization_barrier((cross, residual, weight))
+    same = after(same, weight)
     partial = first_out(same, cross, attn, weight)
     return last_out(twin(same), twin(cross), twin_attn, weight, partial, share_states, residual, gate, fresh)
 

time: 79.9 us -> 80.3 us (level)
  transfers between devices with their start and end apart: 17 -> 17, of which waited for: 8 -> 7; matrix products, arithmetic and copies ran while one was open for 0% -> 0% of each run, Pallas kernels for 24% -> 24%
where the time goes in v9:
time: 80.3 us; the launch traced here: 80.1 us
  starting transfers between devices  26.4 us (33%)
  Pallas kernels  20.7 us (26%)
  blocking collectives  17.1 us (21%)
  waiting for transfers between devices  15.1 us (19%)
    ppermute x17, starting transfers between devices, routed(): return lax.ppermute(array, BOTH, pairs)  26.4 us
    all_to_all x1, blocking collectives, on_device(): mod_rows = lax.all_to_all(payload, 'queue', 0, 0, tiled=True)[:, 0, :]  17.1 us
    ppermute x17, waiting for transfers between devices, routed(): return lax.ppermute(array, BOTH, pairs)  15.1 us
    pallas_call x1, Pallas kernels, keys_values(): pl.pallas_call(kv_kernel, out_shape=(near_out((rows, 2 * each)), near_out...  5.41 us
    pallas_call x1, Pallas kernels, local_attention(): pl.pallas_call(local_kernel, out_shape=(part,) * 3, in_specs=[vmem_spec()...  4.11 us
    pallas_call x1, Pallas kernels, remote_attention(): pl.pallas_call(remote_kernel, out_shape=near_out((span, 3 * PAIR)), in_sp...  3.05 us
    pallas_call x1, Pallas kernels, queries(): pl.pallas_call(query_kernel, out_shape=near_out((normed.shape[0], weight....  1.79 us
    pallas_call x1, Pallas kernels, slices(): pl.pallas_call(slices_kernel, out_shape=(near_out((rows // 2, width)), ne...  1.77 us
  transfers between devices with their start and end apart: 17, of which 7 were waited for; matrix products, arithmetic and copies ran while one was open for 0% of the time, Pallas kernels for 24%

profile of v9, /device:TPU:111, one launch (start us, length us, event | category | flops | bytes accessed | tf_op | source)
XLA Modules:
  0.0 80.1 jit_solution(18085479760566898277)
XLA Ops:
  0.8 1.8 %shard_map.75 = (bf16[256,3072]{1,0:T(8,128)(2,1)S(1)}, bf16[384,1536]{1,0:T(8,128)(2,1)S(1)}) custom-call(bf16[512,3072]{1,0:T(8,128)(2,1)} %hidden.3, bf16[384,3072]{1,0:T(8,128)(2,1)} %out_weight.5), custom_call_target="tpu_custom_call" | custom-call | bytes 4194304 | tf_op jit(solution)/shard_map/pallas_call | solution.py:105
  2.5 1.4 %collective-permute-start = (bf16[256,3072]{1,0:T(8,128)(2,1)S(1)}, bf16[256,3072]{1,0:T(8,128)(2,1)S(1)}, u32[]{:S(2)}, u32[]{:S(2)}) collective-permute-start(bf16[256,3072]{1,0:T(8,128)(2,1)S(1)} %get-tuple-element.36), channel_id=1, source_target_pairs={{0,4},{1,7},{2,6},{3,5},{4,0},{5,3},{6,2},{7,1},{8,12},{9,15},{10,... | collective-permute-start | bytes 4718600 | tf_op jit(solution)/shard_map/ppermute | solution.py:35
  4.6 17.1 %all_to_all.5 = f32[64,1,384]{2,1,0:T(1,128)S(1)} all-to-all(f32[64,1,384]{2,1,0:T(1,128)S(1)} %shard_map.73), channel_id=1, replica_groups=mesh['queue'=64,'heads'=4] {'queue'}, dimensions={0} | all-to-all | bytes 196608 | tf_op jit(solution)/shard_map/all_to_all | solution.py:614
  22.2 2.1 %collective-permute-start.1 = (bf16[256,3072]{1,0:T(8,128)(2,1)S(1)}, bf16[256,3072]{1,0:T(8,128)(2,1)S(1)}, u32[]{:S(2)}, u32[]{:S(2)}) collective-permute-start(bf16[256,3072]{1,0:T(8,128)(2,1)S(1)} %collective-permute-done.second), channel_id=1, source_target_pairs={{0,1},{1,0},{2,3},{3,2},{4,5},{5,4},{6,7},{7,6},{8,9},{9,8},{10,11... | collective-permute-start | bytes 4718600 | tf_op jit(solution)/shard_map/ppermute | solution.py:35
  24.3 1.3 %collective-permute-start.7 = (bf16[384,1536]{1,0:T(8,128)(2,1)S(1)}, bf16[384,1536]{1,0:T(8,128)(2,1)S(1)}, u32[]{:S(2)}, u32[]{:S(2)}) collective-permute-start(bf16[384,1536]{1,0:T(8,128)(2,1)S(1)} %get-tuple-element.48), channel_id=1, source_target_pairs={{0,6},{1,7},{2,4},{3,5},{4,2},{5,3},{6,0},{7,1},{8,14},{9,15},{10,... | collective-permute-start | bytes 3538952 | tf_op jit(solution)/shard_map/ppermute | solution.py:35
  26.3 1.1 %collective-permute-done.1.first = bf16[256,3072]{1,0:T(8,128)(2,1)S(1)} collective-permute-done((bf16[256,3072]{1,0:T(8,128)(2,1)S(1)}, bf16[256,3072]{1,0:T(8,128)(2,1)S(1)}, u32[]{:S(2)}, u32[]{:S(2)}) %collective-permute-start.1) | collective-permute-done | bytes 1572896 | tf_op jit(solution)/shard_map/ppermute | solution.py:35
  27.3 5.4 %shard_map.76 = (bf16[512,768]{1,0:T(8,128)(2,1)S(1)}, bf16[512,384]{1,0:T(8,128)(2,1)S(1)}, bf16[512,384]{1,0:T(8,128)(2,1)S(1)}, bf16[512,3072]{1,0:T(8,128)(2...) custom-call(f32[64,384]{1,0:T(8,128)S(1)} %bitcast.4, ...), custom_call_target="tpu_custom_call" | custom-call | flops 1 | bytes 1 | tf_op jit(solution)/shard_map/pallas_call | solution.py:255
  32.7 4.0 %collective-permute-start.3 = (bf16[512,768]{1,0:T(8,128)(2,1)S(1)}, bf16[512,768]{1,0:T(8,128)(2,1)S(1)}, u32[]{:S(2)}, u32[]{:S(2)}) collective-permute-start(bf16[512,768]{1,0:T(8,128)(2,1)S(1)} %get-tuple-element.39.own_ref), channel_id=1, source_target_pairs={{1,8},{3,10},{4,13},{6,15},{8,1},{9,16},{10,3},{11,18},{12,21},{13... | collective-permute-start | bytes 2359304 | tf_op jit(solution)/shard_map/ppermute | solution.py:35
  36.7 1.2 %collective-permute-start.4 = (bf16[512,384]{1,0:T(8,128)(2,1)S(1)}, bf16[512,384]{1,0:T(8,128)(2,1)S(1)}, u32[]{:S(2)}, u32[]{:S(2)}) collective-permute-start(bf16[512,384]{1,0:T(8,128)(2,1)S(1)} %get-tuple-element.42), channel_id=1, source_target_pairs={{0,1},{1,0},{2,3},{3,2},{4,5},{5,4},{6,7},{7,6},{8,9},{9,8},{10,11... | collective-permute-start | bytes 1179656 | tf_op jit(solution)/shard_map/ppermute | solution.py:35
  38.2 1.8 %shard_map.77.q_ref = bf16[512,384]{1,0:T(8,128)(2,1)S(1)} custom-call(bf16[512,3072]{1,0:T(8,128)(2,1)S(1)} %get-tuple-element.40.normed, bf16[3072,384]{1,0:T(8,128)(2,1)S(1)} %get-tuple-element.41.weight), custom_call_target="tpu_custom_call" | custom-call | flops 1 | bytes 1 | tf_op jit(solution)/shard_map/pallas_call | solution.py:286
  40.0 4.1 %shard_map.78 = (f32[512,384]{1,0:T(8,128)S(1)}, f32[512,384]{1,0:T(8,128)S(1)}, f32[512,384]{1,0:T(8,128)S(1)}) custom-call(bf16[1536,128]{1,0:T(8,128)(2,1)S(1)} %shard_map.74.dead_ref, bf16[512,384]{1,0:T(8,128)(2,1)S(1)} %shard_map.77.q_ref, bf16[512,768]{1,0:T(8,128)(2,1)S(1)} %get-tuple-element.39.own_ref, ...), custom_call_target="tpu_custom_call" | custom-call | flops 1 | bytes 1 | tf_op jit(solution)/shard_map/pallas_call | solution.py:412
  44.1 1.9 %collective-permute-start.14 = (bf16[512,768]{1,0:T(8,128)(2,1)S(1)}, bf16[512,768]{1,0:T(8,128)(2,1)S(1)}, u32[]{:S(2)}, u32[]{:S(2)}) collective-permute-start(bf16[512,768]{1,0:T(8,128)(2,1)S(1)} %get-tuple-element.59.kept), channel_id=1, source_target_pairs={{4,0},{6,2},{8,4},{10,6},{12,8},{13,5},{14,10},{15,7},{16,12},{18,... | collective-permute-start | bytes 2359304 | tf_op jit(solution)/shard_map/ppermute | solution.py:35
  46.7 3.1 %shard_map.79.held = bf16[512,384]{1,0:T(8,128)(2,1)S(1)} custom-call(bf16[1536,128]{1,0:T(8,128)(2,1)S(1)} %shard_map.74.dead_ref, bf16[512,384]{1,0:T(8,128)(2,1)S(1)} %shard_map.77.q_ref, bf16[512,768]{1,0:T(8,128)(2,1)S(1)} %collective-permute-done.3.kv_ref, f32[512,384]{1,0:T(8,128)S(1)} %get-tuple-element.44.o_ref, ...), custom_call_target="tpu_custom_call" | custom-call | flops 1 | bytes 1 | tf_op jit(solution)/shard_map/pallas_call | solution.py:451
  49.7 4.4 %collective-permute-start.8 = (bf16[192,768]{1,0:T(8,128)(2,1)S(1)}, bf16[192,768]{1,0:T(8,128)(2,1)S(1)}, u32[]{:S(2)}, u32[]{:S(2)}) collective-permute-start(bf16[192,768]{1,0:T(8,128)(2,1)S(1)} %get-tuple-element.50), channel_id=1, source_target_pairs={{0,1},{1,0},{2,3},{3,2},{4,5},{5,4},{6,7},{7,6},{8,9},{9,8},{10,11... | collective-permute-start | bytes 884744 | tf_op jit(solution)/shard_map/ppermute | solution.py:35
  54.2 1.9 %collective-permute-start.6 = (bf16[512,384]{1,0:T(8,128)(2,1)S(1)}, bf16[512,384]{1,0:T(8,128)(2,1)S(1)}, u32[]{:S(2)}, u32[]{:S(2)}) collective-permute-start(bf16[512,384]{1,0:T(8,128)(2,1)S(1)} %shard_map.79.held), channel_id=1, source_target_pairs={{4,0},{6,2},{8,4},{10,6},{12,8},{13,5},{14,10},{15,7},{16,12},{18,... | collective-permute-start | bytes 1179656 | tf_op jit(solution)/shard_map/ppermute | solution.py:35
  56.2 1.9 %collective-permute-start.13 = (bf16[512,384]{1,0:T(8,128)(2,1)S(1)}, bf16[512,384]{1,0:T(8,128)(2,1)S(1)}, u32[]{:S(2)}, u32[]{:S(2)}) collective-permute-start(bf16[512,384]{1,0:T(8,128)(2,1)S(1)} %shard_map.79.held), channel_id=1, source_target_pairs={{1,3},{3,1},{4,2},{6,0},{8,6},{9,11},{10,4},{11,9},{12,10},{13,7},... | collective-permute-start | bytes 1179656 | tf_op jit(solution)/shard_map/ppermute | solution.py:35
  58.2 1.5 %collective-permute-start.10 = (bf16[192,768]{1,0:T(8,128)(2,1)S(1)}, bf16[192,768]{1,0:T(8,128)(2,1)S(1)}, u32[]{:S(2)}, u32[]{:S(2)}) collective-permute-start(bf16[192,768]{1,0:T(8,128)(2,1)S(1)} %get-tuple-element.54), channel_id=1, source_target_pairs={{0,1},{1,0},{2,3},{3,2},{4,5},{5,4},{6,7},{7,6},{8,9},{9,8},{10,11... | collective-permute-start | bytes 884744 | tf_op jit(solution)/shard_map/ppermute | solution.py:35
  59.8 1.1 %collective-permute-done.10.far_a = bf16[192,768]{1,0:T(8,128)(2,1)S(1)} collective-permute-done((bf16[192,768]{1,0:T(8,128)(2,1)S(1)}, bf16[192,768]{1,0:T(8,128)(2,1)S(1)}, u32[]{:S(2)}, u32[]{:S(2)}) %collective-permute-start.10) | collective-permute-done | bytes 294944 | tf_op jit(solution)/shard_map/ppermute | solution.py:35
  61.3 1.1 %shard_map.81 = (bf16[1536,768]{1,0:T(8,128)(2,1)S(1)}, f32[1,768]{1,0:T(1,128)S(1)}) custom-call(f32[64,384]{1,0:T(8,128)S(1)} %bitcast.5, bf16[384,3072]{1,0:T(8,128)(2,1)} %out_weight.5, bf16[384,1536]{1,0:T(8,128)(2,1)S(1)} %collective-permute-done.7.source.w_far, bf16[192,768]{1,0:T(8,128)(2,1)S(1)} %collective-permute-done.8.twin_a, ...), custom_call_target="tpu_custom_call" | custom-call | flops 1 | bytes 1 | tf_op jit(solution)/shard_map/pallas_call | solution.py:517
  62.5 3.9 %collective-permute-done.6.same = bf16[512,384]{1,0:T(8,128)(2,1)S(1)} collective-permute-done((bf16[512,384]{1,0:T(8,128)(2,1)S(1)}, bf16[512,384]{1,0:T(8,128)(2,1)S(1)}, u32[]{:S(2)}, u32[]{:S(2)}) %collective-permute-start.6) | collective-permute-done | bytes 393248 | tf_op jit(solution)/shard_map/ppermute | solution.py:35
  66.4 2.3 %collective-permute-start.12 = (bf16[512,384]{1,0:T(8,128)(2,1)S(1)}, bf16[512,384]{1,0:T(8,128)(2,1)S(1)}, u32[]{:S(2)}, u32[]{:S(2)}) collective-permute-start(bf16[512,384]{1,0:T(8,128)(2,1)S(1)} %collective-permute-done.6.same), channel_id=1, source_target_pairs={{0,1},{1,0},{2,3},{3,2},{4,5},{5,4},{6,7},{7,6},{8,9},{9,8},{10,11... | collective-permute-start | bytes 1179656 | tf_op jit(solution)/shard_map/ppermute | solution.py:35
  68.6 7.4 %collective-permute-done.13.cross = bf16[512,384]{1,0:T(8,128)(2,1)S(1)} collective-permute-done((bf16[512,384]{1,0:T(8,128)(2,1)S(1)}, bf16[512,384]{1,0:T(8,128)(2,1)S(1)}, u32[]{:S(2)}, u32[]{:S(2)}) %collective-permute-start.13) | collective-permute-done | bytes 393248 | tf_op jit(solution)/shard_map/ppermute | solution.py:35
  76.0 0.9 %collective-permute-start.15 = (bf16[512,384]{1,0:T(8,128)(2,1)S(1)}, bf16[512,384]{1,0:T(8,128)(2,1)S(1)}, u32[]{:S(2)}, u32[]{:S(2)}) collective-permute-start(bf16[512,384]{1,0:T(8,128)(2,1)S(1)} %collective-permute-done.13.cross), channel_id=1, source_target_pairs={{0,1},{1,0},{2,3},{3,2},{4,5},{5,4},{6,7},{7,6},{8,9},{9,8},{10,11... | collective-permute-start | bytes 1179656 | tf_op jit(solution)/shard_map/ppermute | solution.py:35
  78.3 1.6 %shard_map.83 = bf16[512,768]{1,0:T(8,128)(2,1)} custom-call(bf16[512,384]{1,0:T(8,128)(2,1)S(1)} %collective-permute-done.12.same, bf16[512,384]{1,0:T(8,128)(2,1)S(1)} %collective-permute-done.15.cross, bf16[512,384]{1,0:T(8,128)(2,1)S(1)} %collective-permute-done.16.held, bf16[1536,768]{1,0:T(8,128)(2,1)S(1)} %get-tuple-element.56.weight, ...), custom_call_target="tpu_custom_call" | custom-call | flops 1 | bytes 1 | tf_op jit(solution)/shard_map/pallas_call | solution.py:589
  (33 shorter events, 5.5 us)
Async XLA Ops:
  0.0 3.9 %copy-start.2 = (s32[64]{0:T(128)S(1)}, s32[64]{0:T(128)}, u32[]{:S(2)}) copy-start(s32[64]{0:T(128)} %param.8) | copy-start | bytes 772
  0.0 4.3 %copy-start = (bf16[512,144]{0,1:T(8,128)(2,1)S(1)}, bf16[512,144]{0,1:T(8,128)(2,1)}, u32[]{:S(2)}) copy-start(bf16[512,144]{0,1:T(8,128)(2,1)} %param.10) | copy-start | bytes 442372
  0.0 25.6 %copy-start.1 = (s32[64]{0:T(128)S(1)}, s32[64]{0:T(128)}, u32[]{:S(2)}) copy-start(s32[64]{0:T(128)} %counts_ref) | copy-start | bytes 772
  0.0 27.3 %collective-permute-start.2 = (bf16[3,3072,384]{2,1,0:T(8,128)(2,1)}, bf16[3,3072,384]{2,1,0:T(8,128)(2,1)S(1)}, u32[]{:S(2)}, u32[]{:S(2)}) collective-permute-start(bf16[3,3072,384]{2,1,0:T(8,128)(2,1)} %own_weight.1), channel_id=1, source_target_pairs={{0,1},{1,0},{2,3},{3,2},{4,5},{5,4},{6,7},{7,6},{8,9},{9,8},{10,11... | collective-permute-start | bytes 21233672 | tf_op jit(solution)/shard_map/ppermute | solution.py:35
  2.5 19.6 %collective-permute-start = (bf16[256,3072]{1,0:T(8,128)(2,1)S(1)}, bf16[256,3072]{1,0:T(8,128)(2,1)S(1)}, u32[]{:S(2)}, u32[]{:S(2)}) collective-permute-start(bf16[256,3072]{1,0:T(8,128)(2,1)S(1)} %get-tuple-element.36), channel_id=1, source_target_pairs={{0,4},{1,7},{2,6},{3,5},{4,0},{5,3},{6,2},{7,1},{8,12},{9,15},{10,... | collective-permute-start | bytes 4718600 | tf_op jit(solution)/shard_map/ppermute | solution.py:35
  22.2 5.1 %collective-permute-start.1 = (bf16[256,3072]{1,0:T(8,128)(2,1)S(1)}, bf16[256,3072]{1,0:T(8,128)(2,1)S(1)}, u32[]{:S(2)}, u32[]{:S(2)}) collective-permute-start(bf16[256,3072]{1,0:T(8,128)(2,1)S(1)} %collective-permute-done.second), channel_id=1, source_target_pairs={{0,1},{1,0},{2,3},{3,2},{4,5},{5,4},{6,7},{7,6},{8,9},{9,8},{10,11... | collective-permute-start | bytes 4718600 | tf_op jit(solution)/shard_map/ppermute | solution.py:35
  24.3 31.9 %collective-permute-start.7 = (bf16[384,1536]{1,0:T(8,128)(2,1)S(1)}, bf16[384,1536]{1,0:T(8,128)(2,1)S(1)}, u32[]{:S(2)}, u32[]{:S(2)}) collective-permute-start(bf16[384,1536]{1,0:T(8,128)(2,1)S(1)} %get-tuple-element.48), channel_id=1, source_target_pairs={{0,6},{1,7},{2,4},{3,5},{4,2},{5,3},{6,0},{7,1},{8,14},{9,15},{10,... | collective-permute-start | bytes 3538952 | tf_op jit(solution)/shard_map/ppermute | solution.py:35
  32.7 13.9 %collective-permute-start.3 = (bf16[512,768]{1,0:T(8,128)(2,1)S(1)}, bf16[512,768]{1,0:T(8,128)(2,1)S(1)}, u32[]{:S(2)}, u32[]{:S(2)}) collective-permute-start(bf16[512,768]{1,0:T(8,128)(2,1)S(1)} %get-tuple-element.39.own_ref), channel_id=1, source_target_pairs={{1,8},{3,10},{4,13},{6,15},{8,1},{9,16},{10,3},{11,18},{12,21},{13... | collective-permute-start | bytes 2359304 | tf_op jit(solution)/shard_map/ppermute | solution.py:35
  36.7 3.3 %collective-permute-start.4 = (bf16[512,384]{1,0:T(8,128)(2,1)S(1)}, bf16[512,384]{1,0:T(8,128)(2,1)S(1)}, u32[]{:S(2)}, u32[]{:S(2)}) collective-permute-start(bf16[512,384]{1,0:T(8,128)(2,1)S(1)} %get-tuple-element.42), channel_id=1, source_target_pairs={{0,1},{1,0},{2,3},{3,2},{4,5},{5,4},{6,7},{7,6},{8,9},{9,8},{10,11... | collective-permute-start | bytes 1179656 | tf_op jit(solution)/shard_map/ppermute | solution.py:35
  37.9 2.1 %collective-permute-start.5 = (bf16[512,384]{1,0:T(8,128)(2,1)S(1)}, bf16[512,384]{1,0:T(8,128)(2,1)S(1)}, u32[]{:S(2)}, u32[]{:S(2)}) collective-permute-start(bf16[512,384]{1,0:T(8,128)(2,1)S(1)} %get-tuple-element.43), channel_id=1, source_target_pairs={{0,1},{1,0},{2,3},{3,2},{4,5},{5,4},{6,7},{7,6},{8,9},{9,8},{10,11... | collective-permute-start | bytes 1179656 | tf_op jit(solution)/shard_map/ppermute | solution.py:35
  44.1 31.9 %collective-permute-start.14 = (bf16[512,768]{1,0:T(8,128)(2,1)S(1)}, bf16[512,768]{1,0:T(8,128)(2,1)S(1)}, u32[]{:S(2)}, u32[]{:S(2)}) collective-permute-start(bf16[512,768]{1,0:T(8,128)(2,1)S(1)} %get-tuple-element.59.kept), channel_id=1, source_target_pairs={{4,0},{6,2},{8,4},{10,6},{12,8},{13,5},{14,10},{15,7},{16,12},{18,... | collective-permute-start | bytes 2359304 | tf_op jit(solution)/shard_map/ppermute | solution.py:35
  49.7 8.5 %collective-permute-start.8 = (bf16[192,768]{1,0:T(8,128)(2,1)S(1)}, bf16[192,768]{1,0:T(8,128)(2,1)S(1)}, u32[]{:S(2)}, u32[]{:S(2)}) collective-permute-start(bf16[192,768]{1,0:T(8,128)(2,1)S(1)} %get-tuple-element.50), channel_id=1, source_target_pairs={{0,1},{1,0},{2,3},{3,2},{4,5},{5,4},{6,7},{7,6},{8,9},{9,8},{10,11... | collective-permute-start | bytes 884744 | tf_op jit(solution)/shard_map/ppermute | solution.py:35
  54.1 5.6 %collective-permute-start.9 = (bf16[192,768]{1,0:T(8,128)(2,1)S(1)}, bf16[192,768]{1,0:T(8,128)(2,1)S(1)}, u32[]{:S(2)}, u32[]{:S(2)}) collective-permute-start(bf16[192,768]{1,0:T(8,128)(2,1)S(1)} %get-tuple-element.52), channel_id=1, source_target_pairs={{0,1},{1,0},{2,3},{3,2},{4,5},{5,4},{6,7},{7,6},{8,9},{9,8},{10,11... | collective-permute-start | bytes 884744 | tf_op jit(solution)/shard_map/ppermute | solution.py:35
  54.2 12.1 %collective-permute-start.6 = (bf16[512,384]{1,0:T(8,128)(2,1)S(1)}, bf16[512,384]{1,0:T(8,128)(2,1)S(1)}, u32[]{:S(2)}, u32[]{:S(2)}) collective-permute-start(bf16[512,384]{1,0:T(8,128)(2,1)S(1)} %shard_map.79.held), channel_id=1, source_target_pairs={{4,0},{6,2},{8,4},{10,6},{12,8},{13,5},{14,10},{15,7},{16,12},{18,... | collective-permute-start | bytes 1179656 | tf_op jit(solution)/shard_map/ppermute | solution.py:35
  56.2 19.8 %collective-permute-start.13 = (bf16[512,384]{1,0:T(8,128)(2,1)S(1)}, bf16[512,384]{1,0:T(8,128)(2,1)S(1)}, u32[]{:S(2)}, u32[]{:S(2)}) collective-permute-start(bf16[512,384]{1,0:T(8,128)(2,1)S(1)} %shard_map.79.held), channel_id=1, source_target_pairs={{1,3},{3,1},{4,2},{6,0},{8,6},{9,11},{10,4},{11,9},{12,10},{13,7},... | collective-permute-start | bytes 1179656 | tf_op jit(solution)/shard_map/ppermute | solution.py:35
  58.2 2.7 %collective-permute-start.10 = (bf16[192,768]{1,0:T(8,128)(2,1)S(1)}, bf16[192,768]{1,0:T(8,128)(2,1)S(1)}, u32[]{:S(2)}, u32[]{:S(2)}) collective-permute-start(bf16[192,768]{1,0:T(8,128)(2,1)S(1)} %get-tuple-element.54), channel_id=1, source_target_pairs={{0,1},{1,0},{2,3},{3,2},{4,5},{5,4},{6,7},{7,6},{8,9},{9,8},{10,11... | collective-permute-start | bytes 884744 | tf_op jit(solution)/shard_map/ppermute | solution.py:35
  59.7 1.6 %collective-permute-start.11 = (bf16[192,768]{1,0:T(8,128)(2,1)S(1)}, bf16[192,768]{1,0:T(8,128)(2,1)S(1)}, u32[]{:S(2)}, u32[]{:S(2)}) collective-permute-start(bf16[192,768]{1,0:T(8,128)(2,1)S(1)} %get-tuple-element.55), channel_id=1, source_target_pairs={{0,1},{1,0},{2,3},{3,2},{4,5},{5,4},{6,7},{7,6},{8,9},{9,8},{10,11... | collective-permute-start | bytes 884744 | tf_op jit(solution)/shard_map/ppermute | solution.py:35
  60.9 16.8 %collective-permute-start.16 = (bf16[512,384]{1,0:T(8,128)(2,1)S(1)}, bf16[512,384]{1,0:T(8,128)(2,1)S(1)}, u32[]{:S(2)}, u32[]{:S(2)}) collective-permute-start(bf16[512,384]{1,0:T(8,128)(2,1)S(1)} %shard_map.79.held), channel_id=1, source_target_pairs={{0,1},{1,0},{2,3},{3,2},{4,5},{5,4},{6,7},{7,6},{8,9},{9,8},{10,11... | collective-permute-start | bytes 1179656 | tf_op jit(solution)/shard_map/ppermute | solution.py:35
  66.4 11.4 %collective-permute-start.12 = (bf16[512,384]{1,0:T(8,128)(2,1)S(1)}, bf16[512,384]{1,0:T(8,128)(2,1)S(1)}, u32[]{:S(2)}, u32[]{:S(2)}) collective-permute-start(bf16[512,384]{1,0:T(8,128)(2,1)S(1)} %collective-permute-done.6.same), channel_id=1, source_target_pairs={{0,1},{1,0},{2,3},{3,2},{4,5},{5,4},{6,7},{7,6},{8,9},{9,8},{10,11... | collective-permute-start | bytes 1179656 | tf_op jit(solution)/shard_map/ppermute | solution.py:35
  76.0 2.3 %collective-permute-start.15 = (bf16[512,384]{1,0:T(8,128)(2,1)S(1)}, bf16[512,384]{1,0:T(8,128)(2,1)S(1)}, u32[]{:S(2)}, u32[]{:S(2)}) collective-permute-start(bf16[512,384]{1,0:T(8,128)(2,1)S(1)} %collective-permute-done.13.cross), channel_id=1, source_target_pairs={{0,1},{1,0},{2,3},{3,2},{4,5},{5,4},{6,7},{7,6},{8,9},{9,8},{10,11... | collective-permute-start | bytes 1179656 | tf_op jit(solution)/shard_map/ppermute | solution.py:35
